TPU v7x, 256 devices: a whole 4x4x8 slice. The times are simulated.
256 devices in a mesh: frame: 32 (over z, y_hi, core), fsdp: 8 (over y_lo, x).
Axes of the slice: x: 4, y: 4 (y_hi: 2, y_lo: 2; y = y_hi * 2 + y_lo), z: 8, core: 2. Of those that a mesh axis runs over, the one named last changes fastest.
Arguments:
- query_rows: bfloat16 [8, 4096, 1536], P('fsdp', 'frame'), may hold values from -96 to 96
- key_rows: bfloat16 [8, 4096, 1536], P('fsdp', 'frame'), may hold values from -4 to 4
- value_rows: bfloat16 [8, 4096, 1536], P('fsdp', 'frame'), may hold values from -6 to 6
- frame_of: int32 [8, 32], P('fsdp', 'frame'), may hold values from 0 to 15, never falling along the last dimension, each value on 1 to 4 neighbouring positions
- reach_back: int32 [8, 32], P('fsdp', 'frame'), may hold values from 0 to 2
- reach_ahead: int32 [8, 32], P('fsdp', 'frame'), may hold values from 0 to 2
- out_weight: bfloat16 [1536, 1536], P('fsdp'), may hold values from -0.15625 to 0.15625
- out_grad: bfloat16 [8, 4096, 1536], P('fsdp', 'frame'), may hold values from -6 to 6
Outputs:
- layer_out: bfloat16 [8, 4096, 1536], P('fsdp', 'frame')
- grad_query: bfloat16 [8, 4096, 1536], P('fsdp', 'frame')
- grad_key: bfloat16 [8, 4096, 1536], P('fsdp', 'frame')
- grad_value: bfloat16 [8, 4096, 1536], P('fsdp', 'frame')
- grad_weight: float32 [1536, 1536], P(('frame', 'fsdp'))
Inputs may be any that keep to these rules, and one draw needn't show every extreme that they name: `frame_of`: frame numbers never fall along a clip's tiles; each frame covers 1 to 4 tiles.
All inputs are finite; a program needn't handle non-finite values.
Results may differ from a plain program's by a relative error of at most 0.03.
Values may be sent and summed in bfloat16 or wider, within the bound.
No kernel may reach another device: no remote copies, remote signals or barrier semaphores. Data moves between devices by JAX's collectives and lax.ppermute only.
A program may use at most 128 MiB of HBM per device.

v0:
```python
import jax
import jax.numpy as jnp
from jax import lax
from jax.sharding import PartitionSpec as P

HEADS = 12
HEAD_DIM = 128


masked_score = -1e30


def shifted(value, axis, steps):
    count = lax.axis_size(axis)
    first, last = (max(0, -steps), min(count, count - steps))
    return lax.ppermute(value, axis, [(source, source + steps) for source in range(first, last)])


def shards(
    query_rows, key_rows, value_rows, frame_of, reach_back, reach_ahead, out_weight, out_grad
):
    frame_count = lax.axis_size("frame")
    fsdp_count = lax.axis_size("fsdp")
    position = lax.axis_index("frame")
    queries = query_rows[0]
    token_rows = queries.shape[0]
    tile_count = frame_of.shape[1]
    tile_rows = token_rows // tile_count
    head_count = HEADS
    head_size = HEAD_DIM
    score_scale = head_size ** (-0.5)
    weight = lax.all_gather(out_weight, "fsdp", axis=0, tiled=True)
    own_block = (key_rows[0], value_rows[0], frame_of[0])
    gotten = []
    for offset in (1, -1):
        gotten.append(shifted((own_block[0], own_block[1], own_block[2]), "frame", offset))
    from_left, from_right = gotten
    keys_all = jnp.concatenate([from_left[0], own_block[0], from_right[0]], 0)
    values_all = jnp.concatenate([from_left[1], own_block[1], from_right[1]], 0)
    frames_all = jnp.concatenate([from_left[2], own_block[2], from_right[2]], 0)
    key_tiles = (position - 1) * tile_count + jnp.arange(3 * tile_count, dtype=jnp.int32)
    query_tiles = position * tile_count + jnp.arange(tile_count, dtype=jnp.int32)
    inside = (key_tiles >= 0) & (key_tiles < frame_count * tile_count)
    own_frames = frame_of[0]
    lowest = own_frames - reach_back[0]
    highest = own_frames + reach_ahead[0]
    visible = (
        inside[None, :]
        & (jnp.abs(key_tiles[None, :] - query_tiles[:, None]) <= tile_count)
        & (frames_all[None, :] >= lowest[:, None])
        & (frames_all[None, :] <= highest[:, None])
    )
    token_mask = jnp.repeat(jnp.repeat(visible, tile_rows, 0), tile_rows, 1)
    query_heads = queries.reshape(token_rows, head_count, head_size)
    key_heads = keys_all.reshape(3 * token_rows, head_count, head_size)
    value_heads = values_all.reshape(3 * token_rows, head_count, head_size)
    scores = (
        jnp.einsum("qhd,khd->hqk", query_heads, key_heads, preferred_element_type=jnp.float32)
        * score_scale
    )
    scores = jnp.where(token_mask[None], scores, masked_score)
    row_max = jnp.max(scores, -1)
    logsum = row_max + jnp.log(jnp.sum(jnp.exp(scores - row_max[..., None]), -1))
    probs_full = jnp.exp(scores - logsum[..., None])
    probs_low = probs_full.astype(jnp.bfloat16)
    attended = jnp.einsum(
        "hqk,khd->qhd", probs_low, value_heads, preferred_element_type=jnp.float32
    )
    attended = attended.astype(jnp.bfloat16).reshape(token_rows, -1)
    layer_out = jnp.dot(attended, weight, preferred_element_type=jnp.float32).astype(jnp.bfloat16)
    grad_out = out_grad[0]
    grad_attended = lax.dot_general(
        grad_out, weight, (((1,), (1,)), ((), ())), preferred_element_type=jnp.float32
    ).astype(jnp.bfloat16)
    grad_heads = grad_attended.reshape(token_rows, head_count, head_size)
    delta_terms = jnp.sum(
        (grad_attended.astype(jnp.float32) * attended.astype(jnp.float32)).reshape(
            token_rows, head_count, head_size
        ),
        -1,
    ).T
    grad_probs = jnp.einsum(
        "qhd,khd->hqk", grad_heads, value_heads, preferred_element_type=jnp.float32
    )
    grad_scores = (probs_full * (grad_probs - delta_terms[..., None]) * score_scale).astype(
        jnp.bfloat16
    )
    query_grad = jnp.einsum(
        "hqk,khd->qhd", grad_scores, key_heads, preferred_element_type=jnp.float32
    )
    query_grad = query_grad.astype(jnp.bfloat16).reshape(token_rows, -1)
    key_partial = jnp.einsum(
        "hqk,qhd->khd", grad_scores, query_heads, preferred_element_type=jnp.float32
    ).reshape(3 * token_rows, -1)
    value_partial = jnp.einsum(
        "hqk,qhd->khd", probs_low, grad_heads, preferred_element_type=jnp.float32
    ).reshape(3 * token_rows, -1)
    key_total = key_partial[token_rows : 2 * token_rows]
    value_total = value_partial[token_rows : 2 * token_rows]
    for offset, row_first in ((-1, 0), (1, 2 * token_rows)):
        returned = shifted(
            (
                key_partial[row_first : row_first + token_rows],
                value_partial[row_first : row_first + token_rows],
            ),
            "frame",
            offset,
        )
        key_total = key_total + returned[0]
        value_total = value_total + returned[1]
    factor = float(frame_count * fsdp_count * token_rows) ** (-0.5)
    grad_weight = lax.psum_scatter(
        lax.dot_general(
            attended, grad_out, (((0,), (0,)), ((), ())), preferred_element_type=jnp.float32
        )
        * factor,
        ("frame", "fsdp"),
        scatter_dimension=0,
        tiled=True,
    )
    return (
        layer_out[None],
        query_grad[None],
        key_total.astype(jnp.bfloat16)[None],
        value_total.astype(jnp.bfloat16)[None],
        grad_weight,
    )


def solution(mesh):
    in_specs = (
        P("fsdp", "frame", None),
        P("fsdp", "frame", None),
        P("fsdp", "frame", None),
        P("fsdp", "frame"),
        P("fsdp", "frame"),
        P("fsdp", "frame"),
        P("fsdp", None),
        P("fsdp", "frame", None),
    )
    out_specs = (
        P("fsdp", "frame", None),
        P("fsdp", "frame", None),
        P("fsdp", "frame", None),
        P("fsdp", "frame", None),
        P(("frame", "fsdp"), None),
    )
    return jax.shard_map(shards, mesh=mesh, in_specs=in_specs, out_specs=out_specs, check_vma=False)
```

profile of v0, /device:TPU:2, one launch (start us, length us, event | category | flops | bytes accessed | tf_op | source)
XLA Modules:
  0.0 1475.0 jit_solution(11549187557025394576)
XLA Ops:
  9.1 13.5 collective-permute-start.5
  22.6 13.8 collective-permute-start.4
  37.7 3.1 collective-permute-start
  47.2 6.0 collective-permute-start.2
  62.1 5.1 convolution_multiply_fusion
  67.2 756.4 %fusion = f32[8,1536]{1,0:T(8,128)S(1)} fusion(f32[1536,1536]{1,0:T(8,128)} %convolution_multiply_fusion), kind=kCustom, calls=%all-reduce-scatter | all-reduce-scatter fusion | flops 3145729 | bytes 9486336
  827.5 8.3 collective-permute-start.73
  852.1 21.0 %collective-permute-start.57 = (f32[8,1536]{1,0:T(8,128)S(1)}, f32[8,1536]{1,0:T(8,128)S(1)}, u32[]{:S(2)}, u32[]{:S(2)}) collective-permute-start(f32[8,1536]{1,0:T(8,128)S(1)} %fusion), channel_id=1, source_target_pairs={{0,48},{1,49},{2,50},{3,51},{4,52},{5,53},{6,54},{7,55},{8,56},{9,... | collective-permute-start | bytes 147464
  876.2 3.6 collective-permute-start.54
  882.5 4.8 collective-permute-start.51
  893.9 3.3 collective-permute-start.46
  906.6 8.2 collective-permute-start.41
  914.8 13.1 collective-permute-start.40
  928.0 13.1 collective-permute-start.39
  941.1 13.1 collective-permute-start.38
  954.3 13.1 collective-permute-start.37
  967.4 13.1 collective-permute-start.36
  980.6 13.1 collective-permute-start.35
  993.7 13.1 collective-permute-start.34
  1006.9 13.1 collective-permute-start.33
  1020.0 13.1 collective-permute-start.32
  1033.2 13.1 collective-permute-start.31
  1046.3 13.1 collective-permute-start.30
  1059.5 13.1 collective-permute-start.29
  1072.6 13.1 collective-permute-start.28
  1085.8 13.7 collective-permute-start.27
  1099.5 13.2 collective-permute-start.26
  1112.7 13.1 collective-permute-start.25
  1125.8 13.1 collective-permute-start.24
  1139.0 13.1 collective-permute-start.23
  1152.1 13.1 collective-permute-start.22
  1165.3 13.1 collective-permute-start.21
  1178.4 13.1 collective-permute-start.20
  1191.6 13.1 collective-permute-start.19
  1204.7 13.1 collective-permute-start.18
  1219.9 14.1 collective-permute-start.16
  1234.0 13.1 collective-permute-start.15
  1247.1 13.1 collective-permute-start.14
  1260.3 13.1 collective-permute-start.13
  1273.4 13.1 collective-permute-start.12
  1286.6 13.1 collective-permute-start.11
  1299.7 12.7 collective-permute-start.10
  1316.4 97.2 %concatenate.34 = f32[518,1536]{1,0:T(8,128)} concatenate(f32[6,1536]{1,0:T(8,128)S(1)} %collective-permute-done.73, f32[8,1536]{1,0:T(8,128)S(1)} %collective-permute-done.72, f32[8,1536]{1,0:T(8,128)S(1)} %collective-permute-done.71, f32[8,1536]{1,0:T(8,128)S(1)} %collective-permute-done.70, f32[8,1536]{1,0:T(8,128)S(1)} %collective-permute-done.69, ...), dimensions={0} | concatenate | bytes 6365184
  1415.1 4.0 convolution_convert_fusion
  1424.3 3.1 convolution_bitcast_fusion
  1441.2 2.8 convolution_convert_fusion.2
  1451.1 4.8 collective-permute-start.9
  1459.9 3.9 fusion.4
  (250 shorter events, 99.5 us)
Async XLA Ops:
  7.2 1407.9 %all-gather.2.cloned.1.call-start = ((), (), s32[]{:S(2)}) async-start(), calls=%async_computation | async-start | bytes 5308416 | tf_op jit(solution)/shard_map/all_gather | solution.py:32
  9.1 45.8 %collective-permute-start.5 = (bf16[128,1536]{0,1:T(8,128)(2,1)S(1)}, bf16[128,1536]{0,1:T(8,128)(2,1)S(1)}, u32[]{:S(2)}, u32[]{:S(2)}) collective-permute-start(bf16[128,1536]{0,1:T(8,128)(2,1)S(1)} %bitcast.87), channel_id=1, source_target_pairs={{8,0},{16,8},{24,16},{32,24},{40,32},{48,40},{56,48},{64,56},{72,6... | collective-permute-start | bytes 1179656 | tf_op jit(solution)/shard_map/ppermute | solution.py:16
  22.6 33.3 %collective-permute-start.4 = (bf16[128,1536]{0,1:T(8,128)(2,1)S(1)}, bf16[128,1536]{0,1:T(8,128)(2,1)S(1)}, u32[]{:S(2)}, u32[]{:S(2)}) collective-permute-start(bf16[128,1536]{0,1:T(8,128)(2,1)S(1)} %bitcast.88), channel_id=1, source_target_pairs={{0,8},{8,16},{16,24},{24,32},{32,40},{40,48},{48,56},{56,64},{64,7... | collective-permute-start | bytes 1179656 | tf_op jit(solution)/shard_map/ppermute | solution.py:16
  36.4 20.5 %collective-permute-start.1 = (bf16[128,1536]{1,0:T(8,128)(2,1)}, bf16[128,1536]{1,0:T(8,128)(2,1)S(1)}, u32[]{:S(2)}, u32[]{:S(2)}) collective-permute-start(bf16[128,1536]{1,0:T(8,128)(2,1)} %bitcast.94), channel_id=1, source_target_pairs={{8,0},{16,8},{24,16},{32,24},{40,32},{48,40},{56,48},{64,56},{72,6... | collective-permute-start | bytes 1179656 | tf_op jit(solution)/shard_map/ppermute | solution.py:16
  37.7 20.1 %collective-permute-start = (bf16[128,1536]{1,0:T(8,128)(2,1)}, bf16[128,1536]{1,0:T(8,128)(2,1)S(1)}, u32[]{:S(2)}, u32[]{:S(2)}) collective-permute-start(bf16[128,1536]{1,0:T(8,128)(2,1)} %bitcast.95), channel_id=1, source_target_pairs={{0,8},{8,16},{16,24},{24,32},{32,40},{40,48},{48,56},{56,64},{64,7... | collective-permute-start | bytes 1179656 | tf_op jit(solution)/shard_map/ppermute | solution.py:16
  846.8 26.3 %collective-permute-start.61 = (f32[8,1536]{1,0:T(8,128)S(1)}, f32[8,1536]{1,0:T(8,128)S(1)}, u32[]{:S(2)}, u32[]{:S(2)}) collective-permute-start(f32[8,1536]{1,0:T(8,128)S(1)} %fusion), channel_id=1, source_target_pairs={{0,52},{1,53},{2,54},{3,55},{4,56},{5,57},{6,58},{7,59},{8,60},{9,... | collective-permute-start | bytes 147464
  848.1 26.8 %collective-permute-start.60 = (f32[8,1536]{1,0:T(8,128)S(1)}, f32[8,1536]{1,0:T(8,128)S(1)}, u32[]{:S(2)}, u32[]{:S(2)}) collective-permute-start(f32[8,1536]{1,0:T(8,128)S(1)} %fusion), channel_id=1, source_target_pairs={{0,51},{1,52},{2,53},{3,54},{4,55},{5,56},{6,57},{7,58},{8,59},{9,... | collective-permute-start | bytes 147464
  849.4 26.8 %collective-permute-start.59 = (f32[8,1536]{1,0:T(8,128)S(1)}, f32[8,1536]{1,0:T(8,128)S(1)}, u32[]{:S(2)}, u32[]{:S(2)}) collective-permute-start(f32[8,1536]{1,0:T(8,128)S(1)} %fusion), channel_id=1, source_target_pairs={{0,50},{1,51},{2,52},{3,53},{4,54},{5,55},{6,56},{7,57},{8,58},{9,... | collective-permute-start | bytes 147464
  850.7 29.1 %collective-permute-start.58 = (f32[8,1536]{1,0:T(8,128)S(1)}, f32[8,1536]{1,0:T(8,128)S(1)}, u32[]{:S(2)}, u32[]{:S(2)}) collective-permute-start(f32[8,1536]{1,0:T(8,128)S(1)} %fusion), channel_id=1, source_target_pairs={{0,49},{1,50},{2,51},{3,52},{4,53},{5,54},{6,55},{7,56},{8,57},{9,... | collective-permute-start | bytes 147464
  852.1 29.1 %collective-permute-start.57 = (f32[8,1536]{1,0:T(8,128)S(1)}, f32[8,1536]{1,0:T(8,128)S(1)}, u32[]{:S(2)}, u32[]{:S(2)}) collective-permute-start(f32[8,1536]{1,0:T(8,128)S(1)} %fusion), channel_id=1, source_target_pairs={{0,48},{1,49},{2,50},{3,51},{4,52},{5,53},{6,54},{7,55},{8,56},{9,... | collective-permute-start | bytes 147464
  897.3 17.5 %collective-permute-start.45 = (f32[8,1536]{1,0:T(8,128)S(1)}, f32[8,1536]{1,0:T(8,128)S(1)}, u32[]{:S(2)}, u32[]{:S(2)}) collective-permute-start(f32[8,1536]{1,0:T(8,128)S(1)} %fusion), channel_id=1, source_target_pairs={{0,36},{1,37},{2,38},{3,39},{4,40},{5,41},{6,42},{7,43},{8,44},{9,... | collective-permute-start | bytes 147464
  899.5 28.4 %collective-permute-start.44 = (f32[8,1536]{1,0:T(8,128)S(1)}, f32[8,1536]{1,0:T(8,128)S(1)}, u32[]{:S(2)}, u32[]{:S(2)}) collective-permute-start(f32[8,1536]{1,0:T(8,128)S(1)} %fusion), channel_id=1, source_target_pairs={{0,35},{1,36},{2,37},{3,38},{4,39},{5,40},{6,41},{7,42},{8,43},{9,... | collective-permute-start | bytes 147464
  901.5 39.6 %collective-permute-start.43 = (f32[8,1536]{1,0:T(8,128)S(1)}, f32[8,1536]{1,0:T(8,128)S(1)}, u32[]{:S(2)}, u32[]{:S(2)}) collective-permute-start(f32[8,1536]{1,0:T(8,128)S(1)} %fusion), channel_id=1, source_target_pairs={{0,34},{1,35},{2,36},{3,37},{4,38},{5,39},{6,40},{7,41},{8,42},{9,... | collective-permute-start | bytes 147464
  904.3 50.0 %collective-permute-start.42 = (f32[8,1536]{1,0:T(8,128)S(1)}, f32[8,1536]{1,0:T(8,128)S(1)}, u32[]{:S(2)}, u32[]{:S(2)}) collective-permute-start(f32[8,1536]{1,0:T(8,128)S(1)} %fusion), channel_id=1, source_target_pairs={{0,33},{1,34},{2,35},{3,36},{4,37},{5,38},{6,39},{7,40},{8,41},{9,... | collective-permute-start | bytes 147464
  906.6 60.8 %collective-permute-start.41 = (f32[8,1536]{1,0:T(8,128)S(1)}, f32[8,1536]{1,0:T(8,128)S(1)}, u32[]{:S(2)}, u32[]{:S(2)}) collective-permute-start(f32[8,1536]{1,0:T(8,128)S(1)} %fusion), channel_id=1, source_target_pairs={{0,32},{1,33},{2,34},{3,35},{4,36},{5,37},{6,38},{7,39},{8,40},{9,... | collective-permute-start | bytes 147464
  914.8 65.7 %collective-permute-start.40 = (f32[8,1536]{1,0:T(8,128)S(1)}, f32[8,1536]{1,0:T(8,128)S(1)}, u32[]{:S(2)}, u32[]{:S(2)}) collective-permute-start(f32[8,1536]{1,0:T(8,128)S(1)} %fusion), channel_id=1, source_target_pairs={{0,31},{1,32},{2,33},{3,34},{4,35},{5,36},{6,37},{7,38},{8,39},{9,... | collective-permute-start | bytes 147464
  928.0 65.7 %collective-permute-start.39 = (f32[8,1536]{1,0:T(8,128)S(1)}, f32[8,1536]{1,0:T(8,128)S(1)}, u32[]{:S(2)}, u32[]{:S(2)}) collective-permute-start(f32[8,1536]{1,0:T(8,128)S(1)} %fusion), channel_id=1, source_target_pairs={{0,30},{1,31},{2,32},{3,33},{4,34},{5,35},{6,36},{7,37},{8,38},{9,... | collective-permute-start | bytes 147464
  941.1 65.7 %collective-permute-start.38 = (f32[8,1536]{1,0:T(8,128)S(1)}, f32[8,1536]{1,0:T(8,128)S(1)}, u32[]{:S(2)}, u32[]{:S(2)}) collective-permute-start(f32[8,1536]{1,0:T(8,128)S(1)} %fusion), channel_id=1, source_target_pairs={{0,29},{1,30},{2,31},{3,32},{4,33},{5,34},{6,35},{7,36},{8,37},{9,... | collective-permute-start | bytes 147464
  954.3 65.7 %collective-permute-start.37 = (f32[8,1536]{1,0:T(8,128)S(1)}, f32[8,1536]{1,0:T(8,128)S(1)}, u32[]{:S(2)}, u32[]{:S(2)}) collective-permute-start(f32[8,1536]{1,0:T(8,128)S(1)} %fusion), channel_id=1, source_target_pairs={{0,28},{1,29},{2,30},{3,31},{4,32},{5,33},{6,34},{7,35},{8,36},{9,... | collective-permute-start | bytes 147464
  967.4 65.7 %collective-permute-start.36 = (f32[8,1536]{1,0:T(8,128)S(1)}, f32[8,1536]{1,0:T(8,128)S(1)}, u32[]{:S(2)}, u32[]{:S(2)}) collective-permute-start(f32[8,1536]{1,0:T(8,128)S(1)} %fusion), channel_id=1, source_target_pairs={{0,27},{1,28},{2,29},{3,30},{4,31},{5,32},{6,33},{7,34},{8,35},{9,... | collective-permute-start | bytes 147464
  980.6 65.7 %collective-permute-start.35 = (f32[8,1536]{1,0:T(8,128)S(1)}, f32[8,1536]{1,0:T(8,128)S(1)}, u32[]{:S(2)}, u32[]{:S(2)}) collective-permute-start(f32[8,1536]{1,0:T(8,128)S(1)} %fusion), channel_id=1, source_target_pairs={{0,26},{1,27},{2,28},{3,29},{4,30},{5,31},{6,32},{7,33},{8,34},{9,... | collective-permute-start | bytes 147464
  993.7 65.7 %collective-permute-start.34 = (f32[8,1536]{1,0:T(8,128)S(1)}, f32[8,1536]{1,0:T(8,128)S(1)}, u32[]{:S(2)}, u32[]{:S(2)}) collective-permute-start(f32[8,1536]{1,0:T(8,128)S(1)} %fusion), channel_id=1, source_target_pairs={{0,25},{1,26},{2,27},{3,28},{4,29},{5,30},{6,31},{7,32},{8,33},{9,... | collective-permute-start | bytes 147464
  1006.9 65.7 %collective-permute-start.33 = (f32[8,1536]{1,0:T(8,128)S(1)}, f32[8,1536]{1,0:T(8,128)S(1)}, u32[]{:S(2)}, u32[]{:S(2)}) collective-permute-start(f32[8,1536]{1,0:T(8,128)S(1)} %fusion), channel_id=1, source_target_pairs={{0,24},{1,25},{2,26},{3,27},{4,28},{5,29},{6,30},{7,31},{8,32},{9,... | collective-permute-start | bytes 147464
  1020.0 65.7 %collective-permute-start.32 = (f32[8,1536]{1,0:T(8,128)S(1)}, f32[8,1536]{1,0:T(8,128)S(1)}, u32[]{:S(2)}, u32[]{:S(2)}) collective-permute-start(f32[8,1536]{1,0:T(8,128)S(1)} %fusion), channel_id=1, source_target_pairs={{0,23},{1,24},{2,25},{3,26},{4,27},{5,28},{6,29},{7,30},{8,31},{9,... | collective-permute-start | bytes 147464
  1033.2 66.3 %collective-permute-start.31 = (f32[8,1536]{1,0:T(8,128)S(1)}, f32[8,1536]{1,0:T(8,128)S(1)}, u32[]{:S(2)}, u32[]{:S(2)}) collective-permute-start(f32[8,1536]{1,0:T(8,128)S(1)} %fusion), channel_id=1, source_target_pairs={{0,22},{1,23},{2,24},{3,25},{4,26},{5,27},{6,28},{7,29},{8,30},{9,... | collective-permute-start | bytes 147464
  1046.3 66.3 %collective-permute-start.30 = (f32[8,1536]{1,0:T(8,128)S(1)}, f32[8,1536]{1,0:T(8,128)S(1)}, u32[]{:S(2)}, u32[]{:S(2)}) collective-permute-start(f32[8,1536]{1,0:T(8,128)S(1)} %fusion), channel_id=1, source_target_pairs={{0,21},{1,22},{2,23},{3,24},{4,25},{5,26},{6,27},{7,28},{8,29},{9,... | collective-permute-start | bytes 147464
  1059.5 66.3 %collective-permute-start.29 = (f32[8,1536]{1,0:T(8,128)S(1)}, f32[8,1536]{1,0:T(8,128)S(1)}, u32[]{:S(2)}, u32[]{:S(2)}) collective-permute-start(f32[8,1536]{1,0:T(8,128)S(1)} %fusion), channel_id=1, source_target_pairs={{0,20},{1,21},{2,22},{3,23},{4,24},{5,25},{6,26},{7,27},{8,28},{9,... | collective-permute-start | bytes 147464
  1072.6 66.3 %collective-permute-start.28 = (f32[8,1536]{1,0:T(8,128)S(1)}, f32[8,1536]{1,0:T(8,128)S(1)}, u32[]{:S(2)}, u32[]{:S(2)}) collective-permute-start(f32[8,1536]{1,0:T(8,128)S(1)} %fusion), channel_id=1, source_target_pairs={{0,19},{1,20},{2,21},{3,22},{4,23},{5,24},{6,25},{7,26},{8,27},{9,... | collective-permute-start | bytes 147464
  1085.8 66.3 %collective-permute-start.27 = (f32[8,1536]{1,0:T(8,128)S(1)}, f32[8,1536]{1,0:T(8,128)}, u32[]{:S(2)}, u32[]{:S(2)}) collective-permute-start(f32[8,1536]{1,0:T(8,128)S(1)} %fusion), channel_id=1, source_target_pairs={{0,18},{1,19},{2,20},{3,21},{4,22},{5,23},{6,24},{7,25},{8,26},{9,... | collective-permute-start | bytes 147464
  1099.5 65.7 %collective-permute-start.26 = (f32[8,1536]{1,0:T(8,128)S(1)}, f32[8,1536]{1,0:T(8,128)}, u32[]{:S(2)}, u32[]{:S(2)}) collective-permute-start(f32[8,1536]{1,0:T(8,128)S(1)} %fusion), channel_id=1, source_target_pairs={{0,17},{1,18},{2,19},{3,20},{4,21},{5,22},{6,23},{7,24},{8,25},{9,... | collective-permute-start | bytes 147464
  1112.7 65.7 %collective-permute-start.25 = (f32[8,1536]{1,0:T(8,128)S(1)}, f32[8,1536]{1,0:T(8,128)}, u32[]{:S(2)}, u32[]{:S(2)}) collective-permute-start(f32[8,1536]{1,0:T(8,128)S(1)} %fusion), channel_id=1, source_target_pairs={{0,16},{1,17},{2,18},{3,19},{4,20},{5,21},{6,22},{7,23},{8,24},{9,... | collective-permute-start | bytes 147464
  1125.8 65.7 %collective-permute-start.24 = (f32[8,1536]{1,0:T(8,128)S(1)}, f32[8,1536]{1,0:T(8,128)}, u32[]{:S(2)}, u32[]{:S(2)}) collective-permute-start(f32[8,1536]{1,0:T(8,128)S(1)} %fusion), channel_id=1, source_target_pairs={{0,15},{1,16},{2,17},{3,18},{4,19},{5,20},{6,21},{7,22},{8,23},{9,... | collective-permute-start | bytes 147464
  1139.0 65.7 %collective-permute-start.23 = (f32[8,1536]{1,0:T(8,128)S(1)}, f32[8,1536]{1,0:T(8,128)}, u32[]{:S(2)}, u32[]{:S(2)}) collective-permute-start(f32[8,1536]{1,0:T(8,128)S(1)} %fusion), channel_id=1, source_target_pairs={{0,14},{1,15},{2,16},{3,17},{4,18},{5,19},{6,20},{7,21},{8,22},{9,... | collective-permute-start | bytes 147464
  1152.1 65.7 %collective-permute-start.22 = (f32[8,1536]{1,0:T(8,128)S(1)}, f32[8,1536]{1,0:T(8,128)}, u32[]{:S(2)}, u32[]{:S(2)}) collective-permute-start(f32[8,1536]{1,0:T(8,128)S(1)} %fusion), channel_id=1, source_target_pairs={{0,13},{1,14},{2,15},{3,16},{4,17},{5,18},{6,19},{7,20},{8,21},{9,... | collective-permute-start | bytes 147464
  1165.3 54.6 %collective-permute-start.21 = (f32[8,1536]{1,0:T(8,128)S(1)}, f32[8,1536]{1,0:T(8,128)}, u32[]{:S(2)}, u32[]{:S(2)}) collective-permute-start(f32[8,1536]{1,0:T(8,128)S(1)} %fusion), channel_id=1, source_target_pairs={{0,12},{1,13},{2,14},{3,15},{4,16},{5,17},{6,18},{7,19},{8,20},{9,... | collective-permute-start | bytes 147464
  1178.4 55.6 %collective-permute-start.20 = (f32[8,1536]{1,0:T(8,128)S(1)}, f32[8,1536]{1,0:T(8,128)}, u32[]{:S(2)}, u32[]{:S(2)}) collective-permute-start(f32[8,1536]{1,0:T(8,128)S(1)} %fusion), channel_id=1, source_target_pairs={{0,11},{1,12},{2,13},{3,14},{4,15},{5,16},{6,17},{7,18},{8,19},{9,... | collective-permute-start | bytes 147464
  1191.6 55.6 %collective-permute-start.19 = (f32[8,1536]{1,0:T(8,128)S(1)}, f32[8,1536]{1,0:T(8,128)}, u32[]{:S(2)}, u32[]{:S(2)}) collective-permute-start(f32[8,1536]{1,0:T(8,128)S(1)} %fusion), channel_id=1, source_target_pairs={{0,10},{1,11},{2,12},{3,13},{4,14},{5,15},{6,16},{7,17},{8,18},{9,... | collective-permute-start | bytes 147464
  1204.7 55.6 %collective-permute-start.18 = (f32[8,1536]{1,0:T(8,128)S(1)}, f32[8,1536]{1,0:T(8,128)}, u32[]{:S(2)}, u32[]{:S(2)}) collective-permute-start(f32[8,1536]{1,0:T(8,128)S(1)} %fusion), channel_id=1, source_target_pairs={{0,9},{1,10},{2,11},{3,12},{4,13},{5,14},{6,15},{7,16},{8,17},{9,1... | collective-permute-start | bytes 147464
  1217.8 55.6 %collective-permute-start.17 = (f32[8,1536]{1,0:T(8,128)S(1)}, f32[8,1536]{1,0:T(8,128)}, u32[]{:S(2)}, u32[]{:S(2)}) collective-permute-start(f32[8,1536]{1,0:T(8,128)S(1)} %fusion), channel_id=1, source_target_pairs={{0,8},{1,9},{2,10},{3,11},{4,12},{5,13},{6,14},{7,15},{8,16},{9,17... | collective-permute-start | bytes 147464
  1219.9 66.6 %collective-permute-start.16 = (f32[8,1536]{1,0:T(8,128)S(1)}, f32[8,1536]{1,0:T(8,128)}, u32[]{:S(2)}, u32[]{:S(2)}) collective-permute-start(f32[8,1536]{1,0:T(8,128)S(1)} %fusion), channel_id=1, source_target_pairs={{0,7},{1,8},{2,9},{3,10},{4,11},{5,12},{6,13},{7,14},{8,15},{9,16}... | collective-permute-start | bytes 147464
  1234.0 65.7 %collective-permute-start.15 = (f32[8,1536]{1,0:T(8,128)S(1)}, f32[8,1536]{1,0:T(8,128)}, u32[]{:S(2)}, u32[]{:S(2)}) collective-permute-start(f32[8,1536]{1,0:T(8,128)S(1)} %fusion), channel_id=1, source_target_pairs={{0,6},{1,7},{2,8},{3,9},{4,10},{5,11},{6,12},{7,13},{8,14},{9,15},... | collective-permute-start | bytes 147464
  1247.1 66.6 %collective-permute-start.14 = (f32[8,1536]{1,0:T(8,128)S(1)}, f32[8,1536]{1,0:T(8,128)}, u32[]{:S(2)}, u32[]{:S(2)}) collective-permute-start(f32[8,1536]{1,0:T(8,128)S(1)} %fusion), channel_id=1, source_target_pairs={{0,5},{1,6},{2,7},{3,8},{4,9},{5,10},{6,11},{7,12},{8,13},{9,14},{... | collective-permute-start | bytes 147464
  1260.3 53.5 %collective-permute-start.13 = (f32[8,1536]{1,0:T(8,128)S(1)}, f32[8,1536]{1,0:T(8,128)}, u32[]{:S(2)}, u32[]{:S(2)}) collective-permute-start(f32[8,1536]{1,0:T(8,128)S(1)} %fusion), channel_id=1, source_target_pairs={{0,4},{1,5},{2,6},{3,7},{4,8},{5,9},{6,10},{7,11},{8,12},{9,13},{1... | collective-permute-start | bytes 147464
  1273.4 40.3 %collective-permute-start.12 = (f32[8,1536]{1,0:T(8,128)S(1)}, f32[8,1536]{1,0:T(8,128)}, u32[]{:S(2)}, u32[]{:S(2)}) collective-permute-start(f32[8,1536]{1,0:T(8,128)S(1)} %fusion), channel_id=1, source_target_pairs={{0,3},{1,4},{2,5},{3,6},{4,7},{5,8},{6,9},{7,10},{8,11},{9,12},{10... | collective-permute-start | bytes 147464
  1286.6 27.2 %collective-permute-start.11 = (f32[8,1536]{1,0:T(8,128)S(1)}, f32[8,1536]{1,0:T(8,128)}, u32[]{:S(2)}, u32[]{:S(2)}) collective-permute-start(f32[8,1536]{1,0:T(8,128)S(1)} %fusion), channel_id=1, source_target_pairs={{0,2},{1,3},{2,4},{3,5},{4,6},{5,7},{6,8},{7,9},{8,10},{9,11},{10,... | collective-permute-start | bytes 147464
  1299.7 16.7 %collective-permute-start.10 = (f32[8,1536]{1,0:T(8,128)S(1)}, f32[8,1536]{1,0:T(8,128)}, u32[]{:S(2)}, u32[]{:S(2)}) collective-permute-start(f32[8,1536]{1,0:T(8,128)S(1)} %fusion), channel_id=1, source_target_pairs={{0,1},{1,2},{2,3},{3,4},{4,5},{5,6},{6,7},{7,8},{8,9},{9,10},{10,1... | collective-permute-start | bytes 147464
  1435.2 28.6 %collective-permute-start.7 = (f32[128,1536]{1,0:T(8,128)}, f32[128,1536]{1,0:T(8,128)}, u32[]{:S(2)}, u32[]{:S(2)}) collective-permute-start(f32[128,1536]{1,0:T(8,128)} %copy.85), channel_id=1, source_target_pairs={{0,8},{8,16},{16,24},{24,32},{32,40},{40,48},{48,56},{56,64},{64,7... | collective-permute-start | bytes 2359304 | tf_op jit(solution)/shard_map/ppermute | solution.py:16
  1439.8 24.0 %collective-permute-start.6 = (f32[128,1536]{1,0:T(8,128)}, f32[128,1536]{1,0:T(8,128)}, u32[]{:S(2)}, u32[]{:S(2)}) collective-permute-start(f32[128,1536]{1,0:T(8,128)} %copy.83), channel_id=1, source_target_pairs={{8,0},{16,8},{24,16},{32,24},{40,32},{48,40},{56,48},{64,56},{72,6... | collective-permute-start | bytes 2359304 | tf_op jit(solution)/shard_map/ppermute | solution.py:16
  (80 other events, 14642.3 us)
Sparse Core Ops, SparseCore 0:
  9.8 67.9 all-gather.1
where the time goes:
time: 1500 us; the launch traced here: 1470 us
  blocking collectives  756 us (50%)
  starting transfers between devices  536 us (36%)
  local copies, waits for them, and re-layouts  128 us (9%)
  matrix products  23.7 us (2%)
  between operations  17.6 us (1%)
    unnamed x1, blocking collectives  756 us
    unnamed x64, starting transfers between devices  487 us
    unnamed x113, local copies, waits for them, and re-layouts  105 us
    ppermute x10, starting transfers between devices, shifted(): lax.ppermute(value, axis, [(source, source + steps) for source in range(f...  48.7 us
  transfers between devices with their start and end apart: 75, of which 3 were waited for; matrix products, arithmetic and copies ran while one was open for 61% of the time, Pallas kernels for 0%

commit v1 on v0

v1 whole, which is shorter than its diff:
```python
import jax
import jax.numpy as jnp
import numpy as np
from jax import lax
from jax.experimental import pallas as pl
from jax.experimental.pallas import tpu as pltpu
from jax.sharding import PartitionSpec as P

HEADS = 12
HEAD_DIM = 128
TILE = 128
HD = HEADS * HEAD_DIM
SCALE = HEAD_DIM**-0.5
MASKED = -1e30

SIZES = (8, 2, 2, 2, 4)
NAMES = ("z", "yhi", "core", "ylo", "x")
FRAME = ("z", "yhi", "core")
FSDP = ("ylo", "x")
TILES = 32
ROWS_OUT = 6
GROUP = 8
GROUP_ROWS = HD // GROUP

F32 = jnp.float32
BF16 = jnp.bfloat16
VMEM = pltpu.VMEM
NT = (((1,), (1,)), ((), ()))
NN = (((1,), (0,)), ((), ()))
TN = (((0,), (0,)), ((), ()))


def dot(a, b, dims=NN):
    return lax.dot_general(a, b, dims, preferred_element_type=F32)


def next_tile(value, step):
    return lax.ppermute(value, FRAME, [(i, (i + step) % TILES) for i in range(TILES)])


def core_swap(value):
    return lax.ppermute(value, "core", [(0, 1), (1, 0)])


def gather_x(value):
    spread = jnp.broadcast_to(value[None], (4,) + value.shape)
    return lax.all_to_all(spread, "x", 0, 0, tiled=True)


def head(h):
    return slice(h * HEAD_DIM, (h + 1) * HEAD_DIM)


def biases(meta, position):
    def sees(q, k):
        frame = meta[q, 0]
        return (meta[k, 0] >= frame - meta[q, 1]) & (meta[k, 0] <= frame + meta[q, 2])

    has = (position > 0, None, position < TILES - 1)
    out = {}
    for t in (0, 2):
        out["row", t] = jnp.where(sees(1, t) & has[t], 0.0, MASKED).astype(F32)
        out["col", t] = jnp.where(sees(t, 1) & has[t], 0.0, MASKED).astype(F32)
    return out


def forward_kernel(meta, pos, q, kl, ko, kr, vl, vo, vr, order, att, att_t, stats):
    bias = biases(meta, pos[0])
    lane = lax.broadcasted_iota(jnp.int32, (TILE, 128), 1)
    total = jnp.zeros((TILE, 128), F32)
    for h in range(HEADS):
        c = head(h)
        qh = q[:, c]
        sl = dot(qh, kl[:, c], NT) * SCALE + bias["row", 0]
        so = dot(qh, ko[:, c], NT) * SCALE
        sr = dot(qh, kr[:, c], NT) * SCALE + bias["row", 2]
        top = jnp.max(jnp.maximum(jnp.maximum(sl, so), sr), axis=1, keepdims=True)
        el, eo, er = jnp.exp(sl - top), jnp.exp(so - top), jnp.exp(sr - top)
        mass = jnp.sum(el + eo + er, axis=1, keepdims=True)
        inv = 1.0 / mass
        out = dot((el * inv).astype(BF16), vl[:, c])
        out += dot((eo * inv).astype(BF16), vo[:, c])
        out += dot((er * inv).astype(BF16), vr[:, c])
        att[:, c] = out.astype(BF16)
        total = jnp.where(lane == h, top + jnp.log(mass), total)
    stats[...] = total
    for g in range(GROUP):
        cols = slice(g * GROUP_ROWS, (g + 1) * GROUP_ROWS)
        moved = lax.dot_general(
            order[cols, :], att[...], NT, preferred_element_type=F32
        )
        att_t[g] = moved.astype(BF16)


def weight_kernel(core, att_t, og_mine, og_other, out):
    c = core[0]
    acc = jnp.zeros((GROUP_ROWS, HD), F32)
    for j in range(4):
        acc += dot(att_t[c * 4 + j], og_mine[j])
        acc += dot(att_t[(1 - c) * 4 + j], og_other[j])
    out[...] = (acc * float(GROUP * TILES * TILE) ** -0.5).astype(BF16)


def grad_attended_kernel(core, w_mine, w_other, ogl, ogo, ogr, att, stats, gal, gao, gar, out):
    c = core[0]
    lane = lax.broadcasted_iota(jnp.int32, (TILE, 128), 1)
    total = stats[...]
    half = HD // 2
    for side, w in ((c, w_mine), (1 - c, w_other)):
        for i in range(HEADS // 2):
            block = w[i * HEAD_DIM : (i + 1) * HEAD_DIM, :]
            cols = pl.ds(pl.multiple_of(side * half + i * HEAD_DIM, HEAD_DIM), HEAD_DIM)
            gal[:, cols] = dot(ogl[...], block, NT).astype(BF16)
            gar[:, cols] = dot(ogr[...], block, NT).astype(BF16)
            own = dot(ogo[...], block, NT).astype(BF16)
            gao[:, cols] = own
            delta = jnp.sum(own.astype(F32) * att[:, cols].astype(F32), axis=1, keepdims=True)
            total = jnp.where(lane == HEADS + side * (HEADS // 2) + i, delta, total)
    out[...] = total


def project_kernel(core, w_mine, w_other, att, out):
    half = HD // 2
    c = core[0]
    mine = att[:, pl.ds(pl.multiple_of(c * half, half), half)]
    other = att[:, pl.ds(pl.multiple_of((1 - c) * half, half), half)]
    out[...] = (dot(mine, w_mine[...]) + dot(other, w_other[...])).astype(BF16)


def pair_grads(qh, kh, vh, gh, lse, delta, bias):
    s = dot(qh, kh, NT) * SCALE
    if bias is not None:
        s = s + bias
    p = jnp.exp(s - lse)
    dp = dot(gh, vh, NT)
    ds = (p * (dp - delta) * SCALE).astype(BF16)
    return p.astype(BF16), ds


def row_kernel(meta, pos, q, kl, ko, kr, vl, vo, vr, ga, stats, dq, dk, dv):
    bias = biases(meta, pos[0])
    st = stats[...]
    for h in range(HEADS):
        c = head(h)
        qh, gh = q[:, c], ga[:, c]
        lse, delta = st[:, h : h + 1], st[:, HEADS + h : HEADS + h + 1]
        _, dsl = pair_grads(qh, kl[:, c], vl[:, c], gh, lse, delta, bias["row", 0])
        po, dso = pair_grads(qh, ko[:, c], vo[:, c], gh, lse, delta, None)
        _, dsr = pair_grads(qh, kr[:, c], vr[:, c], gh, lse, delta, bias["row", 2])
        dq[:, c] = (dot(dsl, kl[:, c]) + dot(dso, ko[:, c]) + dot(dsr, kr[:, c])).astype(BF16)
        dk[:, c] = dot(dso, qh, TN)
        dv[:, c] = dot(po, gh, TN)


def column_kernel(meta, pos, ql, qr, ko, vo, gal, gar, sl, sr, dk0, dv0, dk, dv):
    bias = biases(meta, pos[0])
    stl, str_ = sl[...], sr[...]
    for h in range(HEADS):
        c = head(h)
        kh, vh = ko[:, c], vo[:, c]
        dkh, dvh = dk0[:, c], dv0[:, c]
        for q, g, st, t in ((ql, gal, stl, 0), (qr, gar, str_, 2)):
            qh, gh = q[:, c], g[:, c]
            lse, delta = st[:, h : h + 1], st[:, HEADS + h : HEADS + h + 1]
            p, ds = pair_grads(qh, kh, vh, gh, lse, delta, bias["col", t])
            dkh = dkh + dot(ds, qh, TN)
            dvh = dvh + dot(p, gh, TN)
        dk[:, c] = dkh.astype(BF16)
        dv[:, c] = dvh.astype(BF16)


def call(kernel, scalars, arrays, outs, flops, cost_bytes, trans=0):
    return pl.pallas_call(
        kernel,
        in_specs=[pl.BlockSpec(memory_space=pltpu.SMEM)] * len(scalars)
        + [pl.BlockSpec(memory_space=VMEM)] * len(arrays),
        out_specs=[pl.BlockSpec(memory_space=VMEM)] * len(outs),
        out_shape=[jax.ShapeDtypeStruct(s, d) for s, d in outs],
        cost_estimate=pl.CostEstimate(flops=flops, bytes_accessed=cost_bytes, transcendentals=trans),
        compiler_params=pltpu.CompilerParams(vmem_limit_bytes=40 * 1024 * 1024),
    )(*scalars, *arrays)


def column_order():
    features = np.arange(HD).reshape(SIZES + (ROWS_OUT,))
    return features.transpose(2, 4, 0, 1, 3, 5).reshape(-1)


def shards(query_rows, key_rows, value_rows, frame_of, reach_back, reach_ahead, out_weight, out_grad):
    position = lax.axis_index(FRAME)
    core = lax.axis_index("core")
    q, k, v, og = query_rows[0], key_rows[0], value_rows[0], out_grad[0]
    tile = (TILE, HD)
    small = (TILE, 128)
    pos = position.astype(jnp.int32).reshape(1)
    which = core.astype(jnp.int32).reshape(1)

    own_meta = jnp.stack([frame_of[0, 0], reach_back[0, 0], reach_ahead[0, 0]])
    meta_l, meta_r = next_tile(own_meta, 1), next_tile(own_meta, -1)
    meta = jnp.stack([meta_l, own_meta, meta_r])
    kl, kr = next_tile(k, 1), next_tile(k, -1)
    vl, vr = next_tile(v, 1), next_tile(v, -1)

    og_mine = gather_x(og)
    og_other = core_swap(og_mine)

    half_index = core * 2 + lax.axis_index("ylo")
    passed = lax.ppermute(out_weight, ("core", "ylo"), [(0, 1), (3, 2)])
    chosen = jnp.where((half_index == 0) | (half_index == 3), out_weight, passed)
    w_mine = gather_x(chosen).reshape(HD // 2, HD)
    w_other = core_swap(w_mine)

    order = jnp.asarray(column_order(), jnp.int32)
    order = (order[:, None] == lax.broadcasted_iota(jnp.int32, (HD, HD), 1)).astype(BF16)

    flops = 2 * TILE * TILE * HD
    att, att_t, stats = call(
        forward_kernel,
        (meta, pos),
        (q, kl, k, kr, vl, v, vr, order),
        [(tile, BF16), ((GROUP, GROUP_ROWS, TILE), BF16), (small, F32)],
        6 * flops + 2 * TILE * HD * HD,
        8 * 1024 * 1024,
        HEADS * TILE * TILE * 3,
    )

    q2, og2, _, _, _, _ = lax.optimization_barrier((q, og, kl, kr, vl, vr))
    ql, qr = next_tile(q2, 1), next_tile(q2, -1)
    ogl, ogr = next_tile(og2, 1), next_tile(og2, -1)

    regrouped = lax.all_to_all(att_t, ("core", "x"), 0, 0, tiled=True)
    (partial,) = call(
        weight_kernel,
        (which,),
        (regrouped, og_mine, og_other),
        [((GROUP_ROWS, HD), BF16)],
        2 * TILE * HD * HD,
        4 * 1024 * 1024,
    )
    along_z = lax.all_to_all(partial.reshape(8, GROUP_ROWS // 8, HD), "z", 0, 0, tiled=True)
    sum_z = jnp.sum(along_z.astype(F32), axis=0)
    along_y = lax.all_to_all(sum_z.reshape(4, ROWS_OUT, HD), ("yhi", "ylo"), 0, 0, tiled=True)
    grad_weight = jnp.sum(along_y, axis=0)

    gal, gao, gar, stats = call(
        grad_attended_kernel,
        (which,),
        (w_mine, w_other, ogl, og, ogr, att, stats),
        [(tile, BF16), (tile, BF16), (tile, BF16), (small, F32)],
        6 * TILE * HD * HD,
        8 * 1024 * 1024,
    )
    stats_l, stats_r = next_tile(stats, 1), next_tile(stats, -1)
    (layer_out,) = call(
        project_kernel,
        (which,),
        (w_mine, w_other, att),
        [(tile, BF16)],
        2 * TILE * HD * HD,
        6 * 1024 * 1024,
    )
    dq, dk0, dv0 = call(
        row_kernel,
        (meta, pos),
        (q, kl, k, kr, vl, v, vr, gao, stats),
        [(tile, BF16), (tile, F32), (tile, F32)],
        11 * flops,
        6 * 1024 * 1024,
        HEADS * TILE * TILE * 3,
    )
    dk, dv = call(
        column_kernel,
        (meta, pos),
        (ql, qr, k, v, gal, gar, stats_l, stats_r, dk0, dv0),
        [(tile, BF16), (tile, BF16)],
        8 * flops,
        6 * 1024 * 1024,
        HEADS * TILE * TILE * 2,
    )
    return layer_out[None], dq[None], dk[None], dv[None], grad_weight


def solution(mesh):
    fine = jax.sharding.Mesh(np.asarray(mesh.devices).reshape(SIZES), NAMES)
    tokens = P(FSDP, FRAME, None)
    tiles = P(FSDP, FRAME)
    in_specs = (tokens, tokens, tokens, tiles, tiles, tiles, P(FSDP, None), tokens)
    out_specs = (tokens, tokens, tokens, tokens, P(FRAME + FSDP, None))
    return jax.shard_map(shards, mesh=fine, in_specs=in_specs, out_specs=out_specs, check_vma=False)
```

time: 1500 us -> 165 us (0.11); the launches traced: 1470 us -> 164 us
  blocking collectives: 756 us -> 22.1 us
  starting transfers between devices: 536 us -> 52.6 us
  local copies, waits for them, and re-layouts: 128 us -> 13.7 us
  Pallas kernels: 0 us -> 32.3 us
  waiting for transfers between devices: 4.29 us -> 33.7 us
  matrix products: 23.7 us -> 0 us
    unnamed x1 -> x0, blocking collectives: 756 us -> none
    unnamed x64 -> x0, starting transfers between devices: 487 us -> none
    unnamed x113 -> x36, local copies, waits for them, and re-layouts: 105 us -> 8 us
    pallas_call x0 -> x6, Pallas kernels: none -> 32.3 us  [call(): pl.pallas_call(kernel, in_specs=[pl.BlockSpec(memory_space=pltpu.SMEM)] *...]
    all_to_all x0 -> x3, waiting for transfers between devices: none -> 25.8 us  [the longest x2 17.2 us: gather_x(): return lax.all_to_all(spread, 'x', 0, 0, tiled=True)]
    dot_general x9 -> x0, matrix products: 23.7 us -> none  [the longest x1 5.1 us: shards(): lax.dot_general(attended, grad_out, (((0,), (0,)), ((), ())), preferred_e...]
    all_to_all x0 -> x2, blocking collectives: none -> 22.1 us  [the longest x1 11.1 us: shards(): regrouped = lax.all_to_all(att_t, ('core', 'x'), 0, 0, tiled=True)]
    all_to_all x0 -> x3, starting transfers between devices: none -> 20.4 us  [the longest x2 11 us: gather_x(): return lax.all_to_all(spread, 'x', 0, 0, tiled=True)]
  transfers between devices with their start and end apart: 75 -> 18, of which waited for: 3 -> 5; matrix products, arithmetic and copies ran while one was open for 61% -> 5% of each run, Pallas kernels for 0% -> 15%
where the time goes in v1:
time: 165 us; the launch traced here: 164 us
  starting transfers between devices  52.6 us (32%)
  waiting for transfers between devices  33.7 us (20%)
  Pallas kernels  32.3 us (20%)
  blocking collectives  22.1 us (13%)
  local copies, waits for them, and re-layouts  13.7 us (8%)
  other arithmetic  6.58 us (4%)
  between operations  2.78 us (2%)
    pallas_call x6, Pallas kernels, call(): pl.pallas_call(kernel, in_specs=[pl.BlockSpec(memory_space=pltpu.SMEM)] *...  32.3 us
    ppermute x12, starting transfers between devices, next_tile(): lax.ppermute(value, FRAME, [(i, (i + step) % TILES) for i in range(TILES)])  28.9 us
    all_to_all x2, waiting for transfers between devices, gather_x(): return lax.all_to_all(spread, 'x', 0, 0, tiled=True)  17.2 us
    all_to_all x1, blocking collectives, shards(): regrouped = lax.all_to_all(att_t, ('core', 'x'), 0, 0, tiled=True)  11.1 us
    all_to_all x1, blocking collectives, shards(): lax.all_to_all(sum_z.reshape(4, ROWS_OUT, HD), ('yhi', 'ylo'), 0, 0, tile...  11 us
    all_to_all x2, starting transfers between devices, gather_x(): return lax.all_to_all(spread, 'x', 0, 0, tiled=True)  11 us
    all_to_all x1, starting transfers between devices, shards(): lax.all_to_all(partial.reshape(8, GROUP_ROWS // 8, HD), 'z', 0, 0, tiled=...  9.44 us
    all_to_all x1, waiting for transfers between devices, shards(): lax.all_to_all(partial.reshape(8, GROUP_ROWS // 8, HD), 'z', 0, 0, tiled=...  8.56 us
  transfers between devices with their start and end apart: 18, of which 5 were waited for; matrix products, arithmetic and copies ran while one was open for 5% of the time, Pallas kernels for 15%

profile of v1, /device:TPU:2, one launch (start us, length us, event | category | flops | bytes accessed | tf_op | source)
XLA Modules:
  0.0 163.9 jit_solution(1766399973591973376)
XLA Ops:
  0.6 2.4 %broadcast_in_dim.29 = bf16[4,128,1536]{2,1,0:T(8,128)(2,1)} broadcast(bf16[128,1536]{1,0:T(8,128)(2,1)} %bitcast.43), dimensions={1,2} | broadcast | bytes 1966080 | tf_op jit(solution)/shard_map/broadcast_in_dim | solution.py:46
  3.0 5.8 %all-to-all-start.2 = ((bf16[4,128,1536]{2,1,0:T(8,128)(2,1)}), bf16[4,128,1536]{2,1,0:T(8,128)(2,1)S(1)}, u32[]{:S(2)}, u32[]{:S(2)}) async-start(bf16[4,128,1536]{2,1,0:T(8,128)(2,1)} %broadcast_in_dim.29), calls=%async_computation.2 | async-start | bytes 3145728 | tf_op jit(solution)/shard_map/all_to_all | solution.py:47
  8.8 3.3 %collective-permute-start = (bf16[192,1536]{1,0:T(8,128)(2,1)S(1)}, bf16[192,1536]{1,0:T(8,128)(2,1)}, u32[]{:S(2)}, u32[]{:S(2)}) collective-permute-start(bf16[192,1536]{1,0:T(8,128)(2,1)S(1)} %copy-done.16), channel_id=1, source_target_pairs={{0,4},{12,8},{1,5},{13,9},{2,6},{14,10},{3,7},{15,11},{16,20},{28,... | collective-permute-start | bytes 1769480 | tf_op jit(solution)/shard_map/ppermute | solution.py:208
  12.1 6.6 %collective-permute-done = bf16[192,1536]{1,0:T(8,128)(2,1)} collective-permute-done((bf16[192,1536]{1,0:T(8,128)(2,1)S(1)}, bf16[192,1536]{1,0:T(8,128)(2,1)}, u32[]{:S(2)}, u32[]{:S(2)}) %collective-permute-start) | collective-permute-done | bytes 589856 | tf_op jit(solution)/shard_map/ppermute | solution.py:208
  18.7 0.1 broadcast_select_fusion
  18.8 8.3 %all-to-all-done.2.og_mine = bf16[4,128,1536]{2,1,0:T(8,128)(2,1)S(1)} async-done(((bf16[4,128,1536]{2,1,0:T(8,128)(2,1)}), bf16[4,128,1536]{2,1,0:T(8,128)(2,1)S(1)}, u32[]{:S(2)}, u32[]{:S(2)}) %all-to-all-start.2) | async-done | bytes 1572896 | tf_op jit(solution)/shard_map/all_to_all | solution.py:47
  27.1 1.7 %broadcast_in_dim.24 = bf16[4,192,1536]{2,1,0:T(8,128)(2,1)} broadcast(bf16[192,1536]{1,0:T(8,128)(2,1)S(1)} %broadcast_select_fusion), dimensions={1,2} | broadcast | bytes 2949120 | tf_op jit(solution)/shard_map/broadcast_in_dim | solution.py:46
  28.8 0.2 copy-done.1
  29.0 5.2 %all-to-all-start = ((bf16[4,192,1536]{2,1,0:T(8,128)(2,1)}), bf16[4,192,1536]{2,1,0:T(8,128)(2,1)S(1)}, u32[]{:S(2)}, u32[]{:S(2)}) async-start(bf16[4,192,1536]{2,1,0:T(8,128)(2,1)} %broadcast_in_dim.24), calls=%async_computation | async-start | bytes 4718592 | tf_op jit(solution)/shard_map/all_to_all | solution.py:47
  36.2 0.1 pad_add_fusion.1
  36.3 3.3 %collective-permute-start.2 = (s32[3]{0:T(128)S(1)}, s32[3]{0:T(128)S(1)}, u32[]{:S(2)}, u32[]{:S(2)}) collective-permute-start(s32[3]{0:T(128)S(1)} %pad_add_fusion.1), channel_id=1, source_target_pairs={{0,8},{8,16},{16,24},{24,32},{32,40},{40,48},{48,56},{56,64},{64,7... | collective-permute-start | bytes 44 | tf_op jit(solution)/shard_map/ppermute | solution.py:38
  39.6 3.2 %collective-permute-start.3 = (s32[3]{0:T(128)S(1)}, s32[3]{0:T(128)S(1)}, u32[]{:S(2)}, u32[]{:S(2)}) collective-permute-start(s32[3]{0:T(128)S(1)} %pad_add_fusion.1), channel_id=1, source_target_pairs={{0,248},{8,0},{16,8},{24,16},{32,24},{40,32},{48,40},{56,48},{64,5... | collective-permute-start | bytes 44 | tf_op jit(solution)/shard_map/ppermute | solution.py:38
  42.8 2.1 %collective-permute-start.5 = (bf16[128,1536]{1,0:T(8,128)(2,1)S(1)}, bf16[128,1536]{1,0:T(8,128)(2,1)}, u32[]{:S(2)}, u32[]{:S(2)}) collective-permute-start(bf16[128,1536]{1,0:T(8,128)(2,1)S(1)} %bitcast.29), channel_id=1, source_target_pairs={{0,248},{8,0},{16,8},{24,16},{32,24},{40,32},{48,40},{56,48},{64,5... | collective-permute-start | bytes 1179656 | tf_op jit(solution)/shard_map/ppermute | solution.py:38
  45.0 0.0 collective-permute-start.6
  45.0 1.3 collective-permute-done.2
  46.3 4.0 %collective-permute-start.7 = (bf16[128,1536]{1,0:T(8,128)(2,1)S(1)}, bf16[128,1536]{1,0:T(8,128)(2,1)}, u32[]{:S(2)}, u32[]{:S(2)}) collective-permute-start(bf16[128,1536]{1,0:T(8,128)(2,1)S(1)} %bitcast.34), channel_id=1, source_target_pairs={{0,248},{8,0},{16,8},{24,16},{32,24},{40,32},{48,40},{56,48},{64,5... | collective-permute-start | bytes 1179656 | tf_op jit(solution)/shard_map/ppermute | solution.py:38
  50.4 0.0 copy-start.7
  50.4 0.7 copy-done.7
  51.1 8.9 %all-to-all-done = bf16[4,192,1536]{2,1,0:T(8,128)(2,1)S(1)} async-done(((bf16[4,192,1536]{2,1,0:T(8,128)(2,1)}), bf16[4,192,1536]{2,1,0:T(8,128)(2,1)S(1)}, u32[]{:S(2)}, u32[]{:S(2)}) %all-to-all-start) | async-done | bytes 2359328 | tf_op jit(solution)/shard_map/all_to_all | solution.py:47
  60.0 3.0 %fusion.order = bf16[1536,1536]{1,0:T(8,128)(2,1)} fusion(s32[1536]{0:T(1024)S(1)} %copy-done.17), kind=kLoop, calls=%fused_computation.1 | loop fusion | flops 4718592 | bytes 4724736 | tf_op jit(solution)/shard_map/convert_element_type | solution.py:214
  63.0 0.1 fusion.1
  63.1 2.3 %copy-done = bf16[1536,1536]{1,0:T(8,128)(2,1)S(1)} copy-done((bf16[1536,1536]{1,0:T(8,128)(2,1)S(1)}, bf16[1536,1536]{1,0:T(8,128)(2,1)}, u32[]{:S(2)}) %copy-start) | copy-done | bytes 4718616
  65.5 1.0 copy-done.8
  66.5 7.2 %shard_map.128 = (bf16[128,1536]{1,0:T(8,128)(2,1)S(1)}, bf16[8,192,128]{2,1,0:T(8,128)(2,1)S(1)}, f32[128,128]{1,0:T(8,128)S(1)}) custom-call(s32[3,3]{1,0:T(4,128)S(1)} %pad_add_fusion.meta, s32[1]{0:T(128)} %bitcast.8.pos, bf16[128,1536]{1,0:T(8,128)(2,1)S(1)} %bitcast.39, bf16[128,1536]{1,0:T(8,128)(2,1)S(1)} %copy-done.8, ...), custom_call_target="tpu_custom_call" | custom-call | flops 905969664 | bytes 8388608 | tf_op jit(solution)/shard_map/pallas_call | solution.py:173
  73.7 0.0 copy-start.10
  73.7 11.1 %all_to_all.25.att_t = bf16[8,192,128]{2,1,0:T(8,128)(2,1)S(1)} all-to-all(bf16[8,192,128]{2,1,0:T(8,128)(2,1)S(1)} %get-tuple-element.32), channel_id=1, replica_groups=mesh['z'=8,'yhi'=2,'core'=2,'ylo'=2,'x'=4] {'core','x'}, dimensions={0} | all-to-all | bytes 786432 | tf_op jit(solution)/shard_map/all_to_all | solution.py:231
  84.9 2.8 %shard_map.133 = bf16[192,1536]{1,0:T(8,128)(2,1)S(1)} custom-call(s32[1]{0:T(128)} %bitcast.core, bf16[8,192,128]{2,1,0:T(8,128)(2,1)S(1)} %all_to_all.25.att_t, bf16[4,128,1536]{2,1,0:T(8,128)(2,1)S(1)} %copy-done.2, bf16[4,128,1536]{2,1,0:T(8,128)(2,1)} %collective-permute-done.14.og_other), custom_call_target="tpu_custom_call" | custom-call | flops 603979776 | bytes 4194304 | tf_op jit(solution)/shard_map/pallas_call | solution.py:173
  87.7 0.8 copy-done.5
  88.5 9.4 %all-to-all-start.3 = ((bf16[8,24,1536]{2,1,0:T(8,128)(2,1)}), bf16[8,24,1536]{2,1,0:T(8,128)(2,1)}, u32[]{:S(2)}, u32[]{:S(2)}) async-start(bf16[8,24,1536]{2,1,0:T(8,128)(2,1)} %bitcast.38), calls=%async_computation.3 | async-start | bytes 1179648 | tf_op jit(solution)/shard_map/all_to_all | solution.py:240
  98.0 0.0 collective-permute-start.8
  98.0 5.3 %collective-permute-start.9 = (bf16[128,1536]{1,0:T(8,128)(2,1)}, bf16[128,1536]{1,0:T(8,128)(2,1)}, u32[]{:S(2)}, u32[]{:S(2)}) collective-permute-start(bf16[128,1536]{1,0:T(8,128)(2,1)} %bitcast.45), channel_id=1, source_target_pairs={{0,248},{8,0},{16,8},{24,16},{32,24},{40,32},{48,40},{56,48},{64,5... | collective-permute-start | bytes 1179656 | tf_op jit(solution)/shard_map/ppermute | solution.py:38
  103.3 5.4 %collective-permute-start.11 = (bf16[128,1536]{1,0:T(8,128)(2,1)S(1)}, bf16[128,1536]{1,0:T(8,128)(2,1)}, u32[]{:S(2)}, u32[]{:S(2)}) collective-permute-start(bf16[128,1536]{1,0:T(8,128)(2,1)S(1)} %bitcast.41), channel_id=1, source_target_pairs={{0,248},{8,0},{16,8},{24,16},{32,24},{40,32},{48,40},{56,48},{64,5... | collective-permute-start | bytes 1179656 | tf_op jit(solution)/shard_map/ppermute | solution.py:38
  108.7 8.6 %all-to-all-done.3 = bf16[8,24,1536]{2,1,0:T(8,128)(2,1)} async-done(((bf16[8,24,1536]{2,1,0:T(8,128)(2,1)}), bf16[8,24,1536]{2,1,0:T(8,128)(2,1)}, u32[]{:S(2)}, u32[]{:S(2)}) %all-to-all-start.3) | async-done | bytes 589856 | tf_op jit(solution)/shard_map/all_to_all | solution.py:240
  117.2 1.8 %convert_reduce_fusion = f32[24,1536]{1,0:T(8,128)} fusion(bf16[8,24,1536]{2,1,0:T(8,128)(2,1)} %all-to-all-done.3), kind=kLoop, calls=%fused_computation.2 | loop fusion | flops 552960 | bytes 737280 | tf_op jit(solution)/shard_map/reduce_sum | solution.py:241
  119.1 1.6 reshape.31
  120.7 11.0 %all_to_all.26 = f32[4,6,1536]{2,1,0:T(8,128)} all-to-all(f32[4,6,1536]{2,1,0:T(8,128)} %reshape.31), channel_id=1, replica_groups=mesh['z'=8,'yhi'=2,'core'=2,'ylo'=2,'x'=4] {'yhi','ylo'}, dimensions={0} | all-to-all | bytes 294912 | tf_op jit(solution)/shard_map/all_to_all | solution.py:242
  131.7 1.6 reduce_sum.19
  133.2 0.0 copy-start.11
  133.2 1.0 copy-done.11
  134.2 1.0 copy-done.13
  135.2 0.8 copy-done.15
  136.1 5.8 %shard_map.130 = (bf16[128,1536]{1,0:T(8,128)(2,1)S(1)}, bf16[128,1536]{1,0:T(8,128)(2,1)S(1)}, bf16[128,1536]{1,0:T(8,128)(2,1)S(1)}, f32[128,128]{1,0:T(8,128)S(1)}) custom-call(s32[1]{0:T(128)} %bitcast.core, bf16[768,1536]{1,0:T(8,128)(2,1)S(1)} %bitcast.26, bf16[768,1536]{1,0:T(8,128)(2,1)} %collective-permute-done.1.w_other, ...), custom_call_target="tpu_custom_call" | custom-call | flops 1811939328 | bytes 8388608 | tf_op jit(solution)/shard_map/pallas_call | solution.py:173
  141.9 0.0 copy-start.12
  141.9 0.1 collective-permute-start.12
  142.0 5.3 %collective-permute-start.13 = (f32[128,128]{1,0:T(8,128)S(1)}, f32[128,128]{1,0:T(8,128)S(1)}, u32[]{:S(2)}, u32[]{:S(2)}) collective-permute-start(f32[128,128]{1,0:T(8,128)S(1)} %get-tuple-element.23.stats), channel_id=1, source_target_pairs={{0,248},{8,0},{16,8},{24,16},{32,24},{40,32},{48,40},{56,48},{64,5... | collective-permute-start | bytes 196616 | tf_op jit(solution)/shard_map/ppermute | solution.py:38
  147.3 5.7 %shard_map.131 = (bf16[128,1536]{1,0:T(8,128)(2,1)}, f32[128,1536]{1,0:T(8,128)S(1)}, f32[128,1536]{1,0:T(8,128)S(1)}) custom-call(s32[3,3]{1,0:T(4,128)S(1)} %pad_add_fusion.meta, s32[1]{0:T(128)} %bitcast.8.pos, bf16[128,1536]{1,0:T(8,128)(2,1)S(1)} %bitcast.42, bf16[128,1536]{1,0:T(8,128)(2,1)S(1)} %copy-done.9, bf16[128,1536]{1,0:T(8,128)(2,1)S(1)} %bitcast.31, ...), custom_call_target="tpu_custom_call" | custom-call | flops 553648128 | bytes 6291456 | tf_op jit(solution)/shard_map/pallas_call | solution.py:173
  153.0 3.2 %shard_map.129 = bf16[128,1536]{1,0:T(8,128)(2,1)} custom-call(s32[1]{0:T(128)} %bitcast.core, bf16[768,1536]{1,0:T(8,128)(2,1)S(1)} %bitcast.27, bf16[768,1536]{1,0:T(8,128)(2,1)} %collective-permute-done.1.w_other, bf16[128,1536]{1,0:T(8,128)(2,1)S(1)} %copy-done.12), custom_call_target="tpu_custom_call" | custom-call | flops 603979776 | bytes 6291456 | tf_op jit(solution)/shard_map/pallas_call | solution.py:173
  156.2 7.7 %shard_map.132 = (bf16[128,1536]{1,0:T(8,128)(2,1)}, bf16[128,1536]{1,0:T(8,128)(2,1)}) custom-call(s32[3,3]{1,0:T(4,128)S(1)} %pad_add_fusion.meta, s32[1]{0:T(128)} %bitcast.8.pos, bf16[128,1536]{1,0:T(8,128)(2,1)} %collective-permute-done.10.ql, bf16[128,1536]{1,0:T(8,128)(2,1)} %collective-permute-done.11.qr, bf16[128,1536]{1,0:T(8,128)(2,1)S(1)} %bitcast.32, ...), custom_call_target="tpu_custom_call" | custom-call | flops 402653184 | bytes 6291456 | tf_op jit(solution)/shard_map/pallas_call | solution.py:173
  (42 shorter events, 0.1 us)
Async XLA Ops:
  0.6 8.2 %copy-start.16 = (bf16[192,1536]{1,0:T(8,128)(2,1)S(1)}, bf16[192,1536]{1,0:T(8,128)(2,1)}, u32[]{:S(2)}) copy-start(bf16[192,1536]{1,0:T(8,128)(2,1)} %param.15) | copy-start | bytes 1769476
  3.0 24.1 %all-to-all-start.2 = ((bf16[4,128,1536]{2,1,0:T(8,128)(2,1)}), bf16[4,128,1536]{2,1,0:T(8,128)(2,1)S(1)}, u32[]{:S(2)}, u32[]{:S(2)}) async-start(bf16[4,128,1536]{2,1,0:T(8,128)(2,1)} %broadcast_in_dim.29), calls=%async_computation.2 | async-start | bytes 3145728 | tf_op jit(solution)/shard_map/all_to_all | solution.py:47
  8.8 9.9 %collective-permute-start = (bf16[192,1536]{1,0:T(8,128)(2,1)S(1)}, bf16[192,1536]{1,0:T(8,128)(2,1)}, u32[]{:S(2)}, u32[]{:S(2)}) collective-permute-start(bf16[192,1536]{1,0:T(8,128)(2,1)S(1)} %copy-done.16), channel_id=1, source_target_pairs={{0,4},{12,8},{1,5},{13,9},{2,6},{14,10},{3,7},{15,11},{16,20},{28,... | collective-permute-start | bytes 1769480 | tf_op jit(solution)/shard_map/ppermute | solution.py:208
  27.1 2.0 %copy-start.1 = (bf16[4,128,1536]{2,1,0:T(8,128)(2,1)}, bf16[4,128,1536]{2,1,0:T(8,128)(2,1)S(1)}, u32[]{:S(2)}) copy-start(bf16[4,128,1536]{2,1,0:T(8,128)(2,1)S(1)} %all-to-all-done.2.og_mine) | copy-start | bytes 4718596
  28.8 5.4 %copy-start.3 = (bf16[1,128,1536]{2,1,0:T(8,128)(2,1)S(1)}, bf16[1,128,1536]{2,1,0:T(8,128)(2,1)}, u32[]{:S(2)}) copy-start(bf16[1,128,1536]{2,1,0:T(8,128)(2,1)} %param.10) | copy-start | bytes 1179652
  28.8 16.1 %copy-start.4 = (bf16[1,128,1536]{2,1,0:T(8,128)(2,1)S(1)}, bf16[1,128,1536]{2,1,0:T(8,128)(2,1)}, u32[]{:S(2)}) copy-start(bf16[1,128,1536]{2,1,0:T(8,128)(2,1)} %param.11) | copy-start | bytes 1179652
  28.8 31.2 %copy-start.17 = (s32[1536]{0:T(1024)S(1)}, s32[1536]{0:T(1024)}, u32[]{:S(2)}) copy-start(s32[1536]{0:T(1024)} %constant.31.clone) | copy-start | bytes 18436
  29.0 31.0 %all-to-all-start = ((bf16[4,192,1536]{2,1,0:T(8,128)(2,1)}), bf16[4,192,1536]{2,1,0:T(8,128)(2,1)S(1)}, u32[]{:S(2)}, u32[]{:S(2)}) async-start(bf16[4,192,1536]{2,1,0:T(8,128)(2,1)} %broadcast_in_dim.24), calls=%async_computation | async-start | bytes 4718592 | tf_op jit(solution)/shard_map/all_to_all | solution.py:47
  34.2 16.1 %collective-permute-start.4 = (bf16[128,1536]{1,0:T(8,128)(2,1)S(1)}, bf16[128,1536]{1,0:T(8,128)(2,1)S(1)}, u32[]{:S(2)}, u32[]{:S(2)}) collective-permute-start(bf16[128,1536]{1,0:T(8,128)(2,1)S(1)} %bitcast.28), channel_id=1, source_target_pairs={{0,8},{8,16},{16,24},{24,32},{32,40},{40,48},{48,56},{56,64},{64,7... | collective-permute-start | bytes 1179656 | tf_op jit(solution)/shard_map/ppermute | solution.py:38
  36.3 10.0 %collective-permute-start.2 = (s32[3]{0:T(128)S(1)}, s32[3]{0:T(128)S(1)}, u32[]{:S(2)}, u32[]{:S(2)}) collective-permute-start(s32[3]{0:T(128)S(1)} %pad_add_fusion.1), channel_id=1, source_target_pairs={{0,8},{8,16},{16,24},{24,32},{32,40},{40,48},{48,56},{56,64},{64,7... | collective-permute-start | bytes 44 | tf_op jit(solution)/shard_map/ppermute | solution.py:38
  39.6 10.8 %collective-permute-start.3 = (s32[3]{0:T(128)S(1)}, s32[3]{0:T(128)S(1)}, u32[]{:S(2)}, u32[]{:S(2)}) collective-permute-start(s32[3]{0:T(128)S(1)} %pad_add_fusion.1), channel_id=1, source_target_pairs={{0,248},{8,0},{16,8},{24,16},{32,24},{40,32},{48,40},{56,48},{64,5... | collective-permute-start | bytes 44 | tf_op jit(solution)/shard_map/ppermute | solution.py:38
  42.8 20.3 %collective-permute-start.5 = (bf16[128,1536]{1,0:T(8,128)(2,1)S(1)}, bf16[128,1536]{1,0:T(8,128)(2,1)}, u32[]{:S(2)}, u32[]{:S(2)}) collective-permute-start(bf16[128,1536]{1,0:T(8,128)(2,1)S(1)} %bitcast.29), channel_id=1, source_target_pairs={{0,248},{8,0},{16,8},{24,16},{32,24},{40,32},{48,40},{56,48},{64,5... | collective-permute-start | bytes 1179656 | tf_op jit(solution)/shard_map/ppermute | solution.py:38
  45.0 18.1 %collective-permute-start.6 = (bf16[128,1536]{1,0:T(8,128)(2,1)S(1)}, bf16[128,1536]{1,0:T(8,128)(2,1)}, u32[]{:S(2)}, u32[]{:S(2)}) collective-permute-start(bf16[128,1536]{1,0:T(8,128)(2,1)S(1)} %bitcast.33), channel_id=1, source_target_pairs={{0,8},{8,16},{16,24},{24,32},{32,40},{40,48},{48,56},{56,64},{64,7... | collective-permute-start | bytes 1179656 | tf_op jit(solution)/shard_map/ppermute | solution.py:38
  46.3 16.8 %collective-permute-start.7 = (bf16[128,1536]{1,0:T(8,128)(2,1)S(1)}, bf16[128,1536]{1,0:T(8,128)(2,1)}, u32[]{:S(2)}, u32[]{:S(2)}) collective-permute-start(bf16[128,1536]{1,0:T(8,128)(2,1)S(1)} %bitcast.34), channel_id=1, source_target_pairs={{0,248},{8,0},{16,8},{24,16},{32,24},{40,32},{48,40},{56,48},{64,5... | collective-permute-start | bytes 1179656 | tf_op jit(solution)/shard_map/ppermute | solution.py:38
  50.3 34.5 %collective-permute-start.14 = (bf16[4,128,1536]{2,1,0:T(8,128)(2,1)}, bf16[4,128,1536]{2,1,0:T(8,128)(2,1)}, u32[]{:S(2)}, u32[]{:S(2)}) collective-permute-start(bf16[4,128,1536]{2,1,0:T(8,128)(2,1)} %copy-done.1), channel_id=1, source_target_pairs={{0,8},{8,0},{1,9},{9,1},{2,10},{10,2},{3,11},{11,3},{4,12},{12,4},... | collective-permute-start | bytes 4718600 | tf_op jit(solution)/shard_map/ppermute | solution.py:42
  50.4 0.7 copy-start.7
  60.0 3.1 %copy-start.6 = (bf16[1,128,1536]{2,1,0:T(8,128)(2,1)S(1)}, bf16[1,128,1536]{2,1,0:T(8,128)(2,1)}, u32[]{:S(2)}) copy-start(bf16[1,128,1536]{2,1,0:T(8,128)(2,1)} %param.9) | copy-start | bytes 1179652
  60.0 73.2 %collective-permute-start.1 = (bf16[768,1536]{1,0:T(8,128)(2,1)S(1)}, bf16[768,1536]{1,0:T(8,128)(2,1)}, u32[]{:S(2)}, u32[]{:S(2)}) collective-permute-start(bf16[768,1536]{1,0:T(8,128)(2,1)S(1)} %bitcast.25), channel_id=1, source_target_pairs={{0,8},{8,0},{1,9},{9,1},{2,10},{10,2},{3,11},{11,3},{4,12},{12,4},... | collective-permute-start | bytes 7077896 | tf_op jit(solution)/shard_map/ppermute | solution.py:42
  63.1 2.3 %copy-start = (bf16[1536,1536]{1,0:T(8,128)(2,1)S(1)}, bf16[1536,1536]{1,0:T(8,128)(2,1)}, u32[]{:S(2)}) copy-start(bf16[1536,1536]{1,0:T(8,128)(2,1)} %fusion.order) | copy-start | bytes 14155780
  65.5 1.0 copy-start.8
  66.5 18.4 %copy-start.2 = (bf16[4,128,1536]{2,1,0:T(8,128)(2,1)S(1)}, bf16[4,128,1536]{2,1,0:T(8,128)(2,1)}, u32[]{:S(2)}) copy-start(bf16[4,128,1536]{2,1,0:T(8,128)(2,1)} %copy-done.1) | copy-start | bytes 4718596
  73.7 14.0 %copy-start.10 = (bf16[128,1536]{1,0:T(8,128)(2,1)}, bf16[128,1536]{1,0:T(8,128)(2,1)S(1)}, u32[]{:S(2)}) copy-start(bf16[128,1536]{1,0:T(8,128)(2,1)S(1)} %get-tuple-element.19.att) | copy-start | bytes 1179652
  73.7 14.0 %copy-start.14 = (f32[128,128]{1,0:T(8,128)}, f32[128,128]{1,0:T(8,128)S(1)}, u32[]{:S(2)}) copy-start(f32[128,128]{1,0:T(8,128)S(1)} %get-tuple-element.21.stats) | copy-start | bytes 196612
  87.6 0.9 copy-start.5
  88.5 28.7 %all-to-all-start.3 = ((bf16[8,24,1536]{2,1,0:T(8,128)(2,1)}), bf16[8,24,1536]{2,1,0:T(8,128)(2,1)}, u32[]{:S(2)}, u32[]{:S(2)}) async-start(bf16[8,24,1536]{2,1,0:T(8,128)(2,1)} %bitcast.38), calls=%async_computation.3 | async-start | bytes 1179648 | tf_op jit(solution)/shard_map/all_to_all | solution.py:240
  98.0 35.3 %collective-permute-start.8 = (bf16[128,1536]{1,0:T(8,128)(2,1)}, bf16[128,1536]{1,0:T(8,128)(2,1)}, u32[]{:S(2)}, u32[]{:S(2)}) collective-permute-start(bf16[128,1536]{1,0:T(8,128)(2,1)} %bitcast.44), channel_id=1, source_target_pairs={{0,8},{8,16},{16,24},{24,32},{32,40},{40,48},{48,56},{56,64},{64,7... | collective-permute-start | bytes 1179656 | tf_op jit(solution)/shard_map/ppermute | solution.py:38
  98.0 35.3 %collective-permute-start.9 = (bf16[128,1536]{1,0:T(8,128)(2,1)}, bf16[128,1536]{1,0:T(8,128)(2,1)}, u32[]{:S(2)}, u32[]{:S(2)}) collective-permute-start(bf16[128,1536]{1,0:T(8,128)(2,1)} %bitcast.45), channel_id=1, source_target_pairs={{0,248},{8,0},{16,8},{24,16},{32,24},{40,32},{48,40},{56,48},{64,5... | collective-permute-start | bytes 1179656 | tf_op jit(solution)/shard_map/ppermute | solution.py:38
  103.3 52.9 %collective-permute-start.10 = (bf16[128,1536]{1,0:T(8,128)(2,1)S(1)}, bf16[128,1536]{1,0:T(8,128)(2,1)}, u32[]{:S(2)}, u32[]{:S(2)}) collective-permute-start(bf16[128,1536]{1,0:T(8,128)(2,1)S(1)} %bitcast.40), channel_id=1, source_target_pairs={{0,8},{8,16},{16,24},{24,32},{32,40},{40,48},{48,56},{56,64},{64,7... | collective-permute-start | bytes 1179656 | tf_op jit(solution)/shard_map/ppermute | solution.py:38
  103.3 52.9 %collective-permute-start.11 = (bf16[128,1536]{1,0:T(8,128)(2,1)S(1)}, bf16[128,1536]{1,0:T(8,128)(2,1)}, u32[]{:S(2)}, u32[]{:S(2)}) collective-permute-start(bf16[128,1536]{1,0:T(8,128)(2,1)S(1)} %bitcast.41), channel_id=1, source_target_pairs={{0,248},{8,0},{16,8},{24,16},{32,24},{40,32},{48,40},{56,48},{64,5... | collective-permute-start | bytes 1179656 | tf_op jit(solution)/shard_map/ppermute | solution.py:38
  133.2 1.0 copy-start.11
  134.2 1.0 copy-start.13
  135.2 0.8 copy-start.15
  136.1 11.2 %copy-start.9 = (bf16[128,1536]{1,0:T(8,128)(2,1)S(1)}, bf16[128,1536]{1,0:T(8,128)(2,1)}, u32[]{:S(2)}) copy-start(bf16[128,1536]{1,0:T(8,128)(2,1)} %copy-done.7) | copy-start | bytes 1179652
  141.9 11.1 %copy-start.12 = (bf16[128,1536]{1,0:T(8,128)(2,1)S(1)}, bf16[128,1536]{1,0:T(8,128)(2,1)}, u32[]{:S(2)}) copy-start(bf16[128,1536]{1,0:T(8,128)(2,1)} %copy-done.10) | copy-start | bytes 1179652
  141.9 14.3 %collective-permute-start.12 = (f32[128,128]{1,0:T(8,128)S(1)}, f32[128,128]{1,0:T(8,128)S(1)}, u32[]{:S(2)}, u32[]{:S(2)}) collective-permute-start(f32[128,128]{1,0:T(8,128)S(1)} %get-tuple-element.23.stats), channel_id=1, source_target_pairs={{0,8},{8,16},{16,24},{24,32},{32,40},{40,48},{48,56},{56,64},{64,7... | collective-permute-start | bytes 196616 | tf_op jit(solution)/shard_map/ppermute | solution.py:38
  142.0 14.2 %collective-permute-start.13 = (f32[128,128]{1,0:T(8,128)S(1)}, f32[128,128]{1,0:T(8,128)S(1)}, u32[]{:S(2)}, u32[]{:S(2)}) collective-permute-start(f32[128,128]{1,0:T(8,128)S(1)} %get-tuple-element.23.stats), channel_id=1, source_target_pairs={{0,248},{8,0},{16,8},{24,16},{32,24},{40,32},{48,40},{56,48},{64,5... | collective-permute-start | bytes 196616 | tf_op jit(solution)/shard_map/ppermute | solution.py:38

commit v2 on v1

v2 whole, which is shorter than its diff:
```python
import jax
import jax.numpy as jnp
import numpy as np
from jax import lax
from jax.experimental import pallas as pl
from jax.experimental.pallas import tpu as pltpu
from jax.sharding import PartitionSpec as P

HEADS = 12
HEAD_DIM = 128
TILE = 128
HD = HEADS * HEAD_DIM
SCALE = HEAD_DIM**-0.5
MASKED = -1e30

SIZES = (8, 2, 2, 2, 4)
NAMES = ("z", "yhi", "core", "ylo", "x")
FRAME = ("z", "yhi", "core")
FSDP = ("ylo", "x")
TILES = 32
ROWS_OUT = 6
GROUP = 8
GROUP_ROWS = HD // GROUP
EXTRA = 16

F32 = jnp.float32
BF16 = jnp.bfloat16
VMEM = pltpu.VMEM
NT = (((1,), (1,)), ((), ()))
NN = (((1,), (0,)), ((), ()))
TN = (((0,), (0,)), ((), ()))


def dot(a, b, dims=NN):
    return lax.dot_general(a, b, dims, preferred_element_type=F32)


def next_tile(value, step):
    return lax.ppermute(value, FRAME, [(i, (i + step) % TILES) for i in range(TILES)])


def core_swap(value):
    return lax.ppermute(value, "core", [(0, 1), (1, 0)])


def along_x(value, step):
    return lax.ppermute(value, "x", [((i + step) % 4, i) for i in range(4)])


def gather_x(value):
    spread = jnp.broadcast_to(value[None], (4,) + value.shape)
    return lax.all_to_all(spread, "x", 0, 0, tiled=True)


def after(value, *others):
    return lax.optimization_barrier((value, *others))[0]


def head(h):
    return slice(h * HEAD_DIM, (h + 1) * HEAD_DIM)


def visible(frame, low, high, there):
    seen = (frame >= low) & (frame <= high)
    return jnp.minimum(jnp.where(seen, 0.0, MASKED), jnp.where(there, 0.0, MASKED))


def told(tile):
    row = tile[2 * TILE : 2 * TILE + EXTRA, :HEAD_DIM].astype(F32)[:1]
    return row[:, 0:1], row[:, 1:2], row[:, 2:3]


def row_bias(info, left, right):
    frame, back, ahead = (info[n].astype(F32) for n in range(3))
    low, high, position = frame - back, frame + ahead, info[3]
    place = lax.broadcasted_iota(jnp.int32, (1, 3 * TILE), 1)
    on_left = visible(told(left)[0], low, high, position > 0)
    on_right = visible(told(right)[0], low, high, position < TILES - 1)
    return jnp.where(place < TILE, on_left, jnp.where(place < 2 * TILE, 0.0, on_right))


def column_bias(info, left, right):
    frame, position = info[0].astype(F32), info[3]
    place = lax.broadcasted_iota(jnp.int32, (1, 2 * TILE), 1)
    sides = []
    for tile, there in ((left, position > 0), (right, position < TILES - 1)):
        center, back, ahead = told(tile)
        sides.append(visible(frame, center - back, center + ahead, there))
    return jnp.where(place < TILE, sides[0], sides[1])


KEYS = slice(0, TILE)
VALUES = slice(TILE, 2 * TILE)


def forward_kernel(scalars, near, far, copies, outs, scratch):
    (info,) = scalars
    q, k, v, left, right = near
    (order,) = far
    att, att_t, stats = outs
    lane = lax.broadcasted_iota(jnp.int32, (TILE, 128), 1)
    total = jnp.zeros((TILE, 128), F32)
    for h in range(HEADS):
        if h == 0:
            bias = row_bias(info, left, right)
        c = head(h)
        keys = jnp.concatenate([left[KEYS, c], k[:, c], right[KEYS, c]], axis=0)
        values = jnp.concatenate([left[VALUES, c], v[:, c], right[VALUES, c]], axis=0)
        s = dot(q[:, c], keys, NT) * SCALE + bias
        top = jnp.max(s, axis=1, keepdims=True)
        e = jnp.exp(s - top)
        mass = jnp.sum(e, axis=1, keepdims=True)
        p = (e * (1.0 / mass)).astype(BF16)
        att[:, c] = dot(p, values).astype(BF16)
        total = jnp.where(lane == h, top + jnp.log(mass), total)
    stats[...] = total
    copies[0].wait()
    for g in range(GROUP):
        cols = slice(g * GROUP_ROWS, (g + 1) * GROUP_ROWS)
        att_t[g] = dot(order[cols, :], att[...], NT).astype(BF16)


def place(info, n):
    side, step = divmod(n, 4)
    core = info[4] if side == 0 else 1 - info[4]
    return core * 4 + lax.rem(info[5] + step, 4)


def spread_kernel(scalars, near, far, copies, outs, scratch):
    (info,), (out, w) = scalars, outs
    att_t, held, passed, *grads = near
    out[:, :GROUP_ROWS, :] = att_t[...]
    w[...] = jnp.where(info[4] == info[7], held[...], passed[...])
    for side in range(2):
        core = info[4] if side == 0 else 1 - info[4]
        for n in range(0, 4, 2):
            pair = grads[side][n : n + 2].reshape(2 * TILE, HD)
            got = dot(w[...], pair, NT).astype(BF16)
            out[core * 4 + n, GROUP_ROWS:, :] = got[:, :TILE]
            out[core * 4 + n + 1, GROUP_ROWS:, :] = got[:, TILE:]


def weight_kernel(scalars, near, far, copies, outs, scratch):
    (info,), (mixed, *grads), (out,) = scalars, near, outs
    acc = None
    for side in range(2):
        core = info[4] if side == 0 else 1 - info[4]
        left = jnp.concatenate([mixed[core * 4 + n, :GROUP_ROWS, :] for n in range(4)], axis=1)
        term = dot(left, grads[side][...].reshape(4 * TILE, HD))
        acc = term if acc is None else acc + term
    out[...] = (acc * float(GROUP * TILES * TILE) ** -0.5).astype(BF16)


def delta_kernel(scalars, near, far, copies, outs, scratch):
    mixed, att, stats = near
    ga, out = outs
    lane = lax.broadcasted_iota(jnp.int32, (TILE, 128), 1)
    total = stats[...]
    rows = mixed[:, GROUP_ROWS:, :].reshape(HD, TILE)
    for h in range(HEADS):
        c = head(h)
        own = rows[c, :].T
        ga[:TILE, c] = own
        terms = own.astype(F32) * att[:, c].astype(F32)
        total = jnp.where(lane == HEADS + h, jnp.sum(terms, axis=1, keepdims=True), total)
    out[...] = total
    turned = total.T
    rest = [
        jnp.concatenate([turned[k * HEADS + h : k * HEADS + h + 1, :] for h in range(HEADS)], axis=1)
        for k in range(2)
    ]
    terms = []
    for _ in range(3):
        for k in range(2):
            part = rest[k].astype(BF16).astype(F32)
            rest[k] = rest[k] - part
            terms.append(part)
    terms.append(jnp.zeros((EXTRA - len(terms), HD), F32))
    ga[TILE:, :] = jnp.concatenate(terms, axis=0).astype(BF16)


def sum_kernel(scalars, near, far, copies, outs, scratch):
    (info,), (parts,) = scalars, near
    total = parts[0].astype(F32)
    for n in range(1, 8):
        total += parts[n].astype(F32)
    pieces = [total[n * ROWS_OUT : (n + 1) * ROWS_OUT, :] for n in range(4)]
    for step, ref in enumerate(outs):
        want = jnp.bitwise_xor(info[6], step)
        low = jnp.where(want == 0, pieces[0], pieces[1])
        high = jnp.where(want == 2, pieces[2], pieces[3])
        ref[...] = jnp.where(want < 2, low, high)


def project_kernel(scalars, near, far, copies, outs, scratch):
    (info,), (att,), (out,), (turned,) = scalars, near, outs, scratch
    for h in range(HEADS):
        turned[head(h), :] = att[:, head(h)].T
    acc = jnp.zeros((TILE, HD), F32)
    for n in range(GROUP):
        copies[n].wait()
        first = pl.multiple_of(place(info, n) * GROUP_ROWS, GROUP_ROWS)
        acc += dot(turned[pl.ds(first, GROUP_ROWS), :], far[n][...], TN)
    out[...] = acc.astype(BF16)


def backward_kernel(scalars, near, far, copies, outs, scratch):
    (info,), (dq, dk, dv) = scalars, outs
    stats, q, k, v, left, right, ga, ql, qr, gal, gar = near
    st = stats[...]
    for h in range(HEADS):
        if h == 0:
            on_row, on_column = row_bias(info, left, right), column_bias(info, left, right)
        c = head(h)
        keys = jnp.concatenate([left[KEYS, c], k[:, c], right[KEYS, c]], axis=0)
        values = jnp.concatenate([left[VALUES, c], v[:, c], right[VALUES, c]], axis=0)
        qh, gh = q[:, c], ga[:TILE, c]
        s = dot(qh, keys, NT) * SCALE + on_row
        p = jnp.exp(s - st[:, h : h + 1])
        dp = dot(gh, values, NT)
        ds = (p * (dp - st[:, HEADS + h : HEADS + h + 1]) * SCALE).astype(BF16)
        dq[:, c] = dot(ds, keys).astype(BF16)
        dkh = dot(ds[:, TILE : 2 * TILE], qh, TN)
        dvh = dot(p[:, TILE : 2 * TILE].astype(BF16), gh, TN)

        queries = jnp.concatenate([ql[:, c], qr[:, c]], axis=0)
        grads = jnp.concatenate([gal[:TILE, c], gar[:TILE, c]], axis=0)
        sent = [g[TILE:, c].astype(F32) for g in (gal, gar)]
        lse, delta = (
            jnp.concatenate([t[n : n + 1] + t[n + 2 : n + 3] + t[n + 4 : n + 5] for t in sent], axis=1)
            for n in range(2)
        )
        s = dot(k[:, c], queries, NT) * SCALE + on_column
        p = jnp.exp(s - lse)
        dp = dot(v[:, c], grads, NT)
        ds = (p * (dp - delta) * SCALE).astype(BF16)
        dk[:, c] = (dkh + dot(ds, queries)).astype(BF16)
        dv[:, c] = (dvh + dot(p.astype(BF16), grads)).astype(BF16)


def call(kernel, micros, scalars, near, far, outs, scratch=(), mib=4):
    counts = [len(scalars), len(near), len(far), len(outs), len(far), len(scratch)]
    ends = np.cumsum(counts)

    def body(*refs):
        parts = [refs[end - count : end] for end, count in zip(ends, counts)]
        sems = refs[ends[-1]]
        copies = [
            pltpu.make_async_copy(ref, buffer, sems.at[n])
            for n, (ref, buffer) in enumerate(zip(parts[2], parts[4]))
        ]
        for copy in copies:
            copy.start()
        kernel(parts[0], parts[1], parts[4], copies, parts[3], parts[5])

    return pl.pallas_call(
        body,
        in_specs=[pl.BlockSpec(memory_space=pltpu.SMEM)] * len(scalars)
        + [pl.BlockSpec(memory_space=VMEM)] * len(near)
        + [pl.BlockSpec(memory_space=pl.ANY)] * len(far),
        out_specs=[pl.BlockSpec(memory_space=VMEM)] * len(outs),
        out_shape=[jax.ShapeDtypeStruct(s, d) for s, d in outs],
        scratch_shapes=[VMEM(f.shape, f.dtype) for f in far]
        + [VMEM(s, d) for s, d in scratch]
        + [pltpu.SemaphoreType.DMA((max(1, len(far)),))],
        cost_estimate=pl.CostEstimate(flops=int(micros * 1e9), bytes_accessed=1024, transcendentals=0),
        compiler_params=pltpu.CompilerParams(vmem_limit_bytes=mib * 1024 * 1024),
    )(*scalars, *near, *far)


def column_order():
    features = np.arange(HD).reshape(SIZES + (ROWS_OUT,))
    return features.transpose(2, 4, 0, 1, 3, 5).reshape(-1)


def shards(query_rows, key_rows, value_rows, frame_of, reach_back, reach_ahead, out_weight, out_grad):
    core = lax.axis_index("core")
    q, k, v, og = query_rows[0], key_rows[0], value_rows[0], out_grad[0]
    tile = (TILE, HD)
    where = (lax.axis_index(FRAME), core, lax.axis_index("x"), lax.axis_index(("yhi", "ylo")))
    where = where + (lax.axis_index("ylo"),)
    info = jnp.stack([frame_of[0, 0], reach_back[0, 0], reach_ahead[0, 0], *where]).astype(jnp.int32)

    note = jnp.pad(info[None, :3].astype(BF16), ((0, EXTRA - 1), (0, HD - 3)))
    to_send = jnp.concatenate([k, v, note], axis=0)
    left, right = next_tile(to_send, 1), next_tile(to_send, -1)

    og_mine = gather_x(after(og, to_send))
    og_other = core_swap(og_mine)

    w_passed = lax.ppermute(after(out_weight, left, right), ("core", "ylo"), [(0, 1), (3, 2)])

    q2 = after(q, left, right)
    ql, qr = next_tile(q2, 1), next_tile(q2, -1)

    order = jnp.asarray(np.eye(HD, dtype=np.float32)[column_order()], BF16)
    att, att_t, stats = call(
        forward_kernel,
        8,
        (info,),
        (q, k, v, left, right),
        (order,),
        [(tile, BF16), ((GROUP, GROUP_ROWS, TILE), BF16), ((TILE, 128), F32)],
        mib=16,
    )

    mixed, w_block = call(
        spread_kernel,
        2,
        (info,),
        (after(att_t, ql, qr), out_weight, w_passed, og_mine, og_other),
        (),
        [((GROUP, 2 * GROUP_ROWS, TILE), BF16), ((GROUP_ROWS, HD), BF16)],
    )
    mixed = lax.all_to_all(mixed, ("core", "x"), 0, 0, tiled=True)

    ga, stats = call(
        delta_kernel,
        1,
        (),
        (mixed, att, stats),
        (),
        [((TILE + EXTRA, HD), BF16), ((TILE, 128), F32)],
    )
    gal, gar = next_tile(ga, 1), next_tile(ga, -1)

    w_late = after(w_block, ga)
    blocks = [w_block] + [along_x(w_late, step) for step in (1, 2, 3)]

    (partial,) = call(
        weight_kernel,
        2,
        (info,),
        (after(mixed, ga), og_mine, og_other),
        (),
        [((GROUP_ROWS, HD), BF16)],
    )
    along_z = lax.all_to_all(partial.reshape(8, GROUP_ROWS // 8, HD), "z", 0, 0, tiled=True)

    dq, dk, dv = call(
        backward_kernel,
        9,
        (info,),
        (after(stats, partial), q, k, v, left, right, ga, ql, qr, gal, gar),
        (),
        [(tile, BF16)] * 3,
        mib=8,
    )

    pieces = call(
        sum_kernel,
        1,
        (info,),
        (after(along_z, dq),),
        (),
        [((ROWS_OUT, HD), F32)] * 4,
    )
    arrived = []
    for step in (1, 2, 3):
        pairs = [(i, i ^ step) for i in range(4)]
        arrived.append(lax.ppermute(pieces[step], ("yhi", "ylo"), pairs))

    blocks = blocks + [core_swap(after(w, dq)) for w in blocks]
    (layer_out,) = call(
        project_kernel,
        4,
        (info,),
        (after(att, pieces[0]),),
        tuple(blocks),
        [(tile, BF16)],
        scratch=[((HD, TILE), BF16)],
        mib=16,
    )
    grad_weight = after(pieces[0], layer_out) + arrived[0] + arrived[1] + arrived[2]
    return layer_out[None], dq[None], dk[None], dv[None], grad_weight


def solution(mesh):
    fine = jax.sharding.Mesh(np.asarray(mesh.devices).reshape(SIZES), NAMES)
    tokens = P(FSDP, FRAME, None)
    tiles = P(FSDP, FRAME)
    in_specs = (tokens, tokens, tokens, tiles, tiles, tiles, P(FSDP, None), tokens)
    out_specs = (tokens, tokens, tokens, tokens, P(FRAME + FSDP, None))
    return jax.shard_map(shards, mesh=fine, in_specs=in_specs, out_specs=out_specs, check_vma=False)
```

time: 165 us -> 127 us (0.77)
  starting transfers between devices: 52.6 us -> 40.1 us
  waiting for transfers between devices: 33.7 us -> 23.6 us
  blocking collectives: 22.1 us -> 15.2 us
  Pallas kernels: 32.3 us -> 26.5 us
  other arithmetic: 6.58 us -> 2.77 us
    ppermute x12 -> x6, starting transfers between devices: 28.9 us -> 18.8 us  [next_tile(): lax.ppermute(value, FRAME, [(i, (i + step) % TILES) for i in range(TILES)])]
    ppermute x1 -> x7, starting transfers between devices: 3.33 us -> 11.1 us  [the longest x3 4.79 us: shards(): arrived.append(lax.ppermute(pieces[step], ('yhi', 'ylo'), pairs))]
    all_to_all x2 -> x1, blocking collectives: 22.1 us -> 15.2 us  [shards(): mixed = lax.all_to_all(mixed, ('core', 'x'), 0, 0, tiled=True)]
    all_to_all x1, starting transfers between devices: 9.44 us -> 3.55 us  [shards(): lax.all_to_all(partial.reshape(8, GROUP_ROWS // 8, HD), 'z', 0, 0, tiled=...]
    pallas_call x6 -> x7, Pallas kernels: 32.3 us -> 26.5 us  [call(): pl.pallas_call(body, in_specs=[pl.BlockSpec(memory_space=pltpu.SMEM)] * l...]
    all_to_all x2 -> x1, waiting for transfers between devices: 17.2 us -> 11.9 us  [gather_x(): return lax.all_to_all(spread, 'x', 0, 0, tiled=True)]
    all_to_all x2 -> x1, starting transfers between devices: 11 us -> 5.93 us  [gather_x(): return lax.all_to_all(spread, 'x', 0, 0, tiled=True)]
    unnamed x36 -> x38, local copies, waits for them, and re-layouts: 8 us -> 13 us
  transfers between devices with their start and end apart: 18 -> 20, of which waited for: 5 -> 5; matrix products, arithmetic and copies ran while one was open for 5% -> 0% of each run, Pallas kernels for 15% -> 18%
where the time goes in v2:
time: 127 us; the launch traced here: 126 us
  starting transfers between devices  40.1 us (32%)
  Pallas kernels  26.5 us (21%)
  waiting for transfers between devices  23.6 us (19%)
  blocking collectives  15.2 us (12%)
  local copies, waits for them, and re-layouts  14.4 us (11%)
  between operations  2.9 us (2%)
  other arithmetic  2.77 us (2%)
    pallas_call x7, Pallas kernels, call(): pl.pallas_call(body, in_specs=[pl.BlockSpec(memory_space=pltpu.SMEM)] * l...  26.5 us
    ppermute x6, starting transfers between devices, next_tile(): lax.ppermute(value, FRAME, [(i, (i + step) % TILES) for i in range(TILES)])  18.8 us
    all_to_all x1, blocking collectives, shards(): mixed = lax.all_to_all(mixed, ('core', 'x'), 0, 0, tiled=True)  15.2 us
    unnamed x38, local copies, waits for them, and re-layouts  13 us
    all_to_all x1, waiting for transfers between devices, gather_x(): return lax.all_to_all(spread, 'x', 0, 0, tiled=True)  11.9 us
    all_to_all x1, starting transfers between devices, gather_x(): return lax.all_to_all(spread, 'x', 0, 0, tiled=True)  5.93 us
    ppermute x6, waiting for transfers between devices, next_tile(): lax.ppermute(value, FRAME, [(i, (i + step) % TILES) for i in range(TILES)])  5.17 us
    ppermute x3, starting transfers between devices, shards(): arrived.append(lax.ppermute(pieces[step], ('yhi', 'ylo'), pairs))  4.79 us
  transfers between devices with their start and end apart: 20, of which 5 were waited for; matrix products, arithmetic and copies ran while one was open for 0% of the time, Pallas kernels for 18%

profile of v2, /device:TPU:2, one launch (start us, length us, event | category | flops | bytes accessed | tf_op | source)
XLA Modules:
  0.0 125.5 jit_solution(8680396305394541875)
XLA Ops:
  2.6 0.1 fusion.8
  2.7 2.1 %pad_maximum_fusion = bf16[272,1536]{1,0:T(8,128)(2,1)} fusion(bf16[16,1536]{1,0:T(8,128)(2,1)S(1)} %fusion.8, bf16[128,1536]{1,0:T(8,128)(2,1)} %bitcast.23, bf16[128,1536]{1,0:T(8,128)(2,1)} %bitcast.20), kind=kLoop, calls=%fused_computation | loop fusion | flops 2506752 | bytes 1671168 | tf_op jit(solution)/shard_map/concatenate | solution.py:285
  4.8 1.3 %broadcast_in_dim.19 = bf16[4,128,1536]{2,1,0:T(8,128)(2,1)} broadcast(bf16[128,1536]{1,0:T(8,128)(2,1)S(1)} %bitcast.30), dimensions={1,2} | broadcast | bytes 1966080 | tf_op jit(solution)/shard_map/broadcast_in_dim | solution.py:51
  6.1 5.9 %all-to-all-start = ((bf16[4,128,1536]{2,1,0:T(8,128)(2,1)}), bf16[4,128,1536]{2,1,0:T(8,128)(2,1)S(1)}, u32[]{:S(2)}, u32[]{:S(2)}) async-start(bf16[4,128,1536]{2,1,0:T(8,128)(2,1)} %broadcast_in_dim.19), calls=%async_computation | async-start | bytes 3145728 | tf_op jit(solution)/shard_map/all_to_all | solution.py:52
  12.0 6.4 %collective-permute-start.1 = (bf16[272,1536]{1,0:T(8,128)(2,1)}, bf16[272,1536]{1,0:T(8,128)(2,1)S(1)}, u32[]{:S(2)}, u32[]{:S(2)}) collective-permute-start(bf16[272,1536]{1,0:T(8,128)(2,1)} %pad_maximum_fusion), channel_id=1, source_target_pairs={{0,248},{8,0},{16,8},{24,16},{32,24},{40,32},{48,40},{56,48},{64,5... | collective-permute-start | bytes 2506760 | tf_op jit(solution)/shard_map/ppermute | solution.py:39
  18.4 11.9 %all-to-all-done.refs_4_.refs_2_ = bf16[4,128,1536]{2,1,0:T(8,128)(2,1)S(1)} async-done(((bf16[4,128,1536]{2,1,0:T(8,128)(2,1)}), bf16[4,128,1536]{2,1,0:T(8,128)(2,1)S(1)}, u32[]{:S(2)}, u32[]{:S(2)}) %all-to-all-start) | async-done | bytes 1572896 | tf_op jit(solution)/shard_map/all_to_all | solution.py:52
  30.3 0.1 stack.25.refs_0_
  30.4 3.9 %collective-permute-done.refs_4_.refs_5_ = bf16[272,1536]{1,0:T(8,128)(2,1)} collective-permute-done((bf16[272,1536]{1,0:T(8,128)(2,1)}, bf16[272,1536]{1,0:T(8,128)(2,1)}, u32[]{:S(2)}, u32[]{:S(2)}) %collective-permute-start) | collective-permute-done | bytes 835616 | tf_op jit(solution)/shard_map/ppermute | solution.py:39
  34.3 4.8 %collective-permute-start.3 = (bf16[128,1536]{1,0:T(8,128)(2,1)}, bf16[128,1536]{1,0:T(8,128)(2,1)S(1)}, u32[]{:S(2)}, u32[]{:S(2)}) collective-permute-start(bf16[128,1536]{1,0:T(8,128)(2,1)} %bitcast.26), channel_id=1, source_target_pairs={{0,248},{8,0},{16,8},{24,16},{32,24},{40,32},{48,40},{56,48},{64,5... | collective-permute-start | bytes 1179656 | tf_op jit(solution)/shard_map/ppermute | solution.py:39
  39.1 2.6 %collective-permute-start.4 = (bf16[192,1536]{1,0:T(8,128)(2,1)}, bf16[192,1536]{1,0:T(8,128)(2,1)S(1)}, u32[]{:S(2)}, u32[]{:S(2)}) collective-permute-start(bf16[192,1536]{1,0:T(8,128)(2,1)} %refs_2_.1), channel_id=1, source_target_pairs={{0,4},{12,8},{1,5},{13,9},{2,6},{14,10},{3,7},{15,11},{16,20},{28,... | collective-permute-start | bytes 1769480 | tf_op jit(solution)/shard_map/ppermute | solution.py:291
  41.7 0.0 copy-start.9
  41.7 1.0 copy-done.9
  42.7 2.3 %copy-done.15 = bf16[1536,1536]{1,0:T(8,128)(2,1)S(1)} copy-done((bf16[1536,1536]{1,0:T(8,128)(2,1)S(1)}, bf16[1536,1536]{1,0:T(8,128)(2,1)}, u32[]{:S(2)}) %copy-start.15) | copy-done | bytes 4718616
  45.1 7.1 %shard_map.128 = (bf16[128,1536]{1,0:T(8,128)(2,1)S(1)}, bf16[8,192,128]{2,1,0:T(8,128)(2,1)S(1)}, f32[128,128]{1,0:T(8,128)S(1)}) custom-call(s32[8]{0:T(128)S(1)} %stack.25.refs_0_, bf16[128,1536]{1,0:T(8,128)(2,1)S(1)} %bitcast.28, bf16[128,1536]{1,0:T(8,128)(2,1)S(1)} %bitcast.21, bf16[128,1536]{1,0:T(8,128)(2,1)S(1)} %bitcast.24, ...), custom_call_target="tpu_custom_call" | custom-call | flops 8000000000 | bytes 1024 | tf_op jit(solution)/shard_map/pallas_call | solution.py:256
  52.1 0.0 copy-start.11
  52.2 0.0 copy-start.13
  52.2 3.1 %shard_map.129 = (bf16[8,384,128]{2,1,0:T(8,128)(2,1)S(1)}, bf16[192,1536]{1,0:T(8,128)(2,1)}) custom-call(s32[8]{0:T(128)S(1)} %stack.25.refs_0_, bf16[8,192,128]{2,1,0:T(8,128)(2,1)S(1)} %get-tuple-element.36.refs_1_, bf16[192,1536]{1,0:T(8,128)(2,1)S(1)} %copy-done.2, bf16[192,1536]{1,0:T(8,128)(2,1)S(1)} %collective-permute-done.4.refs_3_, ...), custom_call_target="tpu_custom_call" | custom-call | flops 2000000000 | bytes 1024 | tf_op jit(solution)/shard_map/pallas_call | solution.py:256
  55.3 15.2 %all_to_all.15.refs_0_.refs_1_ = bf16[8,384,128]{2,1,0:T(8,128)(2,1)S(1)} all-to-all(bf16[8,384,128]{2,1,0:T(8,128)(2,1)S(1)} %get-tuple-element.39), channel_id=1, replica_groups=mesh['z'=8,'yhi'=2,'core'=2,'ylo'=2,'x'=4] {'core','x'}, dimensions={0} | all-to-all | bytes 1572864 | tf_op jit(solution)/shard_map/all_to_all | solution.py:315
  70.5 1.3 %shard_map.130 = (bf16[144,1536]{1,0:T(8,128)(2,1)}, f32[128,128]{1,0:T(8,128)S(1)}) custom-call(bf16[8,384,128]{2,1,0:T(8,128)(2,1)S(1)} %all_to_all.15.refs_0_.refs_1_, bf16[128,1536]{1,0:T(8,128)(2,1)S(1)} %get-tuple-element.48.refs_1_, f32[128,128]{1,0:T(8,128)S(1)} %get-tuple-element.40.refs_2_), custom_call_target="tpu_custom_call" | custom-call | flops 1000000000 | bytes 1024 | tf_op jit(solution)/shard_map/pallas_call | solution.py:256
  71.8 7.6 %collective-permute-start.7 = (bf16[144,1536]{1,0:T(8,128)(2,1)}, bf16[144,1536]{1,0:T(8,128)(2,1)}, u32[]{:S(2)}, u32[]{:S(2)}) collective-permute-start(bf16[144,1536]{1,0:T(8,128)(2,1)} %get-tuple-element.41.refs_7_), channel_id=1, source_target_pairs={{0,248},{8,0},{16,8},{24,16},{32,24},{40,32},{48,40},{56,48},{64,5... | collective-permute-start | bytes 1327112 | tf_op jit(solution)/shard_map/ppermute | solution.py:39
  79.4 3.2 %collective-permute-start.9 = (bf16[192,1536]{1,0:T(8,128)(2,1)}, bf16[192,1536]{1,0:T(8,128)(2,1)}, u32[]{:S(2)}, u32[]{:S(2)}) collective-permute-start(bf16[192,1536]{1,0:T(8,128)(2,1)} %get-tuple-element.51.refs_2_), channel_id=1, source_target_pairs={{2,0},{3,1},{0,2},{1,3},{6,4},{7,5},{4,6},{5,7},{10,8},{11,9},{8,1... | collective-permute-start | bytes 1769480 | tf_op jit(solution)/shard_map/ppermute | solution.py:47
  82.6 0.5 collective-permute-start.8
  83.1 3.1 %shard_map.131 = bf16[192,1536]{1,0:T(8,128)(2,1)} custom-call(s32[8]{0:T(128)S(1)} %stack.25.refs_0_, bf16[8,384,128]{2,1,0:T(8,128)(2,1)S(1)} %all_to_all.15.refs_0_.refs_1_, bf16[4,128,1536]{2,1,0:T(8,128)(2,1)S(1)} %all-to-all-done.refs_4_.refs_2_, bf16[4,128,1536]{2,1,0:T(8,128)(2,1)} %collective-permute-done.5.refs_5_.refs_3_), custom_call_target="tpu_custom_call" | custom-call | flops 2000000000 | bytes 1024 | tf_op jit(solution)/shard_map/pallas_call | solution.py:256
  86.2 3.5 %all-to-all-start.2 = ((bf16[8,24,1536]{2,1,0:T(8,128)(2,1)}), bf16[8,24,1536]{2,1,0:T(8,128)(2,1)S(1)}, u32[]{:S(2)}, u32[]{:S(2)}) async-start(bf16[8,24,1536]{2,1,0:T(8,128)(2,1)} %bitcast.12), calls=%async_computation.2 | async-start | bytes 1179648 | tf_op jit(solution)/shard_map/all_to_all | solution.py:338
  89.8 1.3 %collective-permute-done.6.refs_10_ = bf16[144,1536]{1,0:T(8,128)(2,1)} collective-permute-done((bf16[144,1536]{1,0:T(8,128)(2,1)}, bf16[144,1536]{1,0:T(8,128)(2,1)}, u32[]{:S(2)}, u32[]{:S(2)}) %collective-permute-start.6) | collective-permute-done | bytes 442400 | tf_op jit(solution)/shard_map/ppermute | solution.py:39
  91.0 1.0 copy-done.10
  92.0 1.0 copy-done.12
  93.0 1.0 copy-done.14
  94.0 7.3 %shard_map.132 = (bf16[128,1536]{1,0:T(8,128)(2,1)}, bf16[128,1536]{1,0:T(8,128)(2,1)}, bf16[128,1536]{1,0:T(8,128)(2,1)}) custom-call(s32[8]{0:T(128)S(1)} %stack.25.refs_0_, f32[128,128]{1,0:T(8,128)S(1)} %get-tuple-element.44.refs_1_, bf16[128,1536]{1,0:T(8,128)(2,1)S(1)} %bitcast.29, bf16[128,1536]{1,0:T(8,128)(2,1)S(1)} %bitcast.22, ...), custom_call_target="tpu_custom_call" | custom-call | flops 8999999488 | bytes 1024 | tf_op jit(solution)/shard_map/pallas_call | solution.py:256
  101.3 0.1 collective-permute-start.11
  101.4 0.5 collective-permute-start.14
  101.9 0.1 collective-permute-start.13
  102.0 3.0 %collective-permute-done.8.refs_3_ = bf16[192,1536]{1,0:T(8,128)(2,1)} collective-permute-done((bf16[192,1536]{1,0:T(8,128)(2,1)}, bf16[192,1536]{1,0:T(8,128)(2,1)}, u32[]{:S(2)}, u32[]{:S(2)}) %collective-permute-start.8) | collective-permute-done | bytes 589856 | tf_op jit(solution)/shard_map/ppermute | solution.py:47
  105.0 0.0 collective-permute-start.12
  105.0 3.6 %all-to-all-done.2.refs_1_ = bf16[8,24,1536]{2,1,0:T(8,128)(2,1)S(1)} async-done(((bf16[8,24,1536]{2,1,0:T(8,128)(2,1)}), bf16[8,24,1536]{2,1,0:T(8,128)(2,1)S(1)}, u32[]{:S(2)}, u32[]{:S(2)}) %all-to-all-start.2) | async-done | bytes 589856 | tf_op jit(solution)/shard_map/all_to_all | solution.py:338
  108.6 0.7 shard_map.133
  109.3 1.0 collective-permute-start.15
  110.2 0.8 copy-done.3
  111.1 2.7 %collective-permute-start.16 = (f32[6,1536]{1,0:T(8,128)S(1)}, f32[6,1536]{1,0:T(8,128)S(1)}, u32[]{:S(2)}, u32[]{:S(2)}) collective-permute-start(f32[6,1536]{1,0:T(8,128)S(1)} %get-tuple-element.59), channel_id=1, source_target_pairs={{0,16},{4,20},{16,0},{20,4},{1,17},{5,21},{17,1},{21,5},{2,18},{6,... | collective-permute-start | bytes 110600 | tf_op jit(solution)/shard_map/ppermute | solution.py:361
  113.8 0.8 copy-done.5
  114.6 1.1 collective-permute-start.17
  115.7 0.8 copy-done.7
  116.5 1.1 copy-done.4
  117.6 1.1 copy-done.6
  118.7 1.1 copy-done.8
  119.7 1.0 copy-done.17
  120.7 4.1 %shard_map.134 = bf16[128,1536]{1,0:T(8,128)(2,1)} custom-call(s32[8]{0:T(128)S(1)} %stack.25.refs_0_, bf16[128,1536]{1,0:T(8,128)(2,1)S(1)} %copy-done.17, bf16[192,1536]{1,0:T(8,128)(2,1)} %get-tuple-element.51.refs_2_, bf16[192,1536]{1,0:T(8,128)(2,1)} %collective-permute-done.8.refs_3_, bf16[192,1536]{1,0:T(8,128)(2,1)} %collective-permute-done.9.refs_4_, ...), custom_call_target="tpu_custom_call" | custom-call | flops 4000000000 | bytes 1024 | tf_op jit(solution)/shard_map/pallas_call | solution.py:256
  124.9 0.6 add_add_fusion
  (43 shorter events, 0.1 us)
Async XLA Ops:
  0.6 4.2 %copy-start.18 = (bf16[1,128,1536]{2,1,0:T(8,128)(2,1)S(1)}, bf16[1,128,1536]{2,1,0:T(8,128)(2,1)}, u32[]{:S(2)}) copy-start(bf16[1,128,1536]{2,1,0:T(8,128)(2,1)} %param.16) | copy-start | bytes 1179652
  6.1 35.6 %copy-start = (bf16[1,128,1536]{2,1,0:T(8,128)(2,1)S(1)}, bf16[1,128,1536]{2,1,0:T(8,128)(2,1)}, u32[]{:S(2)}) copy-start(bf16[1,128,1536]{2,1,0:T(8,128)(2,1)} %param.10) | copy-start | bytes 1179652
  6.1 35.6 %copy-start.1 = (bf16[1,128,1536]{2,1,0:T(8,128)(2,1)S(1)}, bf16[1,128,1536]{2,1,0:T(8,128)(2,1)}, u32[]{:S(2)}) copy-start(bf16[1,128,1536]{2,1,0:T(8,128)(2,1)} %param.11) | copy-start | bytes 1179652
  6.1 24.2 %all-to-all-start = ((bf16[4,128,1536]{2,1,0:T(8,128)(2,1)}), bf16[4,128,1536]{2,1,0:T(8,128)(2,1)S(1)}, u32[]{:S(2)}, u32[]{:S(2)}) async-start(bf16[4,128,1536]{2,1,0:T(8,128)(2,1)} %broadcast_in_dim.19), calls=%async_computation | async-start | bytes 3145728 | tf_op jit(solution)/shard_map/all_to_all | solution.py:52
  12.0 18.4 %collective-permute-start.1 = (bf16[272,1536]{1,0:T(8,128)(2,1)}, bf16[272,1536]{1,0:T(8,128)(2,1)S(1)}, u32[]{:S(2)}, u32[]{:S(2)}) collective-permute-start(bf16[272,1536]{1,0:T(8,128)(2,1)} %pad_maximum_fusion), channel_id=1, source_target_pairs={{0,248},{8,0},{16,8},{24,16},{32,24},{40,32},{48,40},{56,48},{64,5... | collective-permute-start | bytes 2506760 | tf_op jit(solution)/shard_map/ppermute | solution.py:39
  18.4 15.9 %collective-permute-start = (bf16[272,1536]{1,0:T(8,128)(2,1)}, bf16[272,1536]{1,0:T(8,128)(2,1)}, u32[]{:S(2)}, u32[]{:S(2)}) collective-permute-start(bf16[272,1536]{1,0:T(8,128)(2,1)} %pad_maximum_fusion), channel_id=1, source_target_pairs={{0,8},{8,16},{16,24},{24,32},{32,40},{40,48},{48,56},{56,64},{64,7... | collective-permute-start | bytes 2506760 | tf_op jit(solution)/shard_map/ppermute | solution.py:39
  30.3 21.9 %collective-permute-start.5 = (bf16[4,128,1536]{2,1,0:T(8,128)(2,1)S(1)}, bf16[4,128,1536]{2,1,0:T(8,128)(2,1)}, u32[]{:S(2)}, u32[]{:S(2)}) collective-permute-start(bf16[4,128,1536]{2,1,0:T(8,128)(2,1)S(1)} %all-to-all-done.refs_4_.refs_2_), channel_id=1, source_target_pairs={{0,8},{8,0},{1,9},{9,1},{2,10},{10,2},{3,11},{11,3},{4,12},{12,4},... | collective-permute-start | bytes 4718600 | tf_op jit(solution)/shard_map/ppermute | solution.py:43
  34.3 17.9 %copy-start.2 = (bf16[192,1536]{1,0:T(8,128)(2,1)S(1)}, bf16[192,1536]{1,0:T(8,128)(2,1)}, u32[]{:S(2)}) copy-start(bf16[192,1536]{1,0:T(8,128)(2,1)} %refs_2_.1) | copy-start | bytes 1769476
  34.3 17.9 %collective-permute-start.3 = (bf16[128,1536]{1,0:T(8,128)(2,1)}, bf16[128,1536]{1,0:T(8,128)(2,1)S(1)}, u32[]{:S(2)}, u32[]{:S(2)}) collective-permute-start(bf16[128,1536]{1,0:T(8,128)(2,1)} %bitcast.26), channel_id=1, source_target_pairs={{0,248},{8,0},{16,8},{24,16},{32,24},{40,32},{48,40},{56,48},{64,5... | collective-permute-start | bytes 1179656 | tf_op jit(solution)/shard_map/ppermute | solution.py:39
  39.1 13.1 %collective-permute-start.2 = (bf16[128,1536]{1,0:T(8,128)(2,1)}, bf16[128,1536]{1,0:T(8,128)(2,1)S(1)}, u32[]{:S(2)}, u32[]{:S(2)}) collective-permute-start(bf16[128,1536]{1,0:T(8,128)(2,1)} %bitcast.27), channel_id=1, source_target_pairs={{0,8},{8,16},{16,24},{24,32},{32,40},{40,48},{48,56},{56,64},{64,7... | collective-permute-start | bytes 1179656 | tf_op jit(solution)/shard_map/ppermute | solution.py:39
  39.1 13.1 %collective-permute-start.4 = (bf16[192,1536]{1,0:T(8,128)(2,1)}, bf16[192,1536]{1,0:T(8,128)(2,1)S(1)}, u32[]{:S(2)}, u32[]{:S(2)}) collective-permute-start(bf16[192,1536]{1,0:T(8,128)(2,1)} %refs_2_.1), channel_id=1, source_target_pairs={{0,4},{12,8},{1,5},{13,9},{2,6},{14,10},{3,7},{15,11},{16,20},{28,... | collective-permute-start | bytes 1769480 | tf_op jit(solution)/shard_map/ppermute | solution.py:291
  41.7 1.0 copy-start.9
  42.7 2.3 %copy-start.15 = (bf16[1536,1536]{1,0:T(8,128)(2,1)S(1)}, bf16[1536,1536]{1,0:T(8,128)(2,1)}, u32[]{:S(2)}) copy-start(bf16[1536,1536]{1,0:T(8,128)(2,1)} %constant.30.clone.refs_6_) | copy-start | bytes 14155780
  52.1 18.4 %copy-start.16 = (bf16[128,1536]{1,0:T(8,128)(2,1)}, bf16[128,1536]{1,0:T(8,128)(2,1)S(1)}, u32[]{:S(2)}) copy-start(bf16[128,1536]{1,0:T(8,128)(2,1)S(1)} %get-tuple-element.48.refs_1_) | copy-start | bytes 1179652
  52.1 3.1 %copy-start.11 = (bf16[128,1536]{1,0:T(8,128)(2,1)}, bf16[128,1536]{1,0:T(8,128)(2,1)S(1)}, u32[]{:S(2)}) copy-start(bf16[128,1536]{1,0:T(8,128)(2,1)S(1)} %collective-permute-done.3.refs_9_) | copy-start | bytes 1179652
  52.2 3.1 %copy-start.13 = (bf16[128,1536]{1,0:T(8,128)(2,1)}, bf16[128,1536]{1,0:T(8,128)(2,1)S(1)}, u32[]{:S(2)}) copy-start(bf16[128,1536]{1,0:T(8,128)(2,1)S(1)} %collective-permute-done.2.refs_8_) | copy-start | bytes 1179652
  71.8 18.0 %collective-permute-start.7 = (bf16[144,1536]{1,0:T(8,128)(2,1)}, bf16[144,1536]{1,0:T(8,128)(2,1)}, u32[]{:S(2)}, u32[]{:S(2)}) collective-permute-start(bf16[144,1536]{1,0:T(8,128)(2,1)} %get-tuple-element.41.refs_7_), channel_id=1, source_target_pairs={{0,248},{8,0},{16,8},{24,16},{32,24},{40,32},{48,40},{56,48},{64,5... | collective-permute-start | bytes 1327112 | tf_op jit(solution)/shard_map/ppermute | solution.py:39
  79.4 11.7 %collective-permute-start.6 = (bf16[144,1536]{1,0:T(8,128)(2,1)}, bf16[144,1536]{1,0:T(8,128)(2,1)}, u32[]{:S(2)}, u32[]{:S(2)}) collective-permute-start(bf16[144,1536]{1,0:T(8,128)(2,1)} %get-tuple-element.41.refs_7_), channel_id=1, source_target_pairs={{0,8},{8,16},{16,24},{24,32},{32,40},{40,48},{48,56},{56,64},{64,7... | collective-permute-start | bytes 1327112 | tf_op jit(solution)/shard_map/ppermute | solution.py:39
  79.4 22.0 %collective-permute-start.10 = (bf16[192,1536]{1,0:T(8,128)(2,1)}, bf16[192,1536]{1,0:T(8,128)(2,1)}, u32[]{:S(2)}, u32[]{:S(2)}) collective-permute-start(bf16[192,1536]{1,0:T(8,128)(2,1)} %get-tuple-element.51.refs_2_), channel_id=1, source_target_pairs={{3,0},{0,1},{1,2},{2,3},{7,4},{4,5},{5,6},{6,7},{11,8},{8,9},{9,10... | collective-permute-start | bytes 1769480 | tf_op jit(solution)/shard_map/ppermute | solution.py:47
  79.4 22.5 %collective-permute-start.9 = (bf16[192,1536]{1,0:T(8,128)(2,1)}, bf16[192,1536]{1,0:T(8,128)(2,1)}, u32[]{:S(2)}, u32[]{:S(2)}) collective-permute-start(bf16[192,1536]{1,0:T(8,128)(2,1)} %get-tuple-element.51.refs_2_), channel_id=1, source_target_pairs={{2,0},{3,1},{0,2},{1,3},{6,4},{7,5},{4,6},{5,7},{10,8},{11,9},{8,1... | collective-permute-start | bytes 1769480 | tf_op jit(solution)/shard_map/ppermute | solution.py:47
  82.6 22.4 %collective-permute-start.8 = (bf16[192,1536]{1,0:T(8,128)(2,1)}, bf16[192,1536]{1,0:T(8,128)(2,1)}, u32[]{:S(2)}, u32[]{:S(2)}) collective-permute-start(bf16[192,1536]{1,0:T(8,128)(2,1)} %get-tuple-element.51.refs_2_), channel_id=1, source_target_pairs={{1,0},{2,1},{3,2},{0,3},{5,4},{6,5},{7,6},{4,7},{9,8},{10,9},{11,1... | collective-permute-start | bytes 1769480 | tf_op jit(solution)/shard_map/ppermute | solution.py:47
  86.2 22.4 %all-to-all-start.2 = ((bf16[8,24,1536]{2,1,0:T(8,128)(2,1)}), bf16[8,24,1536]{2,1,0:T(8,128)(2,1)S(1)}, u32[]{:S(2)}, u32[]{:S(2)}) async-start(bf16[8,24,1536]{2,1,0:T(8,128)(2,1)} %bitcast.12), calls=%async_computation.2 | async-start | bytes 1179648 | tf_op jit(solution)/shard_map/all_to_all | solution.py:338
  91.0 1.0 copy-start.10
  92.0 1.0 copy-start.12
  93.0 1.0 copy-start.14
  101.3 8.9 %collective-permute-start.11 = (bf16[192,1536]{1,0:T(8,128)(2,1)}, bf16[192,1536]{1,0:T(8,128)(2,1)S(1)}, u32[]{:S(2)}, u32[]{:S(2)}) collective-permute-start(bf16[192,1536]{1,0:T(8,128)(2,1)} %get-tuple-element.51.refs_2_), channel_id=1, source_target_pairs={{0,8},{8,0},{1,9},{9,1},{2,10},{10,2},{3,11},{11,3},{4,12},{12,4},... | collective-permute-start | bytes 1769480 | tf_op jit(solution)/shard_map/ppermute | solution.py:43
  101.4 12.4 %collective-permute-start.14 = (bf16[192,1536]{1,0:T(8,128)(2,1)}, bf16[192,1536]{1,0:T(8,128)(2,1)S(1)}, u32[]{:S(2)}, u32[]{:S(2)}) collective-permute-start(bf16[192,1536]{1,0:T(8,128)(2,1)} %collective-permute-done.10.refs_5_), channel_id=1, source_target_pairs={{0,8},{8,0},{1,9},{9,1},{2,10},{10,2},{3,11},{11,3},{4,12},{12,4},... | collective-permute-start | bytes 1769480 | tf_op jit(solution)/shard_map/ppermute | solution.py:43
  101.9 13.8 %collective-permute-start.13 = (bf16[192,1536]{1,0:T(8,128)(2,1)}, bf16[192,1536]{1,0:T(8,128)(2,1)S(1)}, u32[]{:S(2)}, u32[]{:S(2)}) collective-permute-start(bf16[192,1536]{1,0:T(8,128)(2,1)} %collective-permute-done.9.refs_4_), channel_id=1, source_target_pairs={{0,8},{8,0},{1,9},{9,1},{2,10},{10,2},{3,11},{11,3},{4,12},{12,4},... | collective-permute-start | bytes 1769480 | tf_op jit(solution)/shard_map/ppermute | solution.py:43
  105.0 11.6 %collective-permute-start.12 = (bf16[192,1536]{1,0:T(8,128)(2,1)}, bf16[192,1536]{1,0:T(8,128)(2,1)}, u32[]{:S(2)}, u32[]{:S(2)}) collective-permute-start(bf16[192,1536]{1,0:T(8,128)(2,1)} %collective-permute-done.8.refs_3_), channel_id=1, source_target_pairs={{0,8},{8,0},{1,9},{9,1},{2,10},{10,2},{3,11},{11,3},{4,12},{12,4},... | collective-permute-start | bytes 1769480 | tf_op jit(solution)/shard_map/ppermute | solution.py:43
  109.3 15.6 %collective-permute-start.15 = (f32[6,1536]{1,0:T(8,128)S(1)}, f32[6,1536]{1,0:T(8,128)S(1)}, u32[]{:S(2)}, u32[]{:S(2)}) collective-permute-start(f32[6,1536]{1,0:T(8,128)S(1)} %get-tuple-element.58), channel_id=1, source_target_pairs={{0,4},{4,0},{16,20},{20,16},{1,5},{5,1},{17,21},{21,17},{2,6},{6,2... | collective-permute-start | bytes 110600 | tf_op jit(solution)/shard_map/ppermute | solution.py:361
  110.2 0.8 copy-start.3
  111.1 13.8 %collective-permute-start.16 = (f32[6,1536]{1,0:T(8,128)S(1)}, f32[6,1536]{1,0:T(8,128)S(1)}, u32[]{:S(2)}, u32[]{:S(2)}) collective-permute-start(f32[6,1536]{1,0:T(8,128)S(1)} %get-tuple-element.59), channel_id=1, source_target_pairs={{0,16},{4,20},{16,0},{20,4},{1,17},{5,21},{17,1},{21,5},{2,18},{6,... | collective-permute-start | bytes 110600 | tf_op jit(solution)/shard_map/ppermute | solution.py:361
  113.8 0.8 copy-start.5
  114.6 10.2 %collective-permute-start.17 = (f32[6,1536]{1,0:T(8,128)S(1)}, f32[6,1536]{1,0:T(8,128)S(1)}, u32[]{:S(2)}, u32[]{:S(2)}) collective-permute-start(f32[6,1536]{1,0:T(8,128)S(1)} %get-tuple-element.60), channel_id=1, source_target_pairs={{0,20},{4,16},{16,4},{20,0},{1,21},{5,17},{17,5},{21,1},{2,22},{6,... | collective-permute-start | bytes 110600 | tf_op jit(solution)/shard_map/ppermute | solution.py:361
  115.7 0.8 copy-start.7
  116.5 1.1 copy-start.4
  117.6 1.1 copy-start.6
  118.7 1.1 copy-start.8
  119.7 1.0 copy-start.17

commit v3 on v2

--- a/solution.py
+++ b/solution.py
@@ -22,6 +22,8 @@
 GROUP = 8
 GROUP_ROWS = HD // GROUP
 EXTRA = 16
+SPAN = 384
+CHUNKS = 4
 
 F32 = jnp.float32
 BF16 = jnp.bfloat16
@@ -47,9 +49,8 @@
     return lax.ppermute(value, "x", [((i + step) % 4, i) for i in range(4)])
 
 
-def gather_x(value):
-    spread = jnp.broadcast_to(value[None], (4,) + value.shape)
-    return lax.all_to_all(spread, "x", 0, 0, tiled=True)
+def along_x(value, step):
+    return lax.ppermute(value, "x", [((i + step) % 4, i) for i in range(4)])
 
 
 def after(value, *others):
@@ -73,36 +74,83 @@
 def row_bias(info, left, right):
     frame, back, ahead = (info[n].astype(F32) for n in range(3))
     low, high, position = frame - back, frame + ahead, info[3]
-    place = lax.broadcasted_iota(jnp.int32, (1, 3 * TILE), 1)
+    column = lax.broadcasted_iota(jnp.int32, (1, 3 * TILE), 1)
     on_left = visible(told(left)[0], low, high, position > 0)
     on_right = visible(told(right)[0], low, high, position < TILES - 1)
-    return jnp.where(place < TILE, on_left, jnp.where(place < 2 * TILE, 0.0, on_right))
+    return jnp.where(column < TILE, on_left, jnp.where(column < 2 * TILE, 0.0, on_right))
 
 
 def column_bias(info, left, right):
     frame, position = info[0].astype(F32), info[3]
-    place = lax.broadcasted_iota(jnp.int32, (1, 2 * TILE), 1)
+    column = lax.broadcasted_iota(jnp.int32, (1, 2 * TILE), 1)
     sides = []
     for tile, there in ((left, position > 0), (right, position < TILES - 1)):
         center, back, ahead = told(tile)
         sides.append(visible(frame, center - back, center + ahead, there))
-    return jnp.where(place < TILE, sides[0], sides[1])
+    return jnp.where(column < TILE, sides[0], sides[1])
 
 
 KEYS = slice(0, TILE)
 VALUES = slice(TILE, 2 * TILE)
 
 
+def pack_kernel(frame, back, ahead, k, v, out, sems):
+    copies = [
+        pltpu.make_async_copy(k, out.at[KEYS], sems.at[0]),
+        pltpu.make_async_copy(v, out.at[VALUES], sems.at[1]),
+    ]
+    for copy in copies:
+        copy.start()
+    lane = lax.broadcasted_iota(jnp.int32, (EXTRA, HD), 1)
+    said = jnp.where(lane == 0, frame[0, 0], jnp.where(lane == 1, back[0, 0], ahead[0, 0]))
+    out[2 * TILE :, :] = said.astype(F32).astype(BF16)
+    for copy in copies:
+        copy.wait()
+
+
+def pack(frame, back, ahead, k, v):
+    return pl.pallas_call(
+        pack_kernel,
+        in_specs=[pl.BlockSpec(memory_space=pltpu.SMEM)] * 3 + [pl.BlockSpec(memory_space=pltpu.HBM)] * 2,
+        out_specs=pl.BlockSpec(memory_space=VMEM),
+        out_shape=jax.ShapeDtypeStruct((2 * TILE + EXTRA, HD), BF16),
+        scratch_shapes=[pltpu.SemaphoreType.DMA((2,))],
+        compiler_params=pltpu.CompilerParams(vmem_limit_bytes=56 * 1024 * 1024),
+    )(frame, back, ahead, k, v)
+
+
+def join_kernel(*refs):
+    parts, out, sems = refs[:-2], refs[-2], refs[-1]
+    copies = [
+        pltpu.make_async_copy(part, out.at[n * TILE : (n + 1) * TILE], sems.at[n])
+        for n, part in enumerate(parts)
+    ]
+    for copy in copies:
+        copy.start()
+    for copy in copies:
+        copy.wait()
+
+
+def join(parts):
+    return pl.pallas_call(
+        join_kernel,
+        in_specs=[pl.BlockSpec(memory_space=pltpu.HBM)] * len(parts),
+        out_specs=pl.BlockSpec(memory_space=VMEM),
+        out_shape=jax.ShapeDtypeStruct((len(parts) * TILE, HD), BF16),
+        scratch_shapes=[pltpu.SemaphoreType.DMA((len(parts),))],
+        cost_estimate=pl.CostEstimate(flops=1024, bytes_accessed=1024, transcendentals=0),
+        compiler_params=pltpu.CompilerParams(vmem_limit_bytes=4 * 1024 * 1024),
+    )(*parts)
+
+
 def forward_kernel(scalars, near, far, copies, outs, scratch):
     (info,) = scalars
-    q, k, v, left, right = near
-    (order,) = far
+    q, k, v, left, right, order = near
     att, att_t, stats = outs
+    bias = row_bias(info, left, right)
     lane = lax.broadcasted_iota(jnp.int32, (TILE, 128), 1)
     total = jnp.zeros((TILE, 128), F32)
     for h in range(HEADS):
-        if h == 0:
-            bias = row_bias(info, left, right)
         c = head(h)
         keys = jnp.concatenate([left[KEYS, c], k[:, c], right[KEYS, c]], axis=0)
         values = jnp.concatenate([left[VALUES, c], v[:, c], right[VALUES, c]], axis=0)
@@ -113,11 +161,13 @@
         p = (e * (1.0 / mass)).astype(BF16)
         att[:, c] = dot(p, values).astype(BF16)
         total = jnp.where(lane == h, top + jnp.log(mass), total)
+        if (h + 1) * HEAD_DIM % SPAN == 0:
+            n = (h + 1) * HEAD_DIM // SPAN - 1
+            moved = dot(order[...], att[:, n * SPAN : (n + 1) * SPAN], NT).astype(BF16)
+            rows = SPAN // GROUP
+            for g in range(GROUP):
+                att_t[g, n * rows : (n + 1) * rows, :] = moved[g * rows : (g + 1) * rows]
     stats[...] = total
-    copies[0].wait()
-    for g in range(GROUP):
-        cols = slice(g * GROUP_ROWS, (g + 1) * GROUP_ROWS)
-        att_t[g] = dot(order[cols, :], att[...], NT).astype(BF16)
 
 
 def place(info, n):
@@ -132,21 +182,19 @@
     out[:, :GROUP_ROWS, :] = att_t[...]
     w[...] = jnp.where(info[4] == info[7], held[...], passed[...])
     for side in range(2):
-        core = info[4] if side == 0 else 1 - info[4]
         for n in range(0, 4, 2):
-            pair = grads[side][n : n + 2].reshape(2 * TILE, HD)
+            pair = grads[side][n * TILE : (n + 2) * TILE, :]
             got = dot(w[...], pair, NT).astype(BF16)
-            out[core * 4 + n, GROUP_ROWS:, :] = got[:, :TILE]
-            out[core * 4 + n + 1, GROUP_ROWS:, :] = got[:, TILE:]
+            out[place(info, side * 4 + n), GROUP_ROWS:, :] = got[:, :TILE]
+            out[place(info, side * 4 + n + 1), GROUP_ROWS:, :] = got[:, TILE:]
 
 
 def weight_kernel(scalars, near, far, copies, outs, scratch):
     (info,), (mixed, *grads), (out,) = scalars, near, outs
     acc = None
     for side in range(2):
-        core = info[4] if side == 0 else 1 - info[4]
-        left = jnp.concatenate([mixed[core * 4 + n, :GROUP_ROWS, :] for n in range(4)], axis=1)
-        term = dot(left, grads[side][...].reshape(4 * TILE, HD))
+        rows = [mixed[place(info, side * 4 + n), :GROUP_ROWS, :] for n in range(4)]
+        term = dot(jnp.concatenate(rows, axis=1), grads[side][...])
         acc = term if acc is None else acc + term
     out[...] = (acc * float(GROUP * TILES * TILE) ** -0.5).astype(BF16)
 
@@ -193,22 +241,25 @@
 
 
 def project_kernel(scalars, near, far, copies, outs, scratch):
-    (info,), (att,), (out,), (turned,) = scalars, near, outs, scratch
+    (info,), (att, *blocks), (out,), (turned,) = scalars, near, outs, scratch
     for h in range(HEADS):
         turned[head(h), :] = att[:, head(h)].T
     acc = jnp.zeros((TILE, HD), F32)
     for n in range(GROUP):
-        copies[n].wait()
         first = pl.multiple_of(place(info, n) * GROUP_ROWS, GROUP_ROWS)
-        acc += dot(turned[pl.ds(first, GROUP_ROWS), :], far[n][...], TN)
+        acc += dot(turned[pl.ds(first, GROUP_ROWS), :], blocks[n][...], TN)
     out[...] = acc.astype(BF16)
 
 
 def backward_kernel(scalars, near, far, copies, outs, scratch):
-    (info,), (dq, dk, dv) = scalars, outs
-    stats, q, k, v, left, right, ga, ql, qr, gal, gar = near
+    dq, dk, dv = outs
+    (info,), (stats,) = scalars, near
+    q, k, v, left, right, ga, ql, qr, gal, gar = far
     st = stats[...]
     for h in range(HEADS):
+        if h % (HEADS // CHUNKS) == 0:
+            for copy in copies[h // (HEADS // CHUNKS)]:
+                copy.wait()
         if h == 0:
             on_row, on_column = row_bias(info, left, right), column_bias(info, left, right)
         c = head(h)
@@ -238,39 +289,41 @@
         dv[:, c] = (dvh + dot(p.astype(BF16), grads)).astype(BF16)
 
 
-def call(kernel, micros, scalars, near, far, outs, scratch=(), mib=4):
+def call(kernel, micros, scalars, near, far, outs, scratch=(), mib=4, chunks=1):
     counts = [len(scalars), len(near), len(far), len(outs), len(far), len(scratch)]
     ends = np.cumsum(counts)
 
     def body(*refs):
         parts = [refs[end - count : end] for end, count in zip(ends, counts)]
         sems = refs[ends[-1]]
-        copies = [
-            pltpu.make_async_copy(ref, buffer, sems.at[n])
-            for n, (ref, buffer) in enumerate(zip(parts[2], parts[4]))
-        ]
-        for copy in copies:
-            copy.start()
-        kernel(parts[0], parts[1], parts[4], copies, parts[3], parts[5])
+        copies = [[] for _ in range(chunks)]
+        for chunk in range(chunks):
+            for n, (ref, buffer) in enumerate(zip(parts[2], parts[4])):
+                width = buffer.shape[-1] // chunks
+                cols = (slice(None),) * (len(buffer.shape) - 1) + (pl.ds(chunk * width, width),)
+                copy = pltpu.make_async_copy(ref.at[cols], buffer.at[cols], sems.at[n, chunk])
+                copy.start()
+                copies[chunk].append(copy)
+        kernel(parts[0], parts[1], parts[4], copies if chunks > 1 else copies[0], parts[3], parts[5])
 
     return pl.pallas_call(
         body,
         in_specs=[pl.BlockSpec(memory_space=pltpu.SMEM)] * len(scalars)
         + [pl.BlockSpec(memory_space=VMEM)] * len(near)
-        + [pl.BlockSpec(memory_space=pl.ANY)] * len(far),
+        + [pl.BlockSpec(memory_space=pltpu.HBM)] * len(far),
         out_specs=[pl.BlockSpec(memory_space=VMEM)] * len(outs),
         out_shape=[jax.ShapeDtypeStruct(s, d) for s, d in outs],
         scratch_shapes=[VMEM(f.shape, f.dtype) for f in far]
         + [VMEM(s, d) for s, d in scratch]
-        + [pltpu.SemaphoreType.DMA((max(1, len(far)),))],
+        + [pltpu.SemaphoreType.DMA((max(1, len(far)), chunks))],
         cost_estimate=pl.CostEstimate(flops=int(micros * 1e9), bytes_accessed=1024, transcendentals=0),
         compiler_params=pltpu.CompilerParams(vmem_limit_bytes=mib * 1024 * 1024),
     )(*scalars, *near, *far)
 
 
 def column_order():
-    features = np.arange(HD).reshape(SIZES + (ROWS_OUT,))
-    return features.transpose(2, 4, 0, 1, 3, 5).reshape(-1)
+    features = np.arange(SPAN).reshape(SPAN // 96, 2, 2, 4, ROWS_OUT)
+    return np.eye(SPAN, dtype=np.float32)[features.transpose(1, 3, 0, 2, 4).reshape(-1)]
 
 
 def shards(query_rows, key_rows, value_rows, frame_of, reach_back, reach_ahead, out_weight, out_grad):
@@ -281,51 +334,49 @@
     where = where + (lax.axis_index("ylo"),)
     info = jnp.stack([frame_of[0, 0], reach_back[0, 0], reach_ahead[0, 0], *where]).astype(jnp.int32)
 
-    note = jnp.pad(info[None, :3].astype(BF16), ((0, EXTRA - 1), (0, HD - 3)))
-    to_send = jnp.concatenate([k, v, note], axis=0)
+    to_send = pack(frame_of, reach_back, reach_ahead, k, v)
     left, right = next_tile(to_send, 1), next_tile(to_send, -1)
 
-    og_mine = gather_x(after(og, to_send))
+    w_passed = lax.ppermute(out_weight, ("core", "ylo"), [(0, 1), (3, 2)])
+
+    og_sent = after(og, to_send)
+    og_mine = join([og] + [along_x(og_sent, step) for step in (1, 2, 3)])
     og_other = core_swap(og_mine)
 
-    w_passed = lax.ppermute(after(out_weight, left, right), ("core", "ylo"), [(0, 1), (3, 2)])
-
-    q2 = after(q, left, right)
-    ql, qr = next_tile(q2, 1), next_tile(q2, -1)
-
-    order = jnp.asarray(np.eye(HD, dtype=np.float32)[column_order()], BF16)
+    order = jnp.asarray(column_order(), BF16)
     att, att_t, stats = call(
         forward_kernel,
         8,
         (info,),
-        (q, k, v, left, right),
-        (order,),
+        (q, k, v, left, right, order),
+        (),
         [(tile, BF16), ((GROUP, GROUP_ROWS, TILE), BF16), ((TILE, 128), F32)],
-        mib=16,
-    )
+        mib=8,
+    )
+
+    q2 = after(q, att)
+    ql, qr = next_tile(q2, 1), next_tile(q2, -1)
 
     mixed, w_block = call(
         spread_kernel,
         2,
         (info,),
-        (after(att_t, ql, qr), out_weight, w_passed, og_mine, og_other),
+        (att_t, out_weight, w_passed, og_mine, og_other),
         (),
         [((GROUP, 2 * GROUP_ROWS, TILE), BF16), ((GROUP_ROWS, HD), BF16)],
     )
+    blocks = [w_block] + [along_x(w_block, step) for step in (1, 2, 3)]
     mixed = lax.all_to_all(mixed, ("core", "x"), 0, 0, tiled=True)
 
     ga, stats = call(
         delta_kernel,
         1,
         (),
-        (mixed, att, stats),
+        (after(mixed, ql, qr), att, stats),
         (),
         [((TILE + EXTRA, HD), BF16), ((TILE, 128), F32)],
     )
     gal, gar = next_tile(ga, 1), next_tile(ga, -1)
-
-    w_late = after(w_block, ga)
-    blocks = [w_block] + [along_x(w_late, step) for step in (1, 2, 3)]
 
     (partial,) = call(
         weight_kernel,
@@ -341,11 +392,13 @@
         backward_kernel,
         9,
         (info,),
-        (after(stats, partial), q, k, v, left, right, ga, ql, qr, gal, gar),
-        (),
+        (after(stats, partial, blocks[1], blocks[3]),),
+        (q, k, v, left, right, ga, ql, qr, gal, gar),
         [(tile, BF16)] * 3,
-        mib=8,
-    )
+        mib=56,
+        chunks=CHUNKS,
+    )
+    blocks = blocks + [core_swap(after(w, dq)) for w in blocks]
 
     pieces = call(
         sum_kernel,
@@ -360,16 +413,14 @@
         pairs = [(i, i ^ step) for i in range(4)]
         arrived.append(lax.ppermute(pieces[step], ("yhi", "ylo"), pairs))
 
-    blocks = blocks + [core_swap(after(w, dq)) for w in blocks]
     (layer_out,) = call(
         project_kernel,
         4,
         (info,),
-        (after(att, pieces[0]),),
-        tuple(blocks),
+        (after(att, pieces[0]), *blocks),
+        (),
         [(tile, BF16)],
         scratch=[((HD, TILE), BF16)],
-        mib=16,
     )
     grad_weight = after(pieces[0], layer_out) + arrived[0] + arrived[1] + arrived[2]
     return layer_out[None], dq[None], dk[None], dv[None], grad_weight

time: 127 us -> 112 us (0.88)
  blocking collectives: 15.2 us -> 0 us
  local copies, waits for them, and re-layouts: 14.4 us -> 2.87 us
  waiting for transfers between devices: 23.6 us -> 28.8 us
  starting transfers between devices: 40.1 us -> 44.5 us
  Pallas kernels: 26.5 us -> 30.5 us
  other arithmetic: 2.77 us -> 0.63 us
    all_to_all x1 -> x0, blocking collectives: 15.2 us -> none  [shards(): mixed = lax.all_to_all(mixed, ('core', 'x'), 0, 0, tiled=True)]
    all_to_all x1, waiting for transfers between devices: 11.9 us -> 0.01 us  [shards(): mixed = lax.all_to_all(mixed, ('core', 'x'), 0, 0, tiled=True)]
    unnamed x38 -> x30, local copies, waits for them, and re-layouts: 13 us -> 2.78 us
    ppermute x6, waiting for transfers between devices: 5.17 us -> 12.7 us  [next_tile(): lax.ppermute(value, FRAME, [(i, (i + step) % TILES) for i in range(TILES)])]
    ppermute x3 -> x6, waiting for transfers between devices: 2.99 us -> 9.39 us  [along_x(): return lax.ppermute(value, 'x', [((i + step) % 4, i) for i in range(4)])]
    ppermute x3 -> x6, starting transfers between devices: 3.74 us -> 8.34 us  [along_x(): return lax.ppermute(value, 'x', [((i + step) % 4, i) for i in range(4)])]
    all_to_all x1, waiting for transfers between devices: 3.57 us -> 6.66 us  [shards(): lax.all_to_all(partial.reshape(8, GROUP_ROWS // 8, HD), 'z', 0, 0, tiled=...]
    pallas_call x0 -> x2, Pallas kernels: none -> 2.82 us  [the longest x1 2.04 us: pack(): pl.pallas_call(pack_kernel, in_specs=[pl.BlockSpec(memory_space=pltpu.SME...]
  transfers between devices with their start and end apart: 20 -> 23, of which waited for: 5 -> 8; matrix products, arithmetic and copies ran while one was open for 0% -> 0% of each run, Pallas kernels for 18% -> 22%
where the time goes in v3:
time: 112 us; the launch traced here: 110 us
  starting transfers between devices  44.5 us (40%)
  Pallas kernels  30.5 us (27%)
  waiting for transfers between devices  28.8 us (26%)
  between operations  2.95 us (3%)
  local copies, waits for them, and re-layouts  2.87 us (3%)
    pallas_call x7, Pallas kernels, call(): pl.pallas_call(body, in_specs=[pl.BlockSpec(memory_space=pltpu.SMEM)] * l...  27.7 us
    ppermute x6, starting transfers between devices, next_tile(): lax.ppermute(value, FRAME, [(i, (i + step) % TILES) for i in range(TILES)])  17.2 us
    ppermute x6, waiting for transfers between devices, next_tile(): lax.ppermute(value, FRAME, [(i, (i + step) % TILES) for i in range(TILES)])  12.7 us
    ppermute x6, waiting for transfers between devices, along_x(): return lax.ppermute(value, 'x', [((i + step) % 4, i) for i in range(4)])  9.39 us
    ppermute x6, starting transfers between devices, along_x(): return lax.ppermute(value, 'x', [((i + step) % 4, i) for i in range(4)])  8.34 us
    all_to_all x1, waiting for transfers between devices, shards(): lax.all_to_all(partial.reshape(8, GROUP_ROWS // 8, HD), 'z', 0, 0, tiled=...  6.66 us
    all_to_all x1, starting transfers between devices, shards(): mixed = lax.all_to_all(mixed, ('core', 'x'), 0, 0, tiled=True)  5.02 us
    ppermute x3, starting transfers between devices, shards(): arrived.append(lax.ppermute(pieces[step], ('yhi', 'ylo'), pairs))  4.79 us
  transfers between devices with their start and end apart: 23, of which 8 were waited for; matrix products, arithmetic and copies ran while one was open for 0% of the time, Pallas kernels for 22%

profile of v3, /device:TPU:2, one launch (start us, length us, event | category | flops | bytes accessed | tf_op | source)
XLA Modules:
  0.0 110.3 jit_solution(13974009644028477311)
XLA Ops:
  2.6 2.0 %shard_map.128 = bf16[272,1536]{1,0:T(8,128)(2,1)} custom-call(s32[1,1]{1,0:T(1,128)} %copy.14.frame, s32[1,1]{1,0:T(1,128)} %copy.15.back, s32[1,1]{1,0:T(1,128)} %copy.16.ahead, bf16[128,1536]{1,0:T(8,128)(2,1)} %bitcast.24, bf16[128,1536]{1,0:T(8,128)(2,1)} %bitcast.27), custom_call_target="tpu_custom_call" | custom-call | tf_op jit(solution)/shard_map/pallas_call | solution.py:112
  4.7 0.0 copy-start.1
  4.7 0.0 copy-start.2
  4.7 1.6 %collective-permute-start.5 = (bf16[128,1536]{1,0:T(8,128)(2,1)S(1)}, bf16[128,1536]{1,0:T(8,128)(2,1)S(1)}, u32[]{:S(2)}, u32[]{:S(2)}) collective-permute-start(bf16[128,1536]{1,0:T(8,128)(2,1)S(1)} %bitcast.20), channel_id=1, source_target_pairs={{3,0},{0,1},{1,2},{2,3},{7,4},{4,5},{5,6},{6,7},{11,8},{8,9},{9,10... | collective-permute-start | bytes 1179656 | tf_op jit(solution)/shard_map/ppermute | solution.py:53
  6.3 2.8 %collective-permute-start.4 = (bf16[128,1536]{1,0:T(8,128)(2,1)S(1)}, bf16[128,1536]{1,0:T(8,128)(2,1)S(1)}, u32[]{:S(2)}, u32[]{:S(2)}) collective-permute-start(bf16[128,1536]{1,0:T(8,128)(2,1)S(1)} %bitcast.21), channel_id=1, source_target_pairs={{2,0},{3,1},{0,2},{1,3},{6,4},{7,5},{4,6},{5,7},{10,8},{11,9},{8,1... | collective-permute-start | bytes 1179656 | tf_op jit(solution)/shard_map/ppermute | solution.py:53
  9.2 0.4 collective-permute-start.3
  9.6 7.1 %collective-permute-start.1 = (bf16[272,1536]{1,0:T(8,128)(2,1)}, bf16[272,1536]{1,0:T(8,128)(2,1)}, u32[]{:S(2)}, u32[]{:S(2)}) collective-permute-start(bf16[272,1536]{1,0:T(8,128)(2,1)} %shard_map.128), channel_id=1, source_target_pairs={{0,248},{8,0},{16,8},{24,16},{32,24},{40,32},{48,40},{56,48},{64,5... | collective-permute-start | bytes 2506760 | tf_op jit(solution)/shard_map/ppermute | solution.py:41
  16.7 0.4 collective-permute-done.5.refs_3_
  17.1 2.8 %collective-permute-done.4.refs_2_ = bf16[128,1536]{1,0:T(8,128)(2,1)S(1)} collective-permute-done((bf16[128,1536]{1,0:T(8,128)(2,1)S(1)}, bf16[128,1536]{1,0:T(8,128)(2,1)S(1)}, u32[]{:S(2)}, u32[]{:S(2)}) %collective-permute-start.4) | collective-permute-done | bytes 393248 | tf_op jit(solution)/shard_map/ppermute | solution.py:53
  19.9 6.2 %collective-permute-done.3.refs_1_ = bf16[128,1536]{1,0:T(8,128)(2,1)S(1)} collective-permute-done((bf16[128,1536]{1,0:T(8,128)(2,1)S(1)}, bf16[128,1536]{1,0:T(8,128)(2,1)S(1)}, u32[]{:S(2)}, u32[]{:S(2)}) %collective-permute-start.3) | collective-permute-done | bytes 393248 | tf_op jit(solution)/shard_map/ppermute | solution.py:53
  26.0 0.8 shard_map.130.refs_4_.refs_2_
  26.8 0.1 collective-permute-start.6
  26.9 4.4 %collective-permute-start.2 = (bf16[192,1536]{1,0:T(8,128)(2,1)S(1)}, bf16[192,1536]{1,0:T(8,128)(2,1)}, u32[]{:S(2)}, u32[]{:S(2)}) collective-permute-start(bf16[192,1536]{1,0:T(8,128)(2,1)S(1)} %copy-done.5), channel_id=1, source_target_pairs={{0,4},{12,8},{1,5},{13,9},{2,6},{14,10},{3,7},{15,11},{16,20},{28,... | collective-permute-start | bytes 1769480 | tf_op jit(solution)/shard_map/ppermute | solution.py:340
  31.4 0.1 stack.23.refs_0_
  31.4 1.1 collective-permute-done.refs_4_.refs_5_
  32.5 0.0 copy-start.7
  32.6 1.0 copy-done.7
  33.5 6.5 %shard_map.129 = (bf16[128,1536]{1,0:T(8,128)(2,1)S(1)}, bf16[8,192,128]{2,1,0:T(8,128)(2,1)S(1)}, f32[128,128]{1,0:T(8,128)S(1)}) custom-call(s32[8]{0:T(128)S(1)} %stack.23.refs_0_, bf16[128,1536]{1,0:T(8,128)(2,1)S(1)} %bitcast.31, bf16[128,1536]{1,0:T(8,128)(2,1)S(1)} %bitcast.26, bf16[128,1536]{1,0:T(8,128)(2,1)S(1)} %bitcast.29, ...), custom_call_target="tpu_custom_call" | custom-call | flops 8000000000 | bytes 1024 | tf_op jit(solution)/shard_map/pallas_call | solution.py:309
  40.0 0.0 copy-start.11
  40.0 3.8 %shard_map.131 = (bf16[8,384,128]{2,1,0:T(8,128)(2,1)}, bf16[192,1536]{1,0:T(8,128)(2,1)S(1)}) custom-call(s32[8]{0:T(128)S(1)} %stack.23.refs_0_, bf16[8,192,128]{2,1,0:T(8,128)(2,1)S(1)} %get-tuple-element.32.refs_1_, bf16[192,1536]{1,0:T(8,128)(2,1)S(1)} %copy-done.5, bf16[192,1536]{1,0:T(8,128)(2,1)} %collective-permute-done.2.refs_3_, ...), custom_call_target="tpu_custom_call" | custom-call | flops 2000000000 | bytes 1024 | tf_op jit(solution)/shard_map/pallas_call | solution.py:309
  43.9 0.0 copy-start.12
  43.9 5.0 %all-to-all-start = ((bf16[8,384,128]{2,1,0:T(8,128)(2,1)}), bf16[8,384,128]{2,1,0:T(8,128)(2,1)S(1)}, u32[]{:S(2)}, u32[]{:S(2)}) async-start(bf16[8,384,128]{2,1,0:T(8,128)(2,1)} %get-tuple-element.34), calls=%async_computation | async-start | bytes 1572864 | tf_op jit(solution)/shard_map/all_to_all | solution.py:369
  48.9 8.5 %collective-permute-start.8 = (bf16[128,1536]{1,0:T(8,128)(2,1)S(1)}, bf16[128,1536]{1,0:T(8,128)(2,1)S(1)}, u32[]{:S(2)}, u32[]{:S(2)}) collective-permute-start(bf16[128,1536]{1,0:T(8,128)(2,1)S(1)} %bitcast.32), channel_id=1, source_target_pairs={{0,248},{8,0},{16,8},{24,16},{32,24},{40,32},{48,40},{56,48},{64,5... | collective-permute-start | bytes 1179656 | tf_op jit(solution)/shard_map/ppermute | solution.py:41
  57.4 1.5 %collective-permute-start.10 = (bf16[192,1536]{1,0:T(8,128)(2,1)S(1)}, bf16[192,1536]{1,0:T(8,128)(2,1)}, u32[]{:S(2)}, u32[]{:S(2)}) collective-permute-start(bf16[192,1536]{1,0:T(8,128)(2,1)S(1)} %get-tuple-element.47.refs_2_), channel_id=1, source_target_pairs={{3,0},{0,1},{1,2},{2,3},{7,4},{4,5},{5,6},{6,7},{11,8},{8,9},{9,10... | collective-permute-start | bytes 1769480 | tf_op jit(solution)/shard_map/ppermute | solution.py:53
  58.9 0.6 collective-permute-start.9
  59.4 3.3 %collective-permute-done.8.refs_9_ = bf16[128,1536]{1,0:T(8,128)(2,1)S(1)} collective-permute-done((bf16[128,1536]{1,0:T(8,128)(2,1)S(1)}, bf16[128,1536]{1,0:T(8,128)(2,1)S(1)}, u32[]{:S(2)}, u32[]{:S(2)}) %collective-permute-start.8) | collective-permute-done | bytes 393248 | tf_op jit(solution)/shard_map/ppermute | solution.py:41
  62.8 0.8 copy-done.14
  63.5 4.8 %collective-permute-done.7.refs_8_ = bf16[128,1536]{1,0:T(8,128)(2,1)} collective-permute-done((bf16[128,1536]{1,0:T(8,128)(2,1)S(1)}, bf16[128,1536]{1,0:T(8,128)(2,1)}, u32[]{:S(2)}, u32[]{:S(2)}) %collective-permute-start.7) | collective-permute-done | bytes 393248 | tf_op jit(solution)/shard_map/ppermute | solution.py:41
  68.3 1.0 copy-done.9
  69.3 1.2 %shard_map.132 = (bf16[144,1536]{1,0:T(8,128)(2,1)}, f32[128,128]{1,0:T(8,128)S(1)}) custom-call(bf16[8,384,128]{2,1,0:T(8,128)(2,1)S(1)} %all-to-all-done.refs_0_.refs_1_, bf16[128,1536]{1,0:T(8,128)(2,1)S(1)} %copy-done.9, f32[128,128]{1,0:T(8,128)S(1)} %copy-done.12), custom_call_target="tpu_custom_call" | custom-call | flops 1000000000 | bytes 1024 | tf_op jit(solution)/shard_map/pallas_call | solution.py:309
  70.6 1.6 %collective-permute-start.12 = (bf16[144,1536]{1,0:T(8,128)(2,1)}, bf16[144,1536]{1,0:T(8,128)(2,1)}, u32[]{:S(2)}, u32[]{:S(2)}) collective-permute-start(bf16[144,1536]{1,0:T(8,128)(2,1)} %get-tuple-element.38.refs_7_), channel_id=1, source_target_pairs={{0,248},{8,0},{16,8},{24,16},{32,24},{40,32},{48,40},{56,48},{64,5... | collective-permute-start | bytes 1327112 | tf_op jit(solution)/shard_map/ppermute | solution.py:41
  72.2 1.5 %collective-permute-start.13 = (bf16[192,1536]{1,0:T(8,128)(2,1)S(1)}, bf16[192,1536]{1,0:T(8,128)(2,1)}, u32[]{:S(2)}, u32[]{:S(2)}) collective-permute-start(bf16[192,1536]{1,0:T(8,128)(2,1)S(1)} %get-tuple-element.47.refs_2_), channel_id=1, source_target_pairs={{2,0},{3,1},{0,2},{1,3},{6,4},{7,5},{4,6},{5,7},{10,8},{11,9},{8,1... | collective-permute-start | bytes 1769480 | tf_op jit(solution)/shard_map/ppermute | solution.py:53
  73.7 3.0 %shard_map.133 = bf16[192,1536]{1,0:T(8,128)(2,1)} custom-call(s32[8]{0:T(128)S(1)} %stack.23.refs_0_, bf16[8,384,128]{2,1,0:T(8,128)(2,1)S(1)} %all-to-all-done.refs_0_.refs_1_, bf16[512,1536]{1,0:T(8,128)(2,1)S(1)} %shard_map.130.refs_4_.refs_2_, bf16[512,1536]{1,0:T(8,128)(2,1)} %collective-permute-done.6.refs_5_.refs_3_), custom_call_target="tpu_custom_call" | custom-call | flops 2000000000 | bytes 1024 | tf_op jit(solution)/shard_map/pallas_call | solution.py:309
  76.8 3.5 %all-to-all-start.1 = ((bf16[8,24,1536]{2,1,0:T(8,128)(2,1)}), bf16[8,24,1536]{2,1,0:T(8,128)(2,1)S(1)}, u32[]{:S(2)}, u32[]{:S(2)}) async-start(bf16[8,24,1536]{2,1,0:T(8,128)(2,1)} %bitcast.12), calls=%async_computation.1 | async-start | bytes 1179648 | tf_op jit(solution)/shard_map/all_to_all | solution.py:389
  80.4 0.0 copy-start.4
  80.4 3.5 %collective-permute-done.11.refs_10_ = bf16[144,1536]{1,0:T(8,128)(2,1)} collective-permute-done((bf16[144,1536]{1,0:T(8,128)(2,1)}, bf16[144,1536]{1,0:T(8,128)(2,1)}, u32[]{:S(2)}, u32[]{:S(2)}) %collective-permute-start.11) | collective-permute-done | bytes 442400 | tf_op jit(solution)/shard_map/ppermute | solution.py:41
  83.9 8.9 %shard_map.134 = (bf16[128,1536]{1,0:T(8,128)(2,1)}, bf16[128,1536]{1,0:T(8,128)(2,1)}, bf16[128,1536]{1,0:T(8,128)(2,1)}) custom-call(s32[8]{0:T(128)} %copy-done.3, f32[128,128]{1,0:T(8,128)} %copy-done.13, bf16[128,1536]{1,0:T(8,128)(2,1)} %bitcast.30, bf16[128,1536]{1,0:T(8,128)(2,1)} %bitcast.25, bf16[128,1536]{1,0:T(8,128)(2,1)} %bitcast.28, ...), custom_call_target="tpu_custom_call" | custom-call | flops 8999999488 | bytes 1024 | tf_op jit(solution)/shard_map/pallas_call | solution.py:309
  92.8 0.1 collective-permute-start.14
  92.9 0.5 collective-permute-start.15
  93.4 0.1 collective-permute-start.16
  93.5 0.4 collective-permute-start.17
  93.9 6.7 %all-to-all-done.1.refs_1_ = bf16[8,24,1536]{2,1,0:T(8,128)(2,1)S(1)} async-done(((bf16[8,24,1536]{2,1,0:T(8,128)(2,1)}), bf16[8,24,1536]{2,1,0:T(8,128)(2,1)S(1)}, u32[]{:S(2)}, u32[]{:S(2)}) %all-to-all-start.1) | async-done | bytes 589856 | tf_op jit(solution)/shard_map/all_to_all | solution.py:389
  100.6 0.7 shard_map.135
  101.3 0.3 collective-permute-start.18
  101.5 2.5 %collective-permute-start.19 = (f32[6,1536]{1,0:T(8,128)S(1)}, f32[6,1536]{1,0:T(8,128)S(1)}, u32[]{:S(2)}, u32[]{:S(2)}) collective-permute-start(f32[6,1536]{1,0:T(8,128)S(1)} %get-tuple-element.55), channel_id=1, source_target_pairs={{0,16},{4,20},{16,0},{20,4},{1,17},{5,21},{17,1},{21,5},{2,18},{6,... | collective-permute-start | bytes 110600 | tf_op jit(solution)/shard_map/ppermute | solution.py:414
  104.0 2.0 %collective-permute-start.20 = (f32[6,1536]{1,0:T(8,128)S(1)}, f32[6,1536]{1,0:T(8,128)S(1)}, u32[]{:S(2)}, u32[]{:S(2)}) collective-permute-start(f32[6,1536]{1,0:T(8,128)S(1)} %get-tuple-element.56), channel_id=1, source_target_pairs={{0,20},{4,16},{16,4},{20,0},{1,21},{5,17},{17,5},{21,1},{2,22},{6,... | collective-permute-start | bytes 110600 | tf_op jit(solution)/shard_map/ppermute | solution.py:414
  106.1 3.5 %shard_map.136 = bf16[128,1536]{1,0:T(8,128)(2,1)} custom-call(s32[8]{0:T(128)S(1)} %copy-done.4, bf16[128,1536]{1,0:T(8,128)(2,1)S(1)} %copy-done.10, bf16[192,1536]{1,0:T(8,128)(2,1)S(1)} %get-tuple-element.47.refs_2_, bf16[192,1536]{1,0:T(8,128)(2,1)} %collective-permute-done.9.refs_3_, bf16[192,1536]{1,0:T(8,128)(2,1)} %collective-permute-done.13.refs_4_, ...), custom_call_target="tpu_custom_call" | custom-call | flops 4000000000 | bytes 1024 | tf_op jit(solution)/shard_map/pallas_call | solution.py:309
  109.6 0.6 add_add_fusion
  (39 shorter events, 0.1 us)
Async XLA Ops:
  0.6 4.0 %copy-start = (bf16[1,128,1536]{2,1,0:T(8,128)(2,1)S(1)}, bf16[1,128,1536]{2,1,0:T(8,128)(2,1)}, u32[]{:S(2)}) copy-start(bf16[1,128,1536]{2,1,0:T(8,128)(2,1)} %param.16) | copy-start | bytes 1179652
  4.7 22.2 %copy-start.5 = (bf16[192,1536]{1,0:T(8,128)(2,1)S(1)}, bf16[192,1536]{1,0:T(8,128)(2,1)}, u32[]{:S(2)}) copy-start(bf16[192,1536]{1,0:T(8,128)(2,1)} %refs_2_.1) | copy-start | bytes 1769476
  4.7 27.8 %copy-start.1 = (bf16[1,128,1536]{2,1,0:T(8,128)(2,1)S(1)}, bf16[1,128,1536]{2,1,0:T(8,128)(2,1)}, u32[]{:S(2)}) copy-start(bf16[1,128,1536]{2,1,0:T(8,128)(2,1)} %param.10) | copy-start | bytes 1179652
  4.7 27.8 %copy-start.2 = (bf16[1,128,1536]{2,1,0:T(8,128)(2,1)S(1)}, bf16[1,128,1536]{2,1,0:T(8,128)(2,1)}, u32[]{:S(2)}) copy-start(bf16[1,128,1536]{2,1,0:T(8,128)(2,1)} %param.11) | copy-start | bytes 1179652
  4.7 27.8 %copy-start.6 = (bf16[1,128,1536]{2,1,0:T(8,128)(2,1)S(1)}, bf16[1,128,1536]{2,1,0:T(8,128)(2,1)}, u32[]{:S(2)}) copy-start(bf16[1,128,1536]{2,1,0:T(8,128)(2,1)} %param.9) | copy-start | bytes 1179652
  4.7 12.4 %collective-permute-start.5 = (bf16[128,1536]{1,0:T(8,128)(2,1)S(1)}, bf16[128,1536]{1,0:T(8,128)(2,1)S(1)}, u32[]{:S(2)}, u32[]{:S(2)}) collective-permute-start(bf16[128,1536]{1,0:T(8,128)(2,1)S(1)} %bitcast.20), channel_id=1, source_target_pairs={{3,0},{0,1},{1,2},{2,3},{7,4},{4,5},{5,6},{6,7},{11,8},{8,9},{9,10... | collective-permute-start | bytes 1179656 | tf_op jit(solution)/shard_map/ppermute | solution.py:53
  6.3 13.5 %collective-permute-start.4 = (bf16[128,1536]{1,0:T(8,128)(2,1)S(1)}, bf16[128,1536]{1,0:T(8,128)(2,1)S(1)}, u32[]{:S(2)}, u32[]{:S(2)}) collective-permute-start(bf16[128,1536]{1,0:T(8,128)(2,1)S(1)} %bitcast.21), channel_id=1, source_target_pairs={{2,0},{3,1},{0,2},{1,3},{6,4},{7,5},{4,6},{5,7},{10,8},{11,9},{8,1... | collective-permute-start | bytes 1179656 | tf_op jit(solution)/shard_map/ppermute | solution.py:53
  9.2 16.9 %collective-permute-start.3 = (bf16[128,1536]{1,0:T(8,128)(2,1)S(1)}, bf16[128,1536]{1,0:T(8,128)(2,1)S(1)}, u32[]{:S(2)}, u32[]{:S(2)}) collective-permute-start(bf16[128,1536]{1,0:T(8,128)(2,1)S(1)} %bitcast.22), channel_id=1, source_target_pairs={{1,0},{2,1},{3,2},{0,3},{5,4},{6,5},{7,6},{4,7},{9,8},{10,9},{11,1... | collective-permute-start | bytes 1179656 | tf_op jit(solution)/shard_map/ppermute | solution.py:53
  9.6 21.9 %collective-permute-start.1 = (bf16[272,1536]{1,0:T(8,128)(2,1)}, bf16[272,1536]{1,0:T(8,128)(2,1)}, u32[]{:S(2)}, u32[]{:S(2)}) collective-permute-start(bf16[272,1536]{1,0:T(8,128)(2,1)} %shard_map.128), channel_id=1, source_target_pairs={{0,248},{8,0},{16,8},{24,16},{32,24},{40,32},{48,40},{56,48},{64,5... | collective-permute-start | bytes 2506760 | tf_op jit(solution)/shard_map/ppermute | solution.py:41
  16.7 15.9 %collective-permute-start = (bf16[272,1536]{1,0:T(8,128)(2,1)}, bf16[272,1536]{1,0:T(8,128)(2,1)}, u32[]{:S(2)}, u32[]{:S(2)}) collective-permute-start(bf16[272,1536]{1,0:T(8,128)(2,1)} %shard_map.128), channel_id=1, source_target_pairs={{0,8},{8,16},{16,24},{24,32},{32,40},{40,48},{48,56},{56,64},{64,7... | collective-permute-start | bytes 2506760 | tf_op jit(solution)/shard_map/ppermute | solution.py:41
  26.8 13.2 %collective-permute-start.6 = (bf16[512,1536]{1,0:T(8,128)(2,1)S(1)}, bf16[512,1536]{1,0:T(8,128)(2,1)}, u32[]{:S(2)}, u32[]{:S(2)}) collective-permute-start(bf16[512,1536]{1,0:T(8,128)(2,1)S(1)} %shard_map.130.refs_4_.refs_2_), channel_id=1, source_target_pairs={{0,8},{8,0},{1,9},{9,1},{2,10},{10,2},{3,11},{11,3},{4,12},{12,4},... | collective-permute-start | bytes 4718600 | tf_op jit(solution)/shard_map/ppermute | solution.py:45
  26.9 13.1 %collective-permute-start.2 = (bf16[192,1536]{1,0:T(8,128)(2,1)S(1)}, bf16[192,1536]{1,0:T(8,128)(2,1)}, u32[]{:S(2)}, u32[]{:S(2)}) collective-permute-start(bf16[192,1536]{1,0:T(8,128)(2,1)S(1)} %copy-done.5), channel_id=1, source_target_pairs={{0,4},{12,8},{1,5},{13,9},{2,6},{14,10},{3,7},{15,11},{16,20},{28,... | collective-permute-start | bytes 1769480 | tf_op jit(solution)/shard_map/ppermute | solution.py:340
  31.4 42.3 %copy-start.3 = (s32[8]{0:T(128)}, s32[8]{0:T(128)S(1)}, u32[]{:S(2)}) copy-start(s32[8]{0:T(128)S(1)} %stack.23.refs_0_) | copy-start | bytes 100
  32.5 1.0 copy-start.7
  40.0 3.9 %copy-start.8 = (bf16[128,1536]{1,0:T(8,128)(2,1)}, bf16[128,1536]{1,0:T(8,128)(2,1)S(1)}, u32[]{:S(2)}) copy-start(bf16[128,1536]{1,0:T(8,128)(2,1)S(1)} %get-tuple-element.46.refs_1_) | copy-start | bytes 1179652
  40.0 3.9 %copy-start.11 = (f32[128,128]{1,0:T(8,128)}, f32[128,128]{1,0:T(8,128)S(1)}, u32[]{:S(2)}) copy-start(f32[128,128]{1,0:T(8,128)S(1)} %get-tuple-element.37.refs_2_) | copy-start | bytes 196612
  43.9 24.4 %copy-start.12 = (f32[128,128]{1,0:T(8,128)S(1)}, f32[128,128]{1,0:T(8,128)}, u32[]{:S(2)}) copy-start(f32[128,128]{1,0:T(8,128)} %copy-done.11) | copy-start | bytes 196612
  43.9 24.4 %all-to-all-start = ((bf16[8,384,128]{2,1,0:T(8,128)(2,1)}), bf16[8,384,128]{2,1,0:T(8,128)(2,1)S(1)}, u32[]{:S(2)}, u32[]{:S(2)}) async-start(bf16[8,384,128]{2,1,0:T(8,128)(2,1)} %get-tuple-element.34), calls=%async_computation | async-start | bytes 1572864 | tf_op jit(solution)/shard_map/all_to_all | solution.py:369
  48.9 13.8 %collective-permute-start.8 = (bf16[128,1536]{1,0:T(8,128)(2,1)S(1)}, bf16[128,1536]{1,0:T(8,128)(2,1)S(1)}, u32[]{:S(2)}, u32[]{:S(2)}) collective-permute-start(bf16[128,1536]{1,0:T(8,128)(2,1)S(1)} %bitcast.32), channel_id=1, source_target_pairs={{0,248},{8,0},{16,8},{24,16},{32,24},{40,32},{48,40},{56,48},{64,5... | collective-permute-start | bytes 1179656 | tf_op jit(solution)/shard_map/ppermute | solution.py:41
  57.4 10.9 %collective-permute-start.7 = (bf16[128,1536]{1,0:T(8,128)(2,1)S(1)}, bf16[128,1536]{1,0:T(8,128)(2,1)}, u32[]{:S(2)}, u32[]{:S(2)}) collective-permute-start(bf16[128,1536]{1,0:T(8,128)(2,1)S(1)} %bitcast.33), channel_id=1, source_target_pairs={{0,8},{8,16},{16,24},{24,32},{32,40},{40,48},{48,56},{56,64},{64,7... | collective-permute-start | bytes 1179656 | tf_op jit(solution)/shard_map/ppermute | solution.py:41
  57.4 22.9 %collective-permute-start.10 = (bf16[192,1536]{1,0:T(8,128)(2,1)S(1)}, bf16[192,1536]{1,0:T(8,128)(2,1)}, u32[]{:S(2)}, u32[]{:S(2)}) collective-permute-start(bf16[192,1536]{1,0:T(8,128)(2,1)S(1)} %get-tuple-element.47.refs_2_), channel_id=1, source_target_pairs={{3,0},{0,1},{1,2},{2,3},{7,4},{4,5},{5,6},{6,7},{11,8},{8,9},{9,10... | collective-permute-start | bytes 1769480 | tf_op jit(solution)/shard_map/ppermute | solution.py:53
  58.9 21.5 %collective-permute-start.9 = (bf16[192,1536]{1,0:T(8,128)(2,1)S(1)}, bf16[192,1536]{1,0:T(8,128)(2,1)}, u32[]{:S(2)}, u32[]{:S(2)}) collective-permute-start(bf16[192,1536]{1,0:T(8,128)(2,1)S(1)} %get-tuple-element.47.refs_2_), channel_id=1, source_target_pairs={{1,0},{2,1},{3,2},{0,3},{5,4},{6,5},{7,6},{4,7},{9,8},{10,9},{11,1... | collective-permute-start | bytes 1769480 | tf_op jit(solution)/shard_map/ppermute | solution.py:53
  62.8 0.8 copy-start.14
  68.3 1.0 copy-start.9
  70.6 6.2 %copy-start.13 = (f32[128,128]{1,0:T(8,128)}, f32[128,128]{1,0:T(8,128)S(1)}, u32[]{:S(2)}) copy-start(f32[128,128]{1,0:T(8,128)S(1)} %get-tuple-element.42.refs_1_) | copy-start | bytes 196612
  70.6 9.8 %collective-permute-start.12 = (bf16[144,1536]{1,0:T(8,128)(2,1)}, bf16[144,1536]{1,0:T(8,128)(2,1)}, u32[]{:S(2)}, u32[]{:S(2)}) collective-permute-start(bf16[144,1536]{1,0:T(8,128)(2,1)} %get-tuple-element.38.refs_7_), channel_id=1, source_target_pairs={{0,248},{8,0},{16,8},{24,16},{32,24},{40,32},{48,40},{56,48},{64,5... | collective-permute-start | bytes 1327112 | tf_op jit(solution)/shard_map/ppermute | solution.py:41
  72.2 11.7 %collective-permute-start.11 = (bf16[144,1536]{1,0:T(8,128)(2,1)}, bf16[144,1536]{1,0:T(8,128)(2,1)}, u32[]{:S(2)}, u32[]{:S(2)}) collective-permute-start(bf16[144,1536]{1,0:T(8,128)(2,1)} %get-tuple-element.38.refs_7_), channel_id=1, source_target_pairs={{0,8},{8,16},{16,24},{24,32},{32,40},{40,48},{48,56},{56,64},{64,7... | collective-permute-start | bytes 1327112 | tf_op jit(solution)/shard_map/ppermute | solution.py:41
  72.2 20.5 %collective-permute-start.13 = (bf16[192,1536]{1,0:T(8,128)(2,1)S(1)}, bf16[192,1536]{1,0:T(8,128)(2,1)}, u32[]{:S(2)}, u32[]{:S(2)}) collective-permute-start(bf16[192,1536]{1,0:T(8,128)(2,1)S(1)} %get-tuple-element.47.refs_2_), channel_id=1, source_target_pairs={{2,0},{3,1},{0,2},{1,3},{6,4},{7,5},{4,6},{5,7},{10,8},{11,9},{8,1... | collective-permute-start | bytes 1769480 | tf_op jit(solution)/shard_map/ppermute | solution.py:53
  76.8 23.8 %all-to-all-start.1 = ((bf16[8,24,1536]{2,1,0:T(8,128)(2,1)}), bf16[8,24,1536]{2,1,0:T(8,128)(2,1)S(1)}, u32[]{:S(2)}, u32[]{:S(2)}) async-start(bf16[8,24,1536]{2,1,0:T(8,128)(2,1)} %bitcast.12), calls=%async_computation.1 | async-start | bytes 1179648 | tf_op jit(solution)/shard_map/all_to_all | solution.py:389
  80.4 20.2 %copy-start.4 = (s32[8]{0:T(128)S(1)}, s32[8]{0:T(128)}, u32[]{:S(2)}) copy-start(s32[8]{0:T(128)} %copy-done.3) | copy-start | bytes 100
  92.8 13.3 %copy-start.10 = (bf16[128,1536]{1,0:T(8,128)(2,1)S(1)}, bf16[128,1536]{1,0:T(8,128)(2,1)}, u32[]{:S(2)}) copy-start(bf16[128,1536]{1,0:T(8,128)(2,1)} %copy-done.8) | copy-start | bytes 1179652
  92.8 8.7 %collective-permute-start.14 = (bf16[192,1536]{1,0:T(8,128)(2,1)S(1)}, bf16[192,1536]{1,0:T(8,128)(2,1)S(1)}, u32[]{:S(2)}, u32[]{:S(2)}) collective-permute-start(bf16[192,1536]{1,0:T(8,128)(2,1)S(1)} %get-tuple-element.47.refs_2_), channel_id=1, source_target_pairs={{0,8},{8,0},{1,9},{9,1},{2,10},{10,2},{3,11},{11,3},{4,12},{12,4},... | collective-permute-start | bytes 1769480 | tf_op jit(solution)/shard_map/ppermute | solution.py:45
  92.9 11.1 %collective-permute-start.15 = (bf16[192,1536]{1,0:T(8,128)(2,1)}, bf16[192,1536]{1,0:T(8,128)(2,1)S(1)}, u32[]{:S(2)}, u32[]{:S(2)}) collective-permute-start(bf16[192,1536]{1,0:T(8,128)(2,1)} %collective-permute-done.9.refs_3_), channel_id=1, source_target_pairs={{0,8},{8,0},{1,9},{9,1},{2,10},{10,2},{3,11},{11,3},{4,12},{12,4},... | collective-permute-start | bytes 1769480 | tf_op jit(solution)/shard_map/ppermute | solution.py:45
  93.4 12.7 %collective-permute-start.16 = (bf16[192,1536]{1,0:T(8,128)(2,1)}, bf16[192,1536]{1,0:T(8,128)(2,1)S(1)}, u32[]{:S(2)}, u32[]{:S(2)}) collective-permute-start(bf16[192,1536]{1,0:T(8,128)(2,1)} %collective-permute-done.13.refs_4_), channel_id=1, source_target_pairs={{0,8},{8,0},{1,9},{9,1},{2,10},{10,2},{3,11},{11,3},{4,12},{12,4},... | collective-permute-start | bytes 1769480 | tf_op jit(solution)/shard_map/ppermute | solution.py:45
  93.5 12.6 %collective-permute-start.17 = (bf16[192,1536]{1,0:T(8,128)(2,1)}, bf16[192,1536]{1,0:T(8,128)(2,1)}, u32[]{:S(2)}, u32[]{:S(2)}) collective-permute-start(bf16[192,1536]{1,0:T(8,128)(2,1)} %collective-permute-done.10.refs_5_), channel_id=1, source_target_pairs={{0,8},{8,0},{1,9},{9,1},{2,10},{10,2},{3,11},{11,3},{4,12},{12,4},... | collective-permute-start | bytes 1769480 | tf_op jit(solution)/shard_map/ppermute | solution.py:45
  101.3 8.3 %collective-permute-start.18 = (f32[6,1536]{1,0:T(8,128)S(1)}, f32[6,1536]{1,0:T(8,128)S(1)}, u32[]{:S(2)}, u32[]{:S(2)}) collective-permute-start(f32[6,1536]{1,0:T(8,128)S(1)} %get-tuple-element.54), channel_id=1, source_target_pairs={{0,4},{4,0},{16,20},{20,16},{1,5},{5,1},{17,21},{21,17},{2,6},{6,2... | collective-permute-start | bytes 110600 | tf_op jit(solution)/shard_map/ppermute | solution.py:414
  101.5 8.1 %collective-permute-start.19 = (f32[6,1536]{1,0:T(8,128)S(1)}, f32[6,1536]{1,0:T(8,128)S(1)}, u32[]{:S(2)}, u32[]{:S(2)}) collective-permute-start(f32[6,1536]{1,0:T(8,128)S(1)} %get-tuple-element.55), channel_id=1, source_target_pairs={{0,16},{4,20},{16,0},{20,4},{1,17},{5,21},{17,1},{21,5},{2,18},{6,... | collective-permute-start | bytes 110600 | tf_op jit(solution)/shard_map/ppermute | solution.py:414
  104.0 5.6 %collective-permute-start.20 = (f32[6,1536]{1,0:T(8,128)S(1)}, f32[6,1536]{1,0:T(8,128)S(1)}, u32[]{:S(2)}, u32[]{:S(2)}) collective-permute-start(f32[6,1536]{1,0:T(8,128)S(1)} %get-tuple-element.56), channel_id=1, source_target_pairs={{0,20},{4,16},{16,4},{20,0},{1,21},{5,17},{17,5},{21,1},{2,22},{6,... | collective-permute-start | bytes 110600 | tf_op jit(solution)/shard_map/ppermute | solution.py:414

commit v4 on v3

--- a/solution.py
+++ b/solution.py
@@ -252,9 +252,9 @@
 
 
 def backward_kernel(scalars, near, far, copies, outs, scratch):
-    dq, dk, dv = outs
     (info,), (stats,) = scalars, near
     q, k, v, left, right, ga, ql, qr, gal, gar = far
+    (dq, dk, dv), sems, leaving = scratch[:3], scratch[3], []
     st = stats[...]
     for h in range(HEADS):
         if h % (HEADS // CHUNKS) == 0:
@@ -287,9 +287,19 @@
         ds = (p * (dp - delta) * SCALE).astype(BF16)
         dk[:, c] = (dkh + dot(ds, queries)).astype(BF16)
         dv[:, c] = (dvh + dot(p.astype(BF16), grads)).astype(BF16)
-
-
-def call(kernel, micros, scalars, near, far, outs, scratch=(), mib=4, chunks=1):
+        if (h + 1) % (HEADS // CHUNKS) == 0:
+            chunk = h // (HEADS // CHUNKS)
+            cols = pl.ds(chunk * (HD // CHUNKS), HD // CHUNKS)
+            for n, (done, out) in enumerate(zip((dq, dk, dv), outs)):
+                leaving.append(
+                    pltpu.make_async_copy(done.at[:, cols], out.at[:, cols], sems.at[n, chunk])
+                )
+                leaving[-1].start()
+    for copy in leaving:
+        copy.wait()
+
+
+def call(kernel, micros, scalars, near, far, outs, scratch=(), mib=4, chunks=1, place_out=VMEM):
     counts = [len(scalars), len(near), len(far), len(outs), len(far), len(scratch)]
     ends = np.cumsum(counts)
 
@@ -311,10 +321,10 @@
         in_specs=[pl.BlockSpec(memory_space=pltpu.SMEM)] * len(scalars)
         + [pl.BlockSpec(memory_space=VMEM)] * len(near)
         + [pl.BlockSpec(memory_space=pltpu.HBM)] * len(far),
-        out_specs=[pl.BlockSpec(memory_space=VMEM)] * len(outs),
+        out_specs=[pl.BlockSpec(memory_space=place_out)] * len(outs),
         out_shape=[jax.ShapeDtypeStruct(s, d) for s, d in outs],
         scratch_shapes=[VMEM(f.shape, f.dtype) for f in far]
-        + [VMEM(s, d) for s, d in scratch]
+        + list(scratch)
         + [pltpu.SemaphoreType.DMA((max(1, len(far)), chunks))],
         cost_estimate=pl.CostEstimate(flops=int(micros * 1e9), bytes_accessed=1024, transcendentals=0),
         compiler_params=pltpu.CompilerParams(vmem_limit_bytes=mib * 1024 * 1024),
@@ -365,14 +375,14 @@
         (),
         [((GROUP, 2 * GROUP_ROWS, TILE), BF16), ((GROUP_ROWS, HD), BF16)],
     )
-    blocks = [w_block] + [along_x(w_block, step) for step in (1, 2, 3)]
+    blocks = [w_block, along_x(w_block, 1), None, along_x(w_block, 3)]
     mixed = lax.all_to_all(mixed, ("core", "x"), 0, 0, tiled=True)
 
     ga, stats = call(
         delta_kernel,
         1,
         (),
-        (after(mixed, ql, qr), att, stats),
+        (mixed, att, stats),
         (),
         [((TILE + EXTRA, HD), BF16), ((TILE, 128), F32)],
     )
@@ -382,11 +392,13 @@
         weight_kernel,
         2,
         (info,),
-        (after(mixed, ga), og_mine, og_other),
+        (after(mixed, ga, ql, qr), og_mine, og_other),
         (),
         [((GROUP_ROWS, HD), BF16)],
     )
     along_z = lax.all_to_all(partial.reshape(8, GROUP_ROWS // 8, HD), "z", 0, 0, tiled=True)
+
+    blocks[2] = along_x(after(w_block, partial), 2)
 
     dq, dk, dv = call(
         backward_kernel,
@@ -395,8 +407,10 @@
         (after(stats, partial, blocks[1], blocks[3]),),
         (q, k, v, left, right, ga, ql, qr, gal, gar),
         [(tile, BF16)] * 3,
+        scratch=[VMEM(tile, BF16)] * 3 + [pltpu.SemaphoreType.DMA((3, CHUNKS))],
         mib=56,
         chunks=CHUNKS,
+        place_out=pltpu.HBM,
     )
     blocks = blocks + [core_swap(after(w, dq)) for w in blocks]
 
@@ -420,7 +434,7 @@
         (after(att, pieces[0]), *blocks),
         (),
         [(tile, BF16)],
-        scratch=[((HD, TILE), BF16)],
+        scratch=[VMEM((HD, TILE), BF16)],
     )
     grad_weight = after(pieces[0], layer_out) + arrived[0] + arrived[1] + arrived[2]
     return layer_out[None], dq[None], dk[None], dv[None], grad_weight

time: 112 us -> 108 us (0.964)
  waiting for transfers between devices: 28.8 us -> 19.5 us
  starting transfers between devices: 44.5 us -> 51.2 us
    ppermute x6, starting transfers between devices: 17.2 us -> 25.2 us  [next_tile(): lax.ppermute(value, FRAME, [(i, (i + step) % TILES) for i in range(TILES)])]
    ppermute x6, waiting for transfers between devices: 12.7 us -> 5.88 us  [next_tile(): lax.ppermute(value, FRAME, [(i, (i + step) % TILES) for i in range(TILES)])]
    all_to_all x1, waiting for transfers between devices: 6.66 us -> 2.6 us  [shards(): lax.all_to_all(partial.reshape(8, GROUP_ROWS // 8, HD), 'z', 0, 0, tiled=...]
    unnamed x30 -> x28, local copies, waits for them, and re-layouts: 2.78 us -> 2.02 us
  transfers between devices with their start and end apart: 23 -> 23, of which waited for: 8 -> 8; matrix products, arithmetic and copies ran while one was open for 0% -> 0% of each run, Pallas kernels for 22% -> 23%
where the time goes in v4:
time: 108 us; the launch traced here: 107 us
  starting transfers between devices  51.2 us (47%)
  Pallas kernels  30.4 us (28%)
  waiting for transfers between devices  19.5 us (18%)
  between operations  2.94 us (3%)
  local copies, waits for them, and re-layouts  2.1 us (2%)
    pallas_call x7, Pallas kernels, call(): pl.pallas_call(body, in_specs=[pl.BlockSpec(memory_space=pltpu.SMEM)] * l...  27.6 us
    ppermute x6, starting transfers between devices, next_tile(): lax.ppermute(value, FRAME, [(i, (i + step) % TILES) for i in range(TILES)])  25.2 us
    ppermute x6, waiting for transfers between devices, along_x(): return lax.ppermute(value, 'x', [((i + step) % 4, i) for i in range(4)])  10.2 us
    ppermute x6, starting transfers between devices, along_x(): return lax.ppermute(value, 'x', [((i + step) % 4, i) for i in range(4)])  7.36 us
    ppermute x6, waiting for transfers between devices, next_tile(): lax.ppermute(value, FRAME, [(i, (i + step) % TILES) for i in range(TILES)])  5.88 us
    all_to_all x1, starting transfers between devices, shards(): mixed = lax.all_to_all(mixed, ('core', 'x'), 0, 0, tiled=True)  5.03 us
    ppermute x3, starting transfers between devices, shards(): arrived.append(lax.ppermute(pieces[step], ('yhi', 'ylo'), pairs))  4.78 us
    ppermute x1, starting transfers between devices, shards(): w_passed = lax.ppermute(out_weight, ('core', 'ylo'), [(0, 1), (3, 2)])  4.4 us
  transfers between devices with their start and end apart: 23, of which 8 were waited for; matrix products, arithmetic and copies ran while one was open for 0% of the time, Pallas kernels for 23%

profile of v4, /device:TPU:2, one launch (start us, length us, event | category | flops | bytes accessed | tf_op | source)
XLA Modules:
  0.0 106.8 jit_solution(10017307139024268174)
XLA Ops:
  2.6 2.0 %shard_map.128 = bf16[272,1536]{1,0:T(8,128)(2,1)} custom-call(s32[1,1]{1,0:T(1,128)} %copy.14.frame, s32[1,1]{1,0:T(1,128)} %copy.15.back, s32[1,1]{1,0:T(1,128)} %copy.16.ahead, bf16[128,1536]{1,0:T(8,128)(2,1)} %bitcast.24, bf16[128,1536]{1,0:T(8,128)(2,1)} %bitcast.27), custom_call_target="tpu_custom_call" | custom-call | tf_op jit(solution)/shard_map/pallas_call | solution.py:112
  4.7 0.0 copy-start.5
  4.7 0.0 copy-start.1
  4.7 0.0 copy-start.2
  4.7 0.0 copy-start.6
  4.7 1.6 %collective-permute-start.5 = (bf16[128,1536]{1,0:T(8,128)(2,1)S(1)}, bf16[128,1536]{1,0:T(8,128)(2,1)S(1)}, u32[]{:S(2)}, u32[]{:S(2)}) collective-permute-start(bf16[128,1536]{1,0:T(8,128)(2,1)S(1)} %bitcast.20), channel_id=1, source_target_pairs={{3,0},{0,1},{1,2},{2,3},{7,4},{4,5},{5,6},{6,7},{11,8},{8,9},{9,10... | collective-permute-start | bytes 1179656 | tf_op jit(solution)/shard_map/ppermute | solution.py:53
  6.3 2.8 %collective-permute-start.4 = (bf16[128,1536]{1,0:T(8,128)(2,1)S(1)}, bf16[128,1536]{1,0:T(8,128)(2,1)S(1)}, u32[]{:S(2)}, u32[]{:S(2)}) collective-permute-start(bf16[128,1536]{1,0:T(8,128)(2,1)S(1)} %bitcast.21), channel_id=1, source_target_pairs={{2,0},{3,1},{0,2},{1,3},{6,4},{7,5},{4,6},{5,7},{10,8},{11,9},{8,1... | collective-permute-start | bytes 1179656 | tf_op jit(solution)/shard_map/ppermute | solution.py:53
  9.2 0.4 collective-permute-start.3
  9.6 7.1 %collective-permute-start.1 = (bf16[272,1536]{1,0:T(8,128)(2,1)}, bf16[272,1536]{1,0:T(8,128)(2,1)}, u32[]{:S(2)}, u32[]{:S(2)}) collective-permute-start(bf16[272,1536]{1,0:T(8,128)(2,1)} %shard_map.128), channel_id=1, source_target_pairs={{0,248},{8,0},{16,8},{24,16},{32,24},{40,32},{48,40},{56,48},{64,5... | collective-permute-start | bytes 2506760 | tf_op jit(solution)/shard_map/ppermute | solution.py:41
  16.7 0.4 collective-permute-done.5.refs_3_
  17.1 2.8 %collective-permute-done.4.refs_2_ = bf16[128,1536]{1,0:T(8,128)(2,1)S(1)} collective-permute-done((bf16[128,1536]{1,0:T(8,128)(2,1)S(1)}, bf16[128,1536]{1,0:T(8,128)(2,1)S(1)}, u32[]{:S(2)}, u32[]{:S(2)}) %collective-permute-start.4) | collective-permute-done | bytes 393248 | tf_op jit(solution)/shard_map/ppermute | solution.py:53
  19.9 6.2 %collective-permute-done.3.refs_1_ = bf16[128,1536]{1,0:T(8,128)(2,1)S(1)} collective-permute-done((bf16[128,1536]{1,0:T(8,128)(2,1)S(1)}, bf16[128,1536]{1,0:T(8,128)(2,1)S(1)}, u32[]{:S(2)}, u32[]{:S(2)}) %collective-permute-start.3) | collective-permute-done | bytes 393248 | tf_op jit(solution)/shard_map/ppermute | solution.py:53
  26.0 0.8 shard_map.130.refs_4_.refs_2_
  26.8 0.1 collective-permute-start.6
  26.9 4.4 %collective-permute-start.2 = (bf16[192,1536]{1,0:T(8,128)(2,1)S(1)}, bf16[192,1536]{1,0:T(8,128)(2,1)}, u32[]{:S(2)}, u32[]{:S(2)}) collective-permute-start(bf16[192,1536]{1,0:T(8,128)(2,1)S(1)} %copy-done.5), channel_id=1, source_target_pairs={{0,4},{12,8},{1,5},{13,9},{2,6},{14,10},{3,7},{15,11},{16,20},{28,... | collective-permute-start | bytes 1769480 | tf_op jit(solution)/shard_map/ppermute | solution.py:350
  31.3 0.1 stack.23.refs_0_
  31.4 1.1 %collective-permute-done.refs_4_.refs_5_ = bf16[272,1536]{1,0:T(8,128)(2,1)} collective-permute-done((bf16[272,1536]{1,0:T(8,128)(2,1)}, bf16[272,1536]{1,0:T(8,128)(2,1)}, u32[]{:S(2)}, u32[]{:S(2)}) %collective-permute-start) | collective-permute-done | bytes 835616 | tf_op jit(solution)/shard_map/ppermute | solution.py:41
  32.5 0.0 copy-start.7
  32.6 1.0 copy-done.7
  33.5 6.5 %shard_map.129 = (bf16[128,1536]{1,0:T(8,128)(2,1)S(1)}, bf16[8,192,128]{2,1,0:T(8,128)(2,1)S(1)}, f32[128,128]{1,0:T(8,128)S(1)}) custom-call(s32[8]{0:T(128)S(1)} %stack.23.refs_0_, bf16[128,1536]{1,0:T(8,128)(2,1)S(1)} %bitcast.31, bf16[128,1536]{1,0:T(8,128)(2,1)S(1)} %bitcast.26, bf16[128,1536]{1,0:T(8,128)(2,1)S(1)} %bitcast.29, ...), custom_call_target="tpu_custom_call" | custom-call | flops 8000000000 | bytes 1024 | tf_op jit(solution)/shard_map/pallas_call | solution.py:319
  40.0 0.0 copy-start.8
  40.0 0.0 copy-start.12
  40.0 3.8 %shard_map.131 = (bf16[8,384,128]{2,1,0:T(8,128)(2,1)}, bf16[192,1536]{1,0:T(8,128)(2,1)S(1)}) custom-call(s32[8]{0:T(128)S(1)} %stack.23.refs_0_, bf16[8,192,128]{2,1,0:T(8,128)(2,1)S(1)} %get-tuple-element.32.refs_1_, bf16[192,1536]{1,0:T(8,128)(2,1)S(1)} %copy-done.5, bf16[192,1536]{1,0:T(8,128)(2,1)} %collective-permute-done.2.refs_3_, ...), custom_call_target="tpu_custom_call" | custom-call | flops 2000000000 | bytes 1024 | tf_op jit(solution)/shard_map/pallas_call | solution.py:319
  43.9 0.0 copy-start.13
  43.9 5.0 %all-to-all-start = ((bf16[8,384,128]{2,1,0:T(8,128)(2,1)}), bf16[8,384,128]{2,1,0:T(8,128)(2,1)S(1)}, u32[]{:S(2)}, u32[]{:S(2)}) async-start(bf16[8,384,128]{2,1,0:T(8,128)(2,1)} %get-tuple-element.34), calls=%async_computation | async-start | bytes 1572864 | tf_op jit(solution)/shard_map/all_to_all | solution.py:379
  48.9 8.5 %collective-permute-start.8 = (bf16[128,1536]{1,0:T(8,128)(2,1)S(1)}, bf16[128,1536]{1,0:T(8,128)(2,1)}, u32[]{:S(2)}, u32[]{:S(2)}) collective-permute-start(bf16[128,1536]{1,0:T(8,128)(2,1)S(1)} %bitcast.32), channel_id=1, source_target_pairs={{0,248},{8,0},{16,8},{24,16},{32,24},{40,32},{48,40},{56,48},{64,5... | collective-permute-start | bytes 1179656 | tf_op jit(solution)/shard_map/ppermute | solution.py:41
  57.4 1.5 %collective-permute-start.10 = (bf16[192,1536]{1,0:T(8,128)(2,1)S(1)}, bf16[192,1536]{1,0:T(8,128)(2,1)}, u32[]{:S(2)}, u32[]{:S(2)}) collective-permute-start(bf16[192,1536]{1,0:T(8,128)(2,1)S(1)} %get-tuple-element.47.refs_2_), channel_id=1, source_target_pairs={{3,0},{0,1},{1,2},{2,3},{7,4},{4,5},{5,6},{6,7},{11,8},{8,9},{9,10... | collective-permute-start | bytes 1769480 | tf_op jit(solution)/shard_map/ppermute | solution.py:53
  58.9 0.6 collective-permute-start.9
  59.4 0.8 all-to-all-done.refs_0_.refs_1_
  60.3 1.0 copy-done.9
  61.3 1.3 %shard_map.132 = (bf16[144,1536]{1,0:T(8,128)(2,1)}, f32[128,128]{1,0:T(8,128)S(1)}) custom-call(bf16[8,384,128]{2,1,0:T(8,128)(2,1)S(1)} %all-to-all-done.refs_0_.refs_1_, bf16[128,1536]{1,0:T(8,128)(2,1)S(1)} %copy-done.9, f32[128,128]{1,0:T(8,128)S(1)} %copy-done.13), custom_call_target="tpu_custom_call" | custom-call | flops 1000000000 | bytes 1024 | tf_op jit(solution)/shard_map/pallas_call | solution.py:319
  62.5 9.7 %collective-permute-start.12 = (bf16[144,1536]{1,0:T(8,128)(2,1)}, bf16[144,1536]{1,0:T(8,128)(2,1)}, u32[]{:S(2)}, u32[]{:S(2)}) collective-permute-start(bf16[144,1536]{1,0:T(8,128)(2,1)} %get-tuple-element.36.refs_7_), channel_id=1, source_target_pairs={{0,248},{8,0},{16,8},{24,16},{32,24},{40,32},{48,40},{56,48},{64,5... | collective-permute-start | bytes 1327112 | tf_op jit(solution)/shard_map/ppermute | solution.py:41
  72.2 3.1 %shard_map.133 = bf16[192,1536]{1,0:T(8,128)(2,1)} custom-call(s32[8]{0:T(128)S(1)} %stack.23.refs_0_, bf16[8,384,128]{2,1,0:T(8,128)(2,1)S(1)} %all-to-all-done.refs_0_.refs_1_, bf16[512,1536]{1,0:T(8,128)(2,1)S(1)} %shard_map.130.refs_4_.refs_2_, bf16[512,1536]{1,0:T(8,128)(2,1)} %collective-permute-done.6.refs_5_.refs_3_), custom_call_target="tpu_custom_call" | custom-call | flops 2000000000 | bytes 1024 | tf_op jit(solution)/shard_map/pallas_call | solution.py:319
  75.3 3.5 %all-to-all-start.1 = ((bf16[8,24,1536]{2,1,0:T(8,128)(2,1)}), bf16[8,24,1536]{2,1,0:T(8,128)(2,1)S(1)}, u32[]{:S(2)}, u32[]{:S(2)}) async-start(bf16[8,24,1536]{2,1,0:T(8,128)(2,1)} %bitcast.12), calls=%async_computation.1 | async-start | bytes 1179648 | tf_op jit(solution)/shard_map/all_to_all | solution.py:399
  78.9 0.5 collective-permute-start.13
  79.4 4.8 %collective-permute-done.11.refs_10_ = bf16[144,1536]{1,0:T(8,128)(2,1)} collective-permute-done((bf16[144,1536]{1,0:T(8,128)(2,1)}, bf16[144,1536]{1,0:T(8,128)(2,1)}, u32[]{:S(2)}, u32[]{:S(2)}) %collective-permute-start.11) | collective-permute-done | bytes 442400 | tf_op jit(solution)/shard_map/ppermute | solution.py:41
  84.2 8.8 %shard_map.134 = (bf16[128,1536]{1,0:T(8,128)(2,1)}, bf16[128,1536]{1,0:T(8,128)(2,1)}, bf16[128,1536]{1,0:T(8,128)(2,1)}) custom-call(s32[8]{0:T(128)} %copy-done.3, f32[128,128]{1,0:T(8,128)} %copy-done.11, bf16[128,1536]{1,0:T(8,128)(2,1)} %bitcast.30, bf16[128,1536]{1,0:T(8,128)(2,1)} %bitcast.25, bf16[128,1536]{1,0:T(8,128)(2,1)} %bitcast.28, ...), custom_call_target="tpu_custom_call" | custom-call | flops 8999999488 | bytes 1024 | tf_op jit(solution)/shard_map/pallas_call | solution.py:319
  92.9 0.0 copy-start.10
  93.0 0.1 collective-permute-start.14
  93.1 0.5 collective-permute-start.15
  93.6 0.1 collective-permute-start.17
  93.7 0.8 collective-permute-done.13.refs_4_
  94.5 2.6 %all-to-all-done.1.refs_1_ = bf16[8,24,1536]{2,1,0:T(8,128)(2,1)S(1)} async-done(((bf16[8,24,1536]{2,1,0:T(8,128)(2,1)}), bf16[8,24,1536]{2,1,0:T(8,128)(2,1)S(1)}, u32[]{:S(2)}, u32[]{:S(2)}) %all-to-all-start.1) | async-done | bytes 589856 | tf_op jit(solution)/shard_map/all_to_all | solution.py:399
  97.1 0.7 shard_map.135
  97.8 1.0 collective-permute-start.18
  98.7 3.8 %collective-permute-start.20 = (f32[6,1536]{1,0:T(8,128)S(1)}, f32[6,1536]{1,0:T(8,128)S(1)}, u32[]{:S(2)}, u32[]{:S(2)}) collective-permute-start(f32[6,1536]{1,0:T(8,128)S(1)} %get-tuple-element.56), channel_id=1, source_target_pairs={{0,20},{4,16},{16,4},{20,0},{1,21},{5,17},{17,5},{21,1},{2,22},{6,... | collective-permute-start | bytes 110600 | tf_op jit(solution)/shard_map/ppermute | solution.py:428
  102.6 3.5 %shard_map.136 = bf16[128,1536]{1,0:T(8,128)(2,1)} custom-call(s32[8]{0:T(128)S(1)} %copy-done.4, bf16[128,1536]{1,0:T(8,128)(2,1)S(1)} %copy-done.10, bf16[192,1536]{1,0:T(8,128)(2,1)S(1)} %get-tuple-element.47.refs_2_, bf16[192,1536]{1,0:T(8,128)(2,1)} %collective-permute-done.9.refs_3_, bf16[192,1536]{1,0:T(8,128)(2,1)S(1)} %collective-permute-done.13.refs_4_, ...), custom_call_target="tpu_custom_call" | custom-call | flops 4000000000 | bytes 1024 | tf_op jit(solution)/shard_map/pallas_call | solution.py:319
  106.1 0.6 add_add_fusion
  (37 shorter events, 0.1 us)
Async XLA Ops:
  0.6 4.0 %copy-start = (bf16[1,128,1536]{2,1,0:T(8,128)(2,1)S(1)}, bf16[1,128,1536]{2,1,0:T(8,128)(2,1)}, u32[]{:S(2)}) copy-start(bf16[1,128,1536]{2,1,0:T(8,128)(2,1)} %param.16) | copy-start | bytes 1179652
  4.7 22.2 %copy-start.5 = (bf16[192,1536]{1,0:T(8,128)(2,1)S(1)}, bf16[192,1536]{1,0:T(8,128)(2,1)}, u32[]{:S(2)}) copy-start(bf16[192,1536]{1,0:T(8,128)(2,1)} %refs_2_.1) | copy-start | bytes 1769476
  4.7 27.8 %copy-start.1 = (bf16[1,128,1536]{2,1,0:T(8,128)(2,1)S(1)}, bf16[1,128,1536]{2,1,0:T(8,128)(2,1)}, u32[]{:S(2)}) copy-start(bf16[1,128,1536]{2,1,0:T(8,128)(2,1)} %param.10) | copy-start | bytes 1179652
  4.7 27.8 %copy-start.2 = (bf16[1,128,1536]{2,1,0:T(8,128)(2,1)S(1)}, bf16[1,128,1536]{2,1,0:T(8,128)(2,1)}, u32[]{:S(2)}) copy-start(bf16[1,128,1536]{2,1,0:T(8,128)(2,1)} %param.11) | copy-start | bytes 1179652
  4.7 27.8 %copy-start.6 = (bf16[1,128,1536]{2,1,0:T(8,128)(2,1)S(1)}, bf16[1,128,1536]{2,1,0:T(8,128)(2,1)}, u32[]{:S(2)}) copy-start(bf16[1,128,1536]{2,1,0:T(8,128)(2,1)} %param.9) | copy-start | bytes 1179652
  4.7 12.4 %collective-permute-start.5 = (bf16[128,1536]{1,0:T(8,128)(2,1)S(1)}, bf16[128,1536]{1,0:T(8,128)(2,1)S(1)}, u32[]{:S(2)}, u32[]{:S(2)}) collective-permute-start(bf16[128,1536]{1,0:T(8,128)(2,1)S(1)} %bitcast.20), channel_id=1, source_target_pairs={{3,0},{0,1},{1,2},{2,3},{7,4},{4,5},{5,6},{6,7},{11,8},{8,9},{9,10... | collective-permute-start | bytes 1179656 | tf_op jit(solution)/shard_map/ppermute | solution.py:53
  6.3 13.5 %collective-permute-start.4 = (bf16[128,1536]{1,0:T(8,128)(2,1)S(1)}, bf16[128,1536]{1,0:T(8,128)(2,1)S(1)}, u32[]{:S(2)}, u32[]{:S(2)}) collective-permute-start(bf16[128,1536]{1,0:T(8,128)(2,1)S(1)} %bitcast.21), channel_id=1, source_target_pairs={{2,0},{3,1},{0,2},{1,3},{6,4},{7,5},{4,6},{5,7},{10,8},{11,9},{8,1... | collective-permute-start | bytes 1179656 | tf_op jit(solution)/shard_map/ppermute | solution.py:53
  9.2 16.9 %collective-permute-start.3 = (bf16[128,1536]{1,0:T(8,128)(2,1)S(1)}, bf16[128,1536]{1,0:T(8,128)(2,1)S(1)}, u32[]{:S(2)}, u32[]{:S(2)}) collective-permute-start(bf16[128,1536]{1,0:T(8,128)(2,1)S(1)} %bitcast.22), channel_id=1, source_target_pairs={{1,0},{2,1},{3,2},{0,3},{5,4},{6,5},{7,6},{4,7},{9,8},{10,9},{11,1... | collective-permute-start | bytes 1179656 | tf_op jit(solution)/shard_map/ppermute | solution.py:53
  9.6 21.9 %collective-permute-start.1 = (bf16[272,1536]{1,0:T(8,128)(2,1)}, bf16[272,1536]{1,0:T(8,128)(2,1)}, u32[]{:S(2)}, u32[]{:S(2)}) collective-permute-start(bf16[272,1536]{1,0:T(8,128)(2,1)} %shard_map.128), channel_id=1, source_target_pairs={{0,248},{8,0},{16,8},{24,16},{32,24},{40,32},{48,40},{56,48},{64,5... | collective-permute-start | bytes 2506760 | tf_op jit(solution)/shard_map/ppermute | solution.py:41
  16.7 15.9 %collective-permute-start = (bf16[272,1536]{1,0:T(8,128)(2,1)}, bf16[272,1536]{1,0:T(8,128)(2,1)}, u32[]{:S(2)}, u32[]{:S(2)}) collective-permute-start(bf16[272,1536]{1,0:T(8,128)(2,1)} %shard_map.128), channel_id=1, source_target_pairs={{0,8},{8,16},{16,24},{24,32},{32,40},{40,48},{48,56},{56,64},{64,7... | collective-permute-start | bytes 2506760 | tf_op jit(solution)/shard_map/ppermute | solution.py:41
  26.8 13.2 %collective-permute-start.6 = (bf16[512,1536]{1,0:T(8,128)(2,1)S(1)}, bf16[512,1536]{1,0:T(8,128)(2,1)}, u32[]{:S(2)}, u32[]{:S(2)}) collective-permute-start(bf16[512,1536]{1,0:T(8,128)(2,1)S(1)} %shard_map.130.refs_4_.refs_2_), channel_id=1, source_target_pairs={{0,8},{8,0},{1,9},{9,1},{2,10},{10,2},{3,11},{11,3},{4,12},{12,4},... | collective-permute-start | bytes 4718600 | tf_op jit(solution)/shard_map/ppermute | solution.py:45
  26.9 13.1 %collective-permute-start.2 = (bf16[192,1536]{1,0:T(8,128)(2,1)S(1)}, bf16[192,1536]{1,0:T(8,128)(2,1)}, u32[]{:S(2)}, u32[]{:S(2)}) collective-permute-start(bf16[192,1536]{1,0:T(8,128)(2,1)S(1)} %copy-done.5), channel_id=1, source_target_pairs={{0,4},{12,8},{1,5},{13,9},{2,6},{14,10},{3,7},{15,11},{16,20},{28,... | collective-permute-start | bytes 1769480 | tf_op jit(solution)/shard_map/ppermute | solution.py:350
  31.4 40.8 %copy-start.3 = (s32[8]{0:T(128)}, s32[8]{0:T(128)S(1)}, u32[]{:S(2)}) copy-start(s32[8]{0:T(128)S(1)} %stack.23.refs_0_) | copy-start | bytes 100
  32.5 1.0 copy-start.7
  40.0 3.9 %copy-start.8 = (bf16[128,1536]{1,0:T(8,128)(2,1)}, bf16[128,1536]{1,0:T(8,128)(2,1)S(1)}, u32[]{:S(2)}) copy-start(bf16[128,1536]{1,0:T(8,128)(2,1)S(1)} %get-tuple-element.45.refs_1_) | copy-start | bytes 1179652
  40.0 3.9 %copy-start.12 = (f32[128,128]{1,0:T(8,128)}, f32[128,128]{1,0:T(8,128)S(1)}, u32[]{:S(2)}) copy-start(f32[128,128]{1,0:T(8,128)S(1)} %get-tuple-element.35.refs_2_) | copy-start | bytes 196612
  43.9 16.4 %copy-start.13 = (f32[128,128]{1,0:T(8,128)S(1)}, f32[128,128]{1,0:T(8,128)}, u32[]{:S(2)}) copy-start(f32[128,128]{1,0:T(8,128)} %copy-done.12) | copy-start | bytes 196612
  43.9 16.4 %all-to-all-start = ((bf16[8,384,128]{2,1,0:T(8,128)(2,1)}), bf16[8,384,128]{2,1,0:T(8,128)(2,1)S(1)}, u32[]{:S(2)}, u32[]{:S(2)}) async-start(bf16[8,384,128]{2,1,0:T(8,128)(2,1)} %get-tuple-element.34), calls=%async_computation | async-start | bytes 1572864 | tf_op jit(solution)/shard_map/all_to_all | solution.py:379
  48.9 23.3 %collective-permute-start.8 = (bf16[128,1536]{1,0:T(8,128)(2,1)S(1)}, bf16[128,1536]{1,0:T(8,128)(2,1)}, u32[]{:S(2)}, u32[]{:S(2)}) collective-permute-start(bf16[128,1536]{1,0:T(8,128)(2,1)S(1)} %bitcast.32), channel_id=1, source_target_pairs={{0,248},{8,0},{16,8},{24,16},{32,24},{40,32},{48,40},{56,48},{64,5... | collective-permute-start | bytes 1179656 | tf_op jit(solution)/shard_map/ppermute | solution.py:41
  57.4 22.0 %collective-permute-start.10 = (bf16[192,1536]{1,0:T(8,128)(2,1)S(1)}, bf16[192,1536]{1,0:T(8,128)(2,1)}, u32[]{:S(2)}, u32[]{:S(2)}) collective-permute-start(bf16[192,1536]{1,0:T(8,128)(2,1)S(1)} %get-tuple-element.47.refs_2_), channel_id=1, source_target_pairs={{3,0},{0,1},{1,2},{2,3},{7,4},{4,5},{5,6},{6,7},{11,8},{8,9},{9,10... | collective-permute-start | bytes 1769480 | tf_op jit(solution)/shard_map/ppermute | solution.py:53
  58.9 20.5 %collective-permute-start.9 = (bf16[192,1536]{1,0:T(8,128)(2,1)S(1)}, bf16[192,1536]{1,0:T(8,128)(2,1)}, u32[]{:S(2)}, u32[]{:S(2)}) collective-permute-start(bf16[192,1536]{1,0:T(8,128)(2,1)S(1)} %get-tuple-element.47.refs_2_), channel_id=1, source_target_pairs={{1,0},{2,1},{3,2},{0,3},{5,4},{6,5},{7,6},{4,7},{9,8},{10,9},{11,1... | collective-permute-start | bytes 1769480 | tf_op jit(solution)/shard_map/ppermute | solution.py:53
  59.4 12.8 %collective-permute-start.7 = (bf16[128,1536]{1,0:T(8,128)(2,1)S(1)}, bf16[128,1536]{1,0:T(8,128)(2,1)}, u32[]{:S(2)}, u32[]{:S(2)}) collective-permute-start(bf16[128,1536]{1,0:T(8,128)(2,1)S(1)} %bitcast.33), channel_id=1, source_target_pairs={{0,8},{8,16},{16,24},{24,32},{32,40},{40,48},{48,56},{56,64},{64,7... | collective-permute-start | bytes 1179656 | tf_op jit(solution)/shard_map/ppermute | solution.py:41
  60.3 1.0 copy-start.9
  62.5 12.8 %copy-start.11 = (f32[128,128]{1,0:T(8,128)}, f32[128,128]{1,0:T(8,128)S(1)}, u32[]{:S(2)}) copy-start(f32[128,128]{1,0:T(8,128)S(1)} %get-tuple-element.41.refs_1_) | copy-start | bytes 196612
  62.5 16.9 %collective-permute-start.12 = (bf16[144,1536]{1,0:T(8,128)(2,1)}, bf16[144,1536]{1,0:T(8,128)(2,1)}, u32[]{:S(2)}, u32[]{:S(2)}) collective-permute-start(bf16[144,1536]{1,0:T(8,128)(2,1)} %get-tuple-element.36.refs_7_), channel_id=1, source_target_pairs={{0,248},{8,0},{16,8},{24,16},{32,24},{40,32},{48,40},{56,48},{64,5... | collective-permute-start | bytes 1327112 | tf_op jit(solution)/shard_map/ppermute | solution.py:41
  72.2 12.0 %collective-permute-start.11 = (bf16[144,1536]{1,0:T(8,128)(2,1)}, bf16[144,1536]{1,0:T(8,128)(2,1)}, u32[]{:S(2)}, u32[]{:S(2)}) collective-permute-start(bf16[144,1536]{1,0:T(8,128)(2,1)} %get-tuple-element.36.refs_7_), channel_id=1, source_target_pairs={{0,8},{8,16},{16,24},{24,32},{32,40},{40,48},{48,56},{56,64},{64,7... | collective-permute-start | bytes 1327112 | tf_op jit(solution)/shard_map/ppermute | solution.py:41
  75.3 21.7 %all-to-all-start.1 = ((bf16[8,24,1536]{2,1,0:T(8,128)(2,1)}), bf16[8,24,1536]{2,1,0:T(8,128)(2,1)S(1)}, u32[]{:S(2)}, u32[]{:S(2)}) async-start(bf16[8,24,1536]{2,1,0:T(8,128)(2,1)} %bitcast.12), calls=%async_computation.1 | async-start | bytes 1179648 | tf_op jit(solution)/shard_map/all_to_all | solution.py:399
  78.9 15.6 %collective-permute-start.13 = (bf16[192,1536]{1,0:T(8,128)(2,1)S(1)}, bf16[192,1536]{1,0:T(8,128)(2,1)S(1)}, u32[]{:S(2)}, u32[]{:S(2)}) collective-permute-start(bf16[192,1536]{1,0:T(8,128)(2,1)S(1)} %get-tuple-element.47.refs_2_), channel_id=1, source_target_pairs={{2,0},{3,1},{0,2},{1,3},{6,4},{7,5},{4,6},{5,7},{10,8},{11,9},{8,1... | collective-permute-start | bytes 1769480 | tf_op jit(solution)/shard_map/ppermute | solution.py:53
  79.4 17.7 %copy-start.4 = (s32[8]{0:T(128)S(1)}, s32[8]{0:T(128)}, u32[]{:S(2)}) copy-start(s32[8]{0:T(128)} %copy-done.3) | copy-start | bytes 100
  92.9 9.6 %copy-start.10 = (bf16[128,1536]{1,0:T(8,128)(2,1)S(1)}, bf16[128,1536]{1,0:T(8,128)(2,1)}, u32[]{:S(2)}) copy-start(bf16[128,1536]{1,0:T(8,128)(2,1)} %copy-done.8) | copy-start | bytes 1179652
  93.0 5.8 %collective-permute-start.14 = (bf16[192,1536]{1,0:T(8,128)(2,1)S(1)}, bf16[192,1536]{1,0:T(8,128)(2,1)S(1)}, u32[]{:S(2)}, u32[]{:S(2)}) collective-permute-start(bf16[192,1536]{1,0:T(8,128)(2,1)S(1)} %get-tuple-element.47.refs_2_), channel_id=1, source_target_pairs={{0,8},{8,0},{1,9},{9,1},{2,10},{10,2},{3,11},{11,3},{4,12},{12,4},... | collective-permute-start | bytes 1769480 | tf_op jit(solution)/shard_map/ppermute | solution.py:45
  93.1 5.7 %collective-permute-start.15 = (bf16[192,1536]{1,0:T(8,128)(2,1)}, bf16[192,1536]{1,0:T(8,128)(2,1)S(1)}, u32[]{:S(2)}, u32[]{:S(2)}) collective-permute-start(bf16[192,1536]{1,0:T(8,128)(2,1)} %collective-permute-done.9.refs_3_), channel_id=1, source_target_pairs={{0,8},{8,0},{1,9},{9,1},{2,10},{10,2},{3,11},{11,3},{4,12},{12,4},... | collective-permute-start | bytes 1769480 | tf_op jit(solution)/shard_map/ppermute | solution.py:45
  93.6 9.0 %collective-permute-start.17 = (bf16[192,1536]{1,0:T(8,128)(2,1)}, bf16[192,1536]{1,0:T(8,128)(2,1)}, u32[]{:S(2)}, u32[]{:S(2)}) collective-permute-start(bf16[192,1536]{1,0:T(8,128)(2,1)} %collective-permute-done.10.refs_5_), channel_id=1, source_target_pairs={{0,8},{8,0},{1,9},{9,1},{2,10},{10,2},{3,11},{11,3},{4,12},{12,4},... | collective-permute-start | bytes 1769480 | tf_op jit(solution)/shard_map/ppermute | solution.py:45
  94.5 8.1 %collective-permute-start.16 = (bf16[192,1536]{1,0:T(8,128)(2,1)S(1)}, bf16[192,1536]{1,0:T(8,128)(2,1)}, u32[]{:S(2)}, u32[]{:S(2)}) collective-permute-start(bf16[192,1536]{1,0:T(8,128)(2,1)S(1)} %collective-permute-done.13.refs_4_), channel_id=1, source_target_pairs={{0,8},{8,0},{1,9},{9,1},{2,10},{10,2},{3,11},{11,3},{4,12},{12,4},... | collective-permute-start | bytes 1769480 | tf_op jit(solution)/shard_map/ppermute | solution.py:45
  97.8 8.4 %collective-permute-start.18 = (f32[6,1536]{1,0:T(8,128)S(1)}, f32[6,1536]{1,0:T(8,128)S(1)}, u32[]{:S(2)}, u32[]{:S(2)}) collective-permute-start(f32[6,1536]{1,0:T(8,128)S(1)} %get-tuple-element.54), channel_id=1, source_target_pairs={{0,4},{4,0},{16,20},{20,16},{1,5},{5,1},{17,21},{21,17},{2,6},{6,2... | collective-permute-start | bytes 110600 | tf_op jit(solution)/shard_map/ppermute | solution.py:428
  98.7 7.4 %collective-permute-start.19 = (f32[6,1536]{1,0:T(8,128)S(1)}, f32[6,1536]{1,0:T(8,128)S(1)}, u32[]{:S(2)}, u32[]{:S(2)}) collective-permute-start(f32[6,1536]{1,0:T(8,128)S(1)} %get-tuple-element.55), channel_id=1, source_target_pairs={{0,16},{4,20},{16,0},{20,4},{1,17},{5,21},{17,1},{21,5},{2,18},{6,... | collective-permute-start | bytes 110600 | tf_op jit(solution)/shard_map/ppermute | solution.py:428
  98.7 7.4 %collective-permute-start.20 = (f32[6,1536]{1,0:T(8,128)S(1)}, f32[6,1536]{1,0:T(8,128)S(1)}, u32[]{:S(2)}, u32[]{:S(2)}) collective-permute-start(f32[6,1536]{1,0:T(8,128)S(1)} %get-tuple-element.56), channel_id=1, source_target_pairs={{0,20},{4,16},{16,4},{20,0},{1,21},{5,17},{17,5},{21,1},{2,22},{6,... | collective-permute-start | bytes 110600 | tf_op jit(solution)/shard_map/ppermute | solution.py:428

commit v5 on v4

--- a/solution.py
+++ b/solution.py
@@ -326,7 +326,7 @@
         scratch_shapes=[VMEM(f.shape, f.dtype) for f in far]
         + list(scratch)
         + [pltpu.SemaphoreType.DMA((max(1, len(far)), chunks))],
-        cost_estimate=pl.CostEstimate(flops=int(micros * 1e9), bytes_accessed=1024, transcendentals=0),
+        cost_estimate=pl.CostEstimate(flops=int(micros * 25e8), bytes_accessed=1024, transcendentals=0),
         compiler_params=pltpu.CompilerParams(vmem_limit_bytes=mib * 1024 * 1024),
     )(*scalars, *near, *far)
 

time: 108 us -> 107 us (level)
    ppermute x6, waiting for transfers between devices: 5.88 us -> 4.15 us  [next_tile(): lax.ppermute(value, FRAME, [(i, (i + step) % TILES) for i in range(TILES)])]
    all_to_all x1, starting transfers between devices: 3.55 us -> 4.88 us  [shards(): lax.all_to_all(partial.reshape(8, GROUP_ROWS // 8, HD), 'z', 0, 0, tiled=...]
    ppermute x1, starting transfers between devices: 4.4 us -> 3.19 us  [shards(): w_passed = lax.ppermute(out_weight, ('core', 'ylo'), [(0, 1), (3, 2)])]
    unnamed x28 -> x32, local copies, waits for them, and re-layouts: 2.02 us -> 2.69 us
  transfers between devices with their start and end apart: 23 -> 23, of which waited for: 8 -> 6; matrix products, arithmetic and copies ran while one was open for 0% -> 0% of each run, Pallas kernels for 23% -> 22%
where the time goes in v5:
time: 107 us; the launch traced here: 106 us
  starting transfers between devices  51.3 us (48%)
  Pallas kernels  29.4 us (27%)
  waiting for transfers between devices  18.7 us (17%)
  between operations  2.98 us (3%)
  local copies, waits for them, and re-layouts  2.78 us (3%)
    pallas_call x7, Pallas kernels, call(): pl.pallas_call(body, in_specs=[pl.BlockSpec(memory_space=pltpu.SMEM)] * l...  26.6 us
    ppermute x6, starting transfers between devices, next_tile(): lax.ppermute(value, FRAME, [(i, (i + step) % TILES) for i in range(TILES)])  25.6 us
    ppermute x6, waiting for transfers between devices, along_x(): return lax.ppermute(value, 'x', [((i + step) % 4, i) for i in range(4)])  10.8 us
    ppermute x6, starting transfers between devices, along_x(): return lax.ppermute(value, 'x', [((i + step) % 4, i) for i in range(4)])  7.19 us
    all_to_all x1, starting transfers between devices, shards(): lax.all_to_all(partial.reshape(8, GROUP_ROWS // 8, HD), 'z', 0, 0, tiled=...  4.88 us
    all_to_all x1, starting transfers between devices, shards(): mixed = lax.all_to_all(mixed, ('core', 'x'), 0, 0, tiled=True)  4.88 us
    ppermute x3, starting transfers between devices, shards(): arrived.append(lax.ppermute(pieces[step], ('yhi', 'ylo'), pairs))  4.77 us
    ppermute x6, waiting for transfers between devices, next_tile(): lax.ppermute(value, FRAME, [(i, (i + step) % TILES) for i in range(TILES)])  4.15 us
  transfers between devices with their start and end apart: 23, of which 6 were waited for; matrix products, arithmetic and copies ran while one was open for 0% of the time, Pallas kernels for 22%

profile of v5, /device:TPU:2, one launch (start us, length us, event | category | flops | bytes accessed | tf_op | source)
XLA Modules:
  0.0 105.8 jit_solution(112273088846593017)
XLA Ops:
  2.6 2.0 %shard_map.128 = bf16[272,1536]{1,0:T(8,128)(2,1)} custom-call(s32[1,1]{1,0:T(1,128)} %copy.14.frame, s32[1,1]{1,0:T(1,128)} %copy.15.back, s32[1,1]{1,0:T(1,128)} %copy.16.ahead, bf16[128,1536]{1,0:T(8,128)(2,1)} %bitcast.24, bf16[128,1536]{1,0:T(8,128)(2,1)} %bitcast.27), custom_call_target="tpu_custom_call" | custom-call | tf_op jit(solution)/shard_map/pallas_call | solution.py:112
  4.7 8.0 %collective-permute-start.1 = (bf16[272,1536]{1,0:T(8,128)(2,1)}, bf16[272,1536]{1,0:T(8,128)(2,1)}, u32[]{:S(2)}, u32[]{:S(2)}) collective-permute-start(bf16[272,1536]{1,0:T(8,128)(2,1)} %shard_map.128), channel_id=1, source_target_pairs={{0,248},{8,0},{16,8},{24,16},{32,24},{40,32},{48,40},{56,48},{64,5... | collective-permute-start | bytes 2506760 | tf_op jit(solution)/shard_map/ppermute | solution.py:41
  12.7 1.5 %collective-permute-start.5 = (bf16[128,1536]{1,0:T(8,128)(2,1)S(1)}, bf16[128,1536]{1,0:T(8,128)(2,1)S(1)}, u32[]{:S(2)}, u32[]{:S(2)}) collective-permute-start(bf16[128,1536]{1,0:T(8,128)(2,1)S(1)} %bitcast.20), channel_id=1, source_target_pairs={{3,0},{0,1},{1,2},{2,3},{7,4},{4,5},{5,6},{6,7},{11,8},{8,9},{9,10... | collective-permute-start | bytes 1179656 | tf_op jit(solution)/shard_map/ppermute | solution.py:53
  14.2 1.1 %collective-permute-start.4 = (bf16[128,1536]{1,0:T(8,128)(2,1)S(1)}, bf16[128,1536]{1,0:T(8,128)(2,1)S(1)}, u32[]{:S(2)}, u32[]{:S(2)}) collective-permute-start(bf16[128,1536]{1,0:T(8,128)(2,1)S(1)} %bitcast.21), channel_id=1, source_target_pairs={{2,0},{3,1},{0,2},{1,3},{6,4},{7,5},{4,6},{5,7},{10,8},{11,9},{8,1... | collective-permute-start | bytes 1179656 | tf_op jit(solution)/shard_map/ppermute | solution.py:53
  15.3 2.2 %collective-permute-start.3 = (bf16[128,1536]{1,0:T(8,128)(2,1)S(1)}, bf16[128,1536]{1,0:T(8,128)(2,1)S(1)}, u32[]{:S(2)}, u32[]{:S(2)}) collective-permute-start(bf16[128,1536]{1,0:T(8,128)(2,1)S(1)} %bitcast.22), channel_id=1, source_target_pairs={{1,0},{2,1},{3,2},{0,3},{5,4},{6,5},{7,6},{4,7},{9,8},{10,9},{11,1... | collective-permute-start | bytes 1179656 | tf_op jit(solution)/shard_map/ppermute | solution.py:53
  17.4 0.1 stack.23.refs_0_
  17.5 0.0 copy-start.2
  17.5 0.0 copy-start.9
  17.6 5.8 %collective-permute-done.5.refs_3_ = bf16[128,1536]{1,0:T(8,128)(2,1)S(1)} collective-permute-done((bf16[128,1536]{1,0:T(8,128)(2,1)S(1)}, bf16[128,1536]{1,0:T(8,128)(2,1)S(1)}, u32[]{:S(2)}, u32[]{:S(2)}) %collective-permute-start.5) | collective-permute-done | bytes 393248 | tf_op jit(solution)/shard_map/ppermute | solution.py:53
  23.4 3.2 %collective-permute-start.2 = (bf16[192,1536]{1,0:T(8,128)(2,1)}, bf16[192,1536]{1,0:T(8,128)(2,1)S(1)}, u32[]{:S(2)}, u32[]{:S(2)}) collective-permute-start(bf16[192,1536]{1,0:T(8,128)(2,1)} %refs_2_.1), channel_id=1, source_target_pairs={{0,4},{12,8},{1,5},{13,9},{2,6},{14,10},{3,7},{15,11},{16,20},{28,... | collective-permute-start | bytes 1769480 | tf_op jit(solution)/shard_map/ppermute | solution.py:350
  26.6 0.0 collective-permute-done.4.refs_2_
  26.6 3.0 %collective-permute-done.3.refs_1_ = bf16[128,1536]{1,0:T(8,128)(2,1)S(1)} collective-permute-done((bf16[128,1536]{1,0:T(8,128)(2,1)S(1)}, bf16[128,1536]{1,0:T(8,128)(2,1)S(1)}, u32[]{:S(2)}, u32[]{:S(2)}) %collective-permute-start.3) | collective-permute-done | bytes 393248 | tf_op jit(solution)/shard_map/ppermute | solution.py:53
  29.6 0.8 shard_map.130.refs_4_.refs_2_
  30.4 0.1 collective-permute-start.6
  30.5 0.0 collective-permute-done.1.refs_5_.refs_6_
  30.6 0.0 collective-permute-done.refs_4_.refs_5_
  30.6 6.6 %shard_map.129 = (bf16[128,1536]{1,0:T(8,128)(2,1)S(1)}, bf16[8,192,128]{2,1,0:T(8,128)(2,1)S(1)}, f32[128,128]{1,0:T(8,128)S(1)}) custom-call(s32[8]{0:T(128)S(1)} %stack.23.refs_0_, bf16[128,1536]{1,0:T(8,128)(2,1)} %bitcast.8.refs_1_.refs_2_, bf16[128,1536]{1,0:T(8,128)(2,1)S(1)} %bitcast.26, bf16[128,1536]{1,0:T(8,128)(2,1)S(1)} %bitcast.29, ...), custom_call_target="tpu_custom_call" | custom-call | flops 20000000000 | bytes 1024 | tf_op jit(solution)/shard_map/pallas_call | solution.py:319
  37.2 0.0 copy-start.10
  37.2 0.0 copy-start.14
  37.2 0.0 collective-permute-done.2.refs_3_
  37.2 3.6 %shard_map.131 = (bf16[8,384,128]{2,1,0:T(8,128)(2,1)}, bf16[192,1536]{1,0:T(8,128)(2,1)S(1)}) custom-call(s32[8]{0:T(128)S(1)} %stack.23.refs_0_, bf16[8,192,128]{2,1,0:T(8,128)(2,1)S(1)} %get-tuple-element.32.refs_1_, bf16[192,1536]{1,0:T(8,128)(2,1)} %refs_2_.1, bf16[192,1536]{1,0:T(8,128)(2,1)S(1)} %collective-permute-done.2.refs_3_, ...), custom_call_target="tpu_custom_call" | custom-call | flops 5000000000 | bytes 1024 | tf_op jit(solution)/shard_map/pallas_call | solution.py:319
  40.9 0.8 copy-done.7
  41.7 4.9 %all-to-all-start = ((bf16[8,384,128]{2,1,0:T(8,128)(2,1)}), bf16[8,384,128]{2,1,0:T(8,128)(2,1)S(1)}, u32[]{:S(2)}, u32[]{:S(2)}) async-start(bf16[8,384,128]{2,1,0:T(8,128)(2,1)} %get-tuple-element.34), calls=%async_computation | async-start | bytes 1572864 | tf_op jit(solution)/shard_map/all_to_all | solution.py:379
  46.6 8.2 %collective-permute-start.8 = (bf16[128,1536]{1,0:T(8,128)(2,1)}, bf16[128,1536]{1,0:T(8,128)(2,1)}, u32[]{:S(2)}, u32[]{:S(2)}) collective-permute-start(bf16[128,1536]{1,0:T(8,128)(2,1)} %bitcast.8.refs_1_.refs_2_), channel_id=1, source_target_pairs={{0,248},{8,0},{16,8},{24,16},{32,24},{40,32},{48,40},{56,48},{64,5... | collective-permute-start | bytes 1179656 | tf_op jit(solution)/shard_map/ppermute | solution.py:41
  54.8 1.5 %collective-permute-start.10 = (bf16[192,1536]{1,0:T(8,128)(2,1)S(1)}, bf16[192,1536]{1,0:T(8,128)(2,1)S(1)}, u32[]{:S(2)}, u32[]{:S(2)}) collective-permute-start(bf16[192,1536]{1,0:T(8,128)(2,1)S(1)} %copy-done.8), channel_id=1, source_target_pairs={{3,0},{0,1},{1,2},{2,3},{7,4},{4,5},{5,6},{6,7},{11,8},{8,9},{9,10... | collective-permute-start | bytes 1769480 | tf_op jit(solution)/shard_map/ppermute | solution.py:53
  56.3 0.6 collective-permute-start.9
  56.8 1.1 %all-to-all-done.refs_0_.refs_1_ = bf16[8,384,128]{2,1,0:T(8,128)(2,1)S(1)} async-done(((bf16[8,384,128]{2,1,0:T(8,128)(2,1)}), bf16[8,384,128]{2,1,0:T(8,128)(2,1)S(1)}, u32[]{:S(2)}, u32[]{:S(2)}) %all-to-all-start) | async-done | bytes 786464 | tf_op jit(solution)/shard_map/all_to_all | solution.py:379
  57.9 1.0 copy-done.11
  58.9 0.8 copy-done.15
  59.8 1.3 %shard_map.132 = (bf16[144,1536]{1,0:T(8,128)(2,1)}, f32[128,128]{1,0:T(8,128)S(1)}) custom-call(bf16[8,384,128]{2,1,0:T(8,128)(2,1)S(1)} %all-to-all-done.refs_0_.refs_1_, bf16[128,1536]{1,0:T(8,128)(2,1)S(1)} %copy-done.11, f32[128,128]{1,0:T(8,128)S(1)} %copy-done.15), custom_call_target="tpu_custom_call" | custom-call | flops 2500000000 | bytes 1024 | tf_op jit(solution)/shard_map/pallas_call | solution.py:319
  61.1 9.4 %collective-permute-start.12 = (bf16[144,1536]{1,0:T(8,128)(2,1)}, bf16[144,1536]{1,0:T(8,128)(2,1)}, u32[]{:S(2)}, u32[]{:S(2)}) collective-permute-start(bf16[144,1536]{1,0:T(8,128)(2,1)} %get-tuple-element.36.refs_7_), channel_id=1, source_target_pairs={{0,248},{8,0},{16,8},{24,16},{32,24},{40,32},{48,40},{56,48},{64,5... | collective-permute-start | bytes 1327112 | tf_op jit(solution)/shard_map/ppermute | solution.py:41
  70.5 2.2 %shard_map.133 = bf16[192,1536]{1,0:T(8,128)(2,1)} custom-call(s32[8]{0:T(128)S(1)} %stack.23.refs_0_, bf16[8,384,128]{2,1,0:T(8,128)(2,1)S(1)} %all-to-all-done.refs_0_.refs_1_, bf16[512,1536]{1,0:T(8,128)(2,1)S(1)} %shard_map.130.refs_4_.refs_2_, bf16[512,1536]{1,0:T(8,128)(2,1)S(1)} %copy-done.6), custom_call_target="tpu_custom_call" | custom-call | flops 5000000000 | bytes 1024 | tf_op jit(solution)/shard_map/pallas_call | solution.py:319
  72.7 4.9 %all-to-all-start.1 = ((bf16[8,24,1536]{2,1,0:T(8,128)(2,1)}), bf16[8,24,1536]{2,1,0:T(8,128)(2,1)S(1)}, u32[]{:S(2)}, u32[]{:S(2)}) async-start(bf16[8,24,1536]{2,1,0:T(8,128)(2,1)} %bitcast.12), calls=%async_computation.1 | async-start | bytes 1179648 | tf_op jit(solution)/shard_map/all_to_all | solution.py:399
  77.6 0.4 collective-permute-start.13
  78.0 4.1 %collective-permute-done.11.refs_10_ = bf16[144,1536]{1,0:T(8,128)(2,1)} collective-permute-done((bf16[144,1536]{1,0:T(8,128)(2,1)}, bf16[144,1536]{1,0:T(8,128)(2,1)}, u32[]{:S(2)}, u32[]{:S(2)}) %collective-permute-start.11) | collective-permute-done | bytes 442400 | tf_op jit(solution)/shard_map/ppermute | solution.py:41
  82.1 8.7 %shard_map.134 = (bf16[128,1536]{1,0:T(8,128)(2,1)}, bf16[128,1536]{1,0:T(8,128)(2,1)}, bf16[128,1536]{1,0:T(8,128)(2,1)}) custom-call(s32[8]{0:T(128)} %copy-done.3, f32[128,128]{1,0:T(8,128)} %copy-done.13, bf16[128,1536]{1,0:T(8,128)(2,1)} %bitcast.8.refs_1_.refs_2_, bf16[128,1536]{1,0:T(8,128)(2,1)} %bitcast.25, bf16[128,1536]{1,0:T(8,128)(2,1)} %bitcast.28, ...), custom_call_target="tpu_custom_call" | custom-call | flops 22499999744 | bytes 1024 | tf_op jit(solution)/shard_map/pallas_call | solution.py:319
  90.9 0.0 copy-start.12
  90.9 0.1 collective-permute-start.14
  91.0 0.5 collective-permute-start.15
  91.5 0.1 collective-permute-start.17
  91.6 1.9 %collective-permute-done.13.refs_4_ = bf16[192,1536]{1,0:T(8,128)(2,1)S(1)} collective-permute-done((bf16[192,1536]{1,0:T(8,128)(2,1)S(1)}, bf16[192,1536]{1,0:T(8,128)(2,1)S(1)}, u32[]{:S(2)}, u32[]{:S(2)}) %collective-permute-start.13) | collective-permute-done | bytes 589856 | tf_op jit(solution)/shard_map/ppermute | solution.py:53
  93.5 2.6 %all-to-all-done.1.refs_1_ = bf16[8,24,1536]{2,1,0:T(8,128)(2,1)S(1)} async-done(((bf16[8,24,1536]{2,1,0:T(8,128)(2,1)}), bf16[8,24,1536]{2,1,0:T(8,128)(2,1)S(1)}, u32[]{:S(2)}, u32[]{:S(2)}) %all-to-all-start.1) | async-done | bytes 589856 | tf_op jit(solution)/shard_map/all_to_all | solution.py:399
  96.1 0.7 shard_map.135
  96.8 0.1 collective-permute-start.18
  96.9 0.5 collective-permute-start.19
  97.5 4.2 %collective-permute-start.20 = (f32[6,1536]{1,0:T(8,128)S(1)}, f32[6,1536]{1,0:T(8,128)S(1)}, u32[]{:S(2)}, u32[]{:S(2)}) collective-permute-start(f32[6,1536]{1,0:T(8,128)S(1)} %get-tuple-element.56), channel_id=1, source_target_pairs={{0,20},{4,16},{16,4},{20,0},{1,21},{5,17},{17,5},{21,1},{2,22},{6,... | collective-permute-start | bytes 110600 | tf_op jit(solution)/shard_map/ppermute | solution.py:428
  101.6 3.5 %shard_map.136 = bf16[128,1536]{1,0:T(8,128)(2,1)} custom-call(s32[8]{0:T(128)S(1)} %copy-done.4, bf16[128,1536]{1,0:T(8,128)(2,1)S(1)} %copy-done.12, bf16[192,1536]{1,0:T(8,128)(2,1)S(1)} %copy-done.8, bf16[192,1536]{1,0:T(8,128)(2,1)} %collective-permute-done.9.refs_3_, bf16[192,1536]{1,0:T(8,128)(2,1)S(1)} %collective-permute-done.13.refs_4_, ...), custom_call_target="tpu_custom_call" | custom-call | flops 10000000000 | bytes 1024 | tf_op jit(solution)/shard_map/pallas_call | solution.py:319
  105.2 0.6 add_add_fusion
  (41 shorter events, 0.1 us)
Async XLA Ops:
  0.6 12.1 %copy-start = (bf16[1,128,1536]{2,1,0:T(8,128)(2,1)S(1)}, bf16[1,128,1536]{2,1,0:T(8,128)(2,1)}, u32[]{:S(2)}) copy-start(bf16[1,128,1536]{2,1,0:T(8,128)(2,1)} %param.16) | copy-start | bytes 1179652
  4.7 25.9 %collective-permute-start.1 = (bf16[272,1536]{1,0:T(8,128)(2,1)}, bf16[272,1536]{1,0:T(8,128)(2,1)}, u32[]{:S(2)}, u32[]{:S(2)}) collective-permute-start(bf16[272,1536]{1,0:T(8,128)(2,1)} %shard_map.128), channel_id=1, source_target_pairs={{0,248},{8,0},{16,8},{24,16},{32,24},{40,32},{48,40},{56,48},{64,5... | collective-permute-start | bytes 2506760 | tf_op jit(solution)/shard_map/ppermute | solution.py:41
  12.7 17.9 %collective-permute-start = (bf16[272,1536]{1,0:T(8,128)(2,1)}, bf16[272,1536]{1,0:T(8,128)(2,1)}, u32[]{:S(2)}, u32[]{:S(2)}) collective-permute-start(bf16[272,1536]{1,0:T(8,128)(2,1)} %shard_map.128), channel_id=1, source_target_pairs={{0,8},{8,16},{16,24},{24,32},{32,40},{40,48},{48,56},{56,64},{64,7... | collective-permute-start | bytes 2506760 | tf_op jit(solution)/shard_map/ppermute | solution.py:41
  12.7 10.7 %collective-permute-start.5 = (bf16[128,1536]{1,0:T(8,128)(2,1)S(1)}, bf16[128,1536]{1,0:T(8,128)(2,1)S(1)}, u32[]{:S(2)}, u32[]{:S(2)}) collective-permute-start(bf16[128,1536]{1,0:T(8,128)(2,1)S(1)} %bitcast.20), channel_id=1, source_target_pairs={{3,0},{0,1},{1,2},{2,3},{7,4},{4,5},{5,6},{6,7},{11,8},{8,9},{9,10... | collective-permute-start | bytes 1179656 | tf_op jit(solution)/shard_map/ppermute | solution.py:53
  14.2 12.4 %collective-permute-start.4 = (bf16[128,1536]{1,0:T(8,128)(2,1)S(1)}, bf16[128,1536]{1,0:T(8,128)(2,1)S(1)}, u32[]{:S(2)}, u32[]{:S(2)}) collective-permute-start(bf16[128,1536]{1,0:T(8,128)(2,1)S(1)} %bitcast.21), channel_id=1, source_target_pairs={{2,0},{3,1},{0,2},{1,3},{6,4},{7,5},{4,6},{5,7},{10,8},{11,9},{8,1... | collective-permute-start | bytes 1179656 | tf_op jit(solution)/shard_map/ppermute | solution.py:53
  15.3 14.4 %collective-permute-start.3 = (bf16[128,1536]{1,0:T(8,128)(2,1)S(1)}, bf16[128,1536]{1,0:T(8,128)(2,1)S(1)}, u32[]{:S(2)}, u32[]{:S(2)}) collective-permute-start(bf16[128,1536]{1,0:T(8,128)(2,1)S(1)} %bitcast.22), channel_id=1, source_target_pairs={{1,0},{2,1},{3,2},{0,3},{5,4},{6,5},{7,6},{4,7},{9,8},{10,9},{11,1... | collective-permute-start | bytes 1179656 | tf_op jit(solution)/shard_map/ppermute | solution.py:53
  17.5 53.0 %copy-start.3 = (s32[8]{0:T(128)}, s32[8]{0:T(128)S(1)}, u32[]{:S(2)}) copy-start(s32[8]{0:T(128)S(1)} %stack.23.refs_0_) | copy-start | bytes 100
  17.5 13.0 %copy-start.1 = (bf16[1,128,1536]{2,1,0:T(8,128)(2,1)S(1)}, bf16[1,128,1536]{2,1,0:T(8,128)(2,1)}, u32[]{:S(2)}) copy-start(bf16[1,128,1536]{2,1,0:T(8,128)(2,1)} %param.10) | copy-start | bytes 1179652
  17.5 13.0 %copy-start.2 = (bf16[1,128,1536]{2,1,0:T(8,128)(2,1)S(1)}, bf16[1,128,1536]{2,1,0:T(8,128)(2,1)}, u32[]{:S(2)}) copy-start(bf16[1,128,1536]{2,1,0:T(8,128)(2,1)} %param.11) | copy-start | bytes 1179652
  17.5 13.0 %copy-start.9 = (bf16[384,384]{1,0:T(8,128)(2,1)S(1)}, bf16[384,384]{1,0:T(8,128)(2,1)}, u32[]{:S(2)}) copy-start(bf16[384,384]{1,0:T(8,128)(2,1)} %constant.27.clone.refs_6_) | copy-start | bytes 884740
  23.4 13.8 %collective-permute-start.2 = (bf16[192,1536]{1,0:T(8,128)(2,1)}, bf16[192,1536]{1,0:T(8,128)(2,1)S(1)}, u32[]{:S(2)}, u32[]{:S(2)}) collective-permute-start(bf16[192,1536]{1,0:T(8,128)(2,1)} %refs_2_.1), channel_id=1, source_target_pairs={{0,4},{12,8},{1,5},{13,9},{2,6},{14,10},{3,7},{15,11},{16,20},{28,... | collective-permute-start | bytes 1769480 | tf_op jit(solution)/shard_map/ppermute | solution.py:350
  30.4 6.8 %collective-permute-start.6 = (bf16[512,1536]{1,0:T(8,128)(2,1)S(1)}, bf16[512,1536]{1,0:T(8,128)(2,1)S(1)}, u32[]{:S(2)}, u32[]{:S(2)}) collective-permute-start(bf16[512,1536]{1,0:T(8,128)(2,1)S(1)} %shard_map.130.refs_4_.refs_2_), channel_id=1, source_target_pairs={{0,8},{8,0},{1,9},{9,1},{2,10},{10,2},{3,11},{11,3},{4,12},{12,4},... | collective-permute-start | bytes 4718600 | tf_op jit(solution)/shard_map/ppermute | solution.py:45
  37.2 3.7 %copy-start.10 = (bf16[128,1536]{1,0:T(8,128)(2,1)}, bf16[128,1536]{1,0:T(8,128)(2,1)S(1)}, u32[]{:S(2)}) copy-start(bf16[128,1536]{1,0:T(8,128)(2,1)S(1)} %get-tuple-element.45.refs_1_) | copy-start | bytes 1179652
  37.2 3.7 %copy-start.14 = (f32[128,128]{1,0:T(8,128)}, f32[128,128]{1,0:T(8,128)S(1)}, u32[]{:S(2)}) copy-start(f32[128,128]{1,0:T(8,128)S(1)} %get-tuple-element.35.refs_2_) | copy-start | bytes 196612
  37.2 3.7 %copy-start.5 = (bf16[512,1536]{1,0:T(8,128)(2,1)}, bf16[512,1536]{1,0:T(8,128)(2,1)S(1)}, u32[]{:S(2)}) copy-start(bf16[512,1536]{1,0:T(8,128)(2,1)S(1)} %collective-permute-done.6.refs_5_.refs_3_) | copy-start | bytes 4718596
  40.9 0.8 copy-start.7
  41.7 13.1 %copy-start.8 = (bf16[192,1536]{1,0:T(8,128)(2,1)S(1)}, bf16[192,1536]{1,0:T(8,128)(2,1)}, u32[]{:S(2)}) copy-start(bf16[192,1536]{1,0:T(8,128)(2,1)} %copy-done.7) | copy-start | bytes 1769476
  41.7 16.2 %all-to-all-start = ((bf16[8,384,128]{2,1,0:T(8,128)(2,1)}), bf16[8,384,128]{2,1,0:T(8,128)(2,1)S(1)}, u32[]{:S(2)}, u32[]{:S(2)}) async-start(bf16[8,384,128]{2,1,0:T(8,128)(2,1)} %get-tuple-element.34), calls=%async_computation | async-start | bytes 1572864 | tf_op jit(solution)/shard_map/all_to_all | solution.py:379
  46.6 23.9 %collective-permute-start.8 = (bf16[128,1536]{1,0:T(8,128)(2,1)}, bf16[128,1536]{1,0:T(8,128)(2,1)}, u32[]{:S(2)}, u32[]{:S(2)}) collective-permute-start(bf16[128,1536]{1,0:T(8,128)(2,1)} %bitcast.8.refs_1_.refs_2_), channel_id=1, source_target_pairs={{0,248},{8,0},{16,8},{24,16},{32,24},{40,32},{48,40},{56,48},{64,5... | collective-permute-start | bytes 1179656 | tf_op jit(solution)/shard_map/ppermute | solution.py:41
  54.8 15.7 %collective-permute-start.7 = (bf16[128,1536]{1,0:T(8,128)(2,1)}, bf16[128,1536]{1,0:T(8,128)(2,1)}, u32[]{:S(2)}, u32[]{:S(2)}) collective-permute-start(bf16[128,1536]{1,0:T(8,128)(2,1)} %bitcast.8.refs_1_.refs_2_), channel_id=1, source_target_pairs={{0,8},{8,16},{16,24},{24,32},{32,40},{40,48},{48,56},{56,64},{64,7... | collective-permute-start | bytes 1179656 | tf_op jit(solution)/shard_map/ppermute | solution.py:41
  54.8 23.2 %collective-permute-start.10 = (bf16[192,1536]{1,0:T(8,128)(2,1)S(1)}, bf16[192,1536]{1,0:T(8,128)(2,1)S(1)}, u32[]{:S(2)}, u32[]{:S(2)}) collective-permute-start(bf16[192,1536]{1,0:T(8,128)(2,1)S(1)} %copy-done.8), channel_id=1, source_target_pairs={{3,0},{0,1},{1,2},{2,3},{7,4},{4,5},{5,6},{6,7},{11,8},{8,9},{9,10... | collective-permute-start | bytes 1769480 | tf_op jit(solution)/shard_map/ppermute | solution.py:53
  56.3 21.7 %collective-permute-start.9 = (bf16[192,1536]{1,0:T(8,128)(2,1)S(1)}, bf16[192,1536]{1,0:T(8,128)(2,1)}, u32[]{:S(2)}, u32[]{:S(2)}) collective-permute-start(bf16[192,1536]{1,0:T(8,128)(2,1)S(1)} %copy-done.8), channel_id=1, source_target_pairs={{1,0},{2,1},{3,2},{0,3},{5,4},{6,5},{7,6},{4,7},{9,8},{10,9},{11,1... | collective-permute-start | bytes 1769480 | tf_op jit(solution)/shard_map/ppermute | solution.py:53
  57.9 1.0 copy-start.11
  58.9 0.8 copy-start.15
  59.8 10.7 %copy-start.6 = (bf16[512,1536]{1,0:T(8,128)(2,1)S(1)}, bf16[512,1536]{1,0:T(8,128)(2,1)}, u32[]{:S(2)}) copy-start(bf16[512,1536]{1,0:T(8,128)(2,1)} %copy-done.5) | copy-start | bytes 4718596
  61.0 11.6 %copy-start.13 = (f32[128,128]{1,0:T(8,128)}, f32[128,128]{1,0:T(8,128)S(1)}, u32[]{:S(2)}) copy-start(f32[128,128]{1,0:T(8,128)S(1)} %get-tuple-element.41.refs_1_) | copy-start | bytes 196612
  61.1 16.9 %collective-permute-start.12 = (bf16[144,1536]{1,0:T(8,128)(2,1)}, bf16[144,1536]{1,0:T(8,128)(2,1)}, u32[]{:S(2)}, u32[]{:S(2)}) collective-permute-start(bf16[144,1536]{1,0:T(8,128)(2,1)} %get-tuple-element.36.refs_7_), channel_id=1, source_target_pairs={{0,248},{8,0},{16,8},{24,16},{32,24},{40,32},{48,40},{56,48},{64,5... | collective-permute-start | bytes 1327112 | tf_op jit(solution)/shard_map/ppermute | solution.py:41
  70.5 11.7 %collective-permute-start.11 = (bf16[144,1536]{1,0:T(8,128)(2,1)}, bf16[144,1536]{1,0:T(8,128)(2,1)}, u32[]{:S(2)}, u32[]{:S(2)}) collective-permute-start(bf16[144,1536]{1,0:T(8,128)(2,1)} %get-tuple-element.36.refs_7_), channel_id=1, source_target_pairs={{0,8},{8,16},{16,24},{24,32},{32,40},{40,48},{48,56},{56,64},{64,7... | collective-permute-start | bytes 1327112 | tf_op jit(solution)/shard_map/ppermute | solution.py:41
  72.7 23.4 %all-to-all-start.1 = ((bf16[8,24,1536]{2,1,0:T(8,128)(2,1)}), bf16[8,24,1536]{2,1,0:T(8,128)(2,1)S(1)}, u32[]{:S(2)}, u32[]{:S(2)}) async-start(bf16[8,24,1536]{2,1,0:T(8,128)(2,1)} %bitcast.12), calls=%async_computation.1 | async-start | bytes 1179648 | tf_op jit(solution)/shard_map/all_to_all | solution.py:399
  77.6 15.9 %collective-permute-start.13 = (bf16[192,1536]{1,0:T(8,128)(2,1)S(1)}, bf16[192,1536]{1,0:T(8,128)(2,1)S(1)}, u32[]{:S(2)}, u32[]{:S(2)}) collective-permute-start(bf16[192,1536]{1,0:T(8,128)(2,1)S(1)} %copy-done.8), channel_id=1, source_target_pairs={{2,0},{3,1},{0,2},{1,3},{6,4},{7,5},{4,6},{5,7},{10,8},{11,9},{8,1... | collective-permute-start | bytes 1769480 | tf_op jit(solution)/shard_map/ppermute | solution.py:53
  78.0 18.1 %copy-start.4 = (s32[8]{0:T(128)S(1)}, s32[8]{0:T(128)}, u32[]{:S(2)}) copy-start(s32[8]{0:T(128)} %copy-done.3) | copy-start | bytes 100
  90.9 10.7 %copy-start.12 = (bf16[128,1536]{1,0:T(8,128)(2,1)S(1)}, bf16[128,1536]{1,0:T(8,128)(2,1)}, u32[]{:S(2)}) copy-start(bf16[128,1536]{1,0:T(8,128)(2,1)} %copy-done.10) | copy-start | bytes 1179652
  90.9 6.0 %collective-permute-start.14 = (bf16[192,1536]{1,0:T(8,128)(2,1)S(1)}, bf16[192,1536]{1,0:T(8,128)(2,1)S(1)}, u32[]{:S(2)}, u32[]{:S(2)}) collective-permute-start(bf16[192,1536]{1,0:T(8,128)(2,1)S(1)} %copy-done.8), channel_id=1, source_target_pairs={{0,8},{8,0},{1,9},{9,1},{2,10},{10,2},{3,11},{11,3},{4,12},{12,4},... | collective-permute-start | bytes 1769480 | tf_op jit(solution)/shard_map/ppermute | solution.py:45
  91.0 6.4 %collective-permute-start.15 = (bf16[192,1536]{1,0:T(8,128)(2,1)}, bf16[192,1536]{1,0:T(8,128)(2,1)}, u32[]{:S(2)}, u32[]{:S(2)}) collective-permute-start(bf16[192,1536]{1,0:T(8,128)(2,1)} %collective-permute-done.9.refs_3_), channel_id=1, source_target_pairs={{0,8},{8,0},{1,9},{9,1},{2,10},{10,2},{3,11},{11,3},{4,12},{12,4},... | collective-permute-start | bytes 1769480 | tf_op jit(solution)/shard_map/ppermute | solution.py:45
  91.5 10.1 %collective-permute-start.17 = (bf16[192,1536]{1,0:T(8,128)(2,1)S(1)}, bf16[192,1536]{1,0:T(8,128)(2,1)}, u32[]{:S(2)}, u32[]{:S(2)}) collective-permute-start(bf16[192,1536]{1,0:T(8,128)(2,1)S(1)} %collective-permute-done.10.refs_5_), channel_id=1, source_target_pairs={{0,8},{8,0},{1,9},{9,1},{2,10},{10,2},{3,11},{11,3},{4,12},{12,4},... | collective-permute-start | bytes 1769480 | tf_op jit(solution)/shard_map/ppermute | solution.py:45
  93.5 8.1 %collective-permute-start.16 = (bf16[192,1536]{1,0:T(8,128)(2,1)S(1)}, bf16[192,1536]{1,0:T(8,128)(2,1)}, u32[]{:S(2)}, u32[]{:S(2)}) collective-permute-start(bf16[192,1536]{1,0:T(8,128)(2,1)S(1)} %collective-permute-done.13.refs_4_), channel_id=1, source_target_pairs={{0,8},{8,0},{1,9},{9,1},{2,10},{10,2},{3,11},{11,3},{4,12},{12,4},... | collective-permute-start | bytes 1769480 | tf_op jit(solution)/shard_map/ppermute | solution.py:45
  96.8 8.4 %collective-permute-start.18 = (f32[6,1536]{1,0:T(8,128)S(1)}, f32[6,1536]{1,0:T(8,128)S(1)}, u32[]{:S(2)}, u32[]{:S(2)}) collective-permute-start(f32[6,1536]{1,0:T(8,128)S(1)} %get-tuple-element.54), channel_id=1, source_target_pairs={{0,4},{4,0},{16,20},{20,16},{1,5},{5,1},{17,21},{21,17},{2,6},{6,2... | collective-permute-start | bytes 110600 | tf_op jit(solution)/shard_map/ppermute | solution.py:428
  96.9 8.3 %collective-permute-start.19 = (f32[6,1536]{1,0:T(8,128)S(1)}, f32[6,1536]{1,0:T(8,128)S(1)}, u32[]{:S(2)}, u32[]{:S(2)}) collective-permute-start(f32[6,1536]{1,0:T(8,128)S(1)} %get-tuple-element.55), channel_id=1, source_target_pairs={{0,16},{4,20},{16,0},{20,4},{1,17},{5,21},{17,1},{21,5},{2,18},{6,... | collective-permute-start | bytes 110600 | tf_op jit(solution)/shard_map/ppermute | solution.py:428
  97.5 7.7 %collective-permute-start.20 = (f32[6,1536]{1,0:T(8,128)S(1)}, f32[6,1536]{1,0:T(8,128)S(1)}, u32[]{:S(2)}, u32[]{:S(2)}) collective-permute-start(f32[6,1536]{1,0:T(8,128)S(1)} %get-tuple-element.56), channel_id=1, source_target_pairs={{0,20},{4,16},{16,4},{20,0},{1,21},{5,17},{17,5},{21,1},{2,22},{6,... | collective-permute-start | bytes 110600 | tf_op jit(solution)/shard_map/ppermute | solution.py:428
